TPU v7x, 512 devices: a whole 4x8x8 slice. The times are simulated.
512 devices in a mesh: dp: 2 (over x_hi), context: 32 (over x_lo, z, core), embodime: 8 (over y).
Axes of the slice: x: 4 (x_hi: 2, x_lo: 2; x = x_hi * 2 + x_lo), y: 8, z: 8, core: 2. Of those that a mesh axis runs over, the one named last changes fastest.
Arguments:
- query_tokens: bfloat16 [2, 8, 4096, 2560], P('dp', 'embodime', 'context'), may hold values from -40 to 40
- key_tokens: bfloat16 [2, 8, 4096, 2560], P('dp', 'embodime', 'context'), may hold values from -8 to 8
- value_tokens: bfloat16 [2, 8, 4096, 2560], P('dp', 'embodime', 'context'), may hold values from -6 to 6
- out_grad: bfloat16 [2, 8, 4096, 2560], P('dp', 'embodime', 'context'), may hold values from -6 to 6
- actions: bfloat16 [2, 8, 4096, 128], P('dp', 'embodime', 'context'), may hold values from -6 to 6
- clip_lengths: int32 [2, 8, 16], P('dp', 'embodime'), may hold values from 1 to 3, 32 in all within a row
- clip_robots: int32 [2, 8, 16], P('dp', 'embodime'), may hold values from 0 to 3
- adapters: bfloat16 [8, 4, 128, 64], P('embodime'), may hold values from -0.5 to 0.5
- up_proj: bfloat16 [64, 2560], replicated, may hold values from -0.75 to 0.75
Outputs:
- key_grad: bfloat16 [2, 8, 4096, 2560], P('dp', 'embodime', 'context')
- value_grad: bfloat16 [2, 8, 4096, 2560], P('dp', 'embodime', 'context')
- adapter_grad: float32 [8, 4, 128, 64], P('embodime')
- up_grad: float32 [64, 2560], replicated
Inputs may be any that keep to these rules, and one draw needn't show every extreme that they name: `clip_lengths`: each row sums to 32 and its largest entry is exactly 3.
All inputs are finite; a program needn't handle non-finite values.
Results may differ from a plain program's by a relative error of at most 0.0076.
Values may be sent and summed in bfloat16 or wider, within the bound.
No kernel may reach another device: no remote copies, remote signals or barrier semaphores. Data moves between devices by JAX's collectives and lax.ppermute only.
A program may use at most 64 MiB of HBM per device.

v0:
```python
import jax
import jax.numpy as jnp
from jax import lax
from jax.sharding import PartitionSpec as P

HEAD_DIM = 128


HIGH = lax.Precision.HIGHEST


def from_behind(shard, axis, by):
    peers = lax.axis_size(axis)
    pairs = [(i, i + by) for i in range(peers) if 0 <= i + by < peers]
    return lax.ppermute(shard, axis, pairs)


def local(
    query_tokens,
    key_tokens,
    value_tokens,
    out_grad,
    actions,
    clip_lengths,
    clip_robots,
    adapters,
    up_proj,
):
    tokens_here = query_tokens.shape[2]
    width = query_tokens.shape[3]
    heads = width // HEAD_DIM
    own_frame = lax.axis_index("context")
    context_size = lax.axis_size("context")
    longest = min(3, context_size // 2)
    lengths_row = clip_lengths[0, 0]
    clip_ends = jnp.cumsum(lengths_row)
    clip_index = jnp.sum((clip_ends <= own_frame).astype(jnp.int32))
    clip_hot = jnp.arange(lengths_row.shape[0], dtype=jnp.int32) == clip_index
    clip_start = jnp.sum(jnp.where(clip_hot, clip_ends - lengths_row, 0))
    robot_index = jnp.sum(jnp.where(clip_hot, clip_robots[0, 0], 0))
    robot_hot = (jnp.arange(adapters.shape[1], dtype=jnp.int32) == robot_index).astype(jnp.float32)
    robot_table = jnp.einsum(
        "r,rak->ak", robot_hot, adapters[0].astype(jnp.float32), precision=HIGH
    )
    action_rows = actions[0, 0].astype(jnp.float32)
    adapted = jnp.dot(action_rows, robot_table, precision=HIGH).astype(jnp.bfloat16)
    query_rows = (
        query_tokens[0, 0] + jnp.dot(adapted, up_proj, preferred_element_type=jnp.float32)
    ).astype(jnp.bfloat16)
    own_pair = jnp.stack([key_tokens[0, 0], value_tokens[0, 0]])
    pairs = [own_pair]
    moving = own_pair
    for offset in range(1, longest):
        moving = from_behind(moving, "context", 1)
        pairs.append(moving)
    split_shape = (tokens_here, heads, HEAD_DIM)
    query3 = query_rows.reshape(split_shape)
    grad3 = out_grad[0, 0].reshape(split_shape)
    score_scale = HEAD_DIM ** (-0.5)

    def block_scores(pair, offset):
        raw = (
            jnp.einsum(
                "qhe,khe->hqk",
                query3,
                pair[0].reshape(split_shape),
                preferred_element_type=jnp.float32,
            )
            * score_scale
        )
        return jnp.where(own_frame - offset >= clip_start, raw, -jnp.inf)

    def block_products(pair):
        return jnp.einsum(
            "qhe,khe->hqk", grad3, pair[1].reshape(split_shape), preferred_element_type=jnp.float32
        )

    first = block_scores(pairs[0], 0)
    run_max = jnp.max(first, -1)
    run_sum = jnp.zeros_like(run_max)
    run_dot = jnp.zeros_like(run_max)
    for offset, pair in enumerate(pairs):
        scores = first if offset == 0 else block_scores(pair, offset)
        prods = block_products(pair)
        new_max = jnp.maximum(run_max, jnp.max(scores, -1))
        factor = jnp.exp(run_max - new_max)
        weights = jnp.exp(scores - new_max[..., None])
        run_sum = run_sum * factor + jnp.sum(weights, -1)
        run_dot = run_dot * factor + jnp.sum(weights * prods, -1)
        run_max = new_max
    row_delta = run_dot / run_sum
    query_grad = jnp.zeros(split_shape, jnp.float32)
    totals = jnp.zeros((2, tokens_here, width), jnp.float32)
    for offset, pair in enumerate(pairs):
        scores = block_scores(pair, offset)
        prods = block_products(pair)
        probs = jnp.exp(scores - run_max[..., None]) / run_sum[..., None]
        prob_b = probs.astype(jnp.bfloat16)
        dscore = (probs * (prods - row_delta[..., None]) * score_scale).astype(jnp.bfloat16)
        query_grad = query_grad + jnp.einsum(
            "hqk,khe->qhe", dscore, pair[0].reshape(split_shape), preferred_element_type=jnp.float32
        )
        key_part = jnp.einsum("hqk,qhe->khe", dscore, query3, preferred_element_type=jnp.float32)
        value_part = jnp.einsum("hqk,qhe->khe", prob_b, grad3, preferred_element_type=jnp.float32)
        parts = jnp.stack(
            [key_part.reshape(tokens_here, width), value_part.reshape(tokens_here, width)]
        )
        if offset == 0:
            totals = parts
        else:
            returned = from_behind(parts.astype(jnp.bfloat16), "context", -offset)
            totals = totals + returned.astype(jnp.float32)
    query_flat = query_grad.reshape(tokens_here, width)
    adapted_grad = jnp.dot(query_flat, up_proj.astype(jnp.float32).T, precision=HIGH)
    up_term = jnp.dot(adapted.astype(jnp.float32).T, query_flat, precision=HIGH)
    action_term = jnp.dot(action_rows.T, adapted_grad, precision=HIGH)
    adapter_term = robot_hot[:, None, None] * action_term[None, :, :]
    adapter_total = lax.psum(adapter_term, ("dp", "context"))
    up_total = lax.psum(up_term, ("dp", "context", "embodime"))
    key_grad = totals[0].astype(jnp.bfloat16).reshape(1, 1, tokens_here, width)
    value_grad = totals[1].astype(jnp.bfloat16).reshape(1, 1, tokens_here, width)
    return (key_grad, value_grad, adapter_total[None], up_total)


def solution(mesh):
    placed = (
        P("dp", "embodime", "context", None),
        P("dp", "embodime", "context", None),
        P("dp", "embodime", "context", None),
        P("dp", "embodime", "context", None),
        P("dp", "embodime", "context", None),
        P("dp", "embodime", None),
        P("dp", "embodime", None),
        P("embodime", None, None, None),
        P(),
    )
    return jax.shard_map(
        local,
        mesh=mesh,
        in_specs=placed,
        out_specs=(
            P("dp", "embodime", "context", None),
            P("dp", "embodime", "context", None),
            P("embodime", None, None, None),
            P(),
        ),
        check_vma=False,
    )
```

profile of v0, /device:TPU:1, one launch (start us, length us, event | category | flops | bytes accessed | tf_op | source)
XLA Modules:
  0.0 565.8 jit_solution(13534924171258101121)
XLA Ops:
  10.3 5.4 collective-permute-start
  24.3 1.6 fusion.32
  25.8 4.7 collective-permute-done
  30.6 4.4 collective-permute-start.1
  38.7 11.1 %collective-permute-done.1 = bf16[2,128,2560]{1,2,0:T(8,128)(2,1)S(1)} collective-permute-done((bf16[2,128,2560]{1,2,0:T(8,128)(2,1)}, bf16[2,128,2560]{1,2,0:T(8,128)(2,1)S(1)}, u32[]{:S(2)}, u32[]{:S(2)}) %collective-permute-start.1) | collective-permute-done | bytes 1310752 | tf_op jit(solution)/shard_map/ppermute | solution.py:15
  56.7 2.2 copy.76
  58.9 2.2 copy.72
  61.1 5.0 multiply_convert_fusion.1
  68.4 2.2 copy.71
  70.6 2.5 convolution_convert_fusion.1
  73.1 2.2 copy.75
  75.3 1.7 convolution_bitcast_fusion
  84.7 1.9 collective-permute-start.2
  87.8 2.7 fusion.34
  90.5 1.7 fusion.14
  92.3 1.7 fusion.36
  94.0 1.8 copy.68
  97.3 18.0 %collective-permute-done.3 = bf16[2,128,2560]{2,1,0:T(8,128)(2,1)} collective-permute-done((bf16[2,128,2560]{2,1,0:T(8,128)(2,1)}, bf16[2,128,2560]{2,1,0:T(8,128)(2,1)}, u32[]{:S(2)}, u32[]{:S(2)}) %collective-permute-start.3) | collective-permute-done | bytes 1310752 | tf_op jit(solution)/shard_map/ppermute | solution.py:15
  115.3 14.8 %collective-permute-done.2 = bf16[2,128,2560]{2,1,0:T(8,128)(2,1)} collective-permute-done((bf16[2,128,2560]{2,1,0:T(8,128)(2,1)}, bf16[2,128,2560]{2,1,0:T(8,128)(2,1)}, u32[]{:S(2)}, u32[]{:S(2)}) %collective-permute-start.2) | collective-permute-done | bytes 1310752 | tf_op jit(solution)/shard_map/ppermute | solution.py:15
  130.1 2.6 fusion.2
  133.9 148.0 %all-reduce.3.cloned.1.call-done = f32[1,4,128,64]{2,3,1,0:T(8,128)} async-done(((f32[1,4,128,64]{2,3,1,0:T(8,128)}), f32[1,4,128,64]{2,3,1,0:T(8,128)}) %all-reduce.3.cloned.1.call-update) | async-done | bytes 131088 | tf_op jit(solution)/shard_map/psum | solution.py:118
  281.9 273.5 %all-reduce.5.cloned.1.call-done = f32[64,2560]{1,0:T(8,128)} async-done(((f32[64,2560]{1,0:T(8,128)}), f32[64,2560]{1,0:T(8,128)}) %all-reduce.5.cloned.1.call-update) | async-done | bytes 655376 | tf_op jit(solution)/shard_map/psum | solution.py:119
  555.4 1.6 copy.107
  557.0 2.0 copy.108
  (95 shorter events, 33.8 us)
Async XLA Ops:
  7.2 15.0 %copy-start = (bf16[64,2560]{1,0:T(8,128)(2,1)S(1)}, bf16[64,2560]{1,0:T(8,128)(2,1)}, u32[]{:S(2)}) copy-start(bf16[64,2560]{1,0:T(8,128)(2,1)} %param.17) | copy-start | bytes 983044
  7.2 274.7 %all-reduce.3.cloned.1.call-start = ((), (), s32[]{:S(2)}) async-start(), calls=%async_computation | async-start | bytes 262144 | tf_op jit(solution)/shard_map/psum | solution.py:118
  8.7 1.6 copy-start.5
  9.1 6.7 %copy-start.24 = (s32[1,1,16]{2,1,0:T(1,128)S(1)}, s32[1,1,16]{2,1,0:T(1,128)}, u32[]{:S(2)}) copy-start(s32[1,1,16]{2,1,0:T(1,128)} %param.14) | copy-start | bytes 196
  9.1 10.8 %copy-start.26 = (s32[1,1,16]{2,1,0:T(1,128)S(1)}, s32[1,1,16]{2,1,0:T(1,128)}, u32[]{:S(2)}) copy-start(s32[1,1,16]{2,1,0:T(1,128)} %param.15) | copy-start | bytes 196
  9.1 12.0 %copy-start.25 = (bf16[1,4,128,64]{2,3,1,0:T(8,128)(2,1)S(1)}, bf16[1,4,128,64]{2,3,1,0:T(8,128)(2,1)}, u32[]{:S(2)}) copy-start(bf16[1,4,128,64]{2,3,1,0:T(8,128)(2,1)} %param.16) | copy-start | bytes 196612
  9.1 12.8 %copy-start.23 = (bf16[1,1,128,128]{3,2,1,0:T(8,128)(2,1)S(1)}, bf16[1,1,128,128]{3,2,1,0:T(8,128)(2,1)}, u32[]{:S(2)}) copy-start(bf16[1,1,128,128]{3,2,1,0:T(8,128)(2,1)} %param.13) | copy-start | bytes 98308
  9.1 13.0 %copy-start.20 = (bf16[1,1,128,2560]{3,2,1,0:T(8,128)(2,1)S(1)}, bf16[1,1,128,2560]{3,2,1,0:T(8,128)(2,1)}, u32[]{:S(2)}) copy-start(bf16[1,1,128,2560]{3,2,1,0:T(8,128)(2,1)} %param.9) | copy-start | bytes 1966084
  10.3 20.2 %collective-permute-start = (bf16[2,128,2560]{1,2,0:T(8,128)(2,1)}, bf16[2,128,2560]{1,2,0:T(8,128)(2,1)}, u32[]{:S(2)}, u32[]{:S(2)}) collective-permute-start(bf16[2,128,2560]{1,2,0:T(8,128)(2,1)} %pad_maximum_fusion), channel_id=1, source_target_pairs={{0,8},{8,16},{16,24},{24,32},{32,40},{40,48},{48,56},{56,64},{64,7... | collective-permute-start | bytes 3932168 | tf_op jit(solution)/shard_map/ppermute | solution.py:15
  24.3 10.7 %copy-start.7 = (bf16[1,1,128,2560]{2,3,1,0:T(8,128)(2,1)S(1)}, bf16[1,1,128,2560]{2,3,1,0:T(8,128)(2,1)}, u32[]{:S(2)}) copy-start(bf16[1,1,128,2560]{2,3,1,0:T(8,128)(2,1)} %copy-done.6) | copy-start | bytes 1966084
  30.6 19.2 %collective-permute-start.1 = (bf16[2,128,2560]{1,2,0:T(8,128)(2,1)}, bf16[2,128,2560]{1,2,0:T(8,128)(2,1)S(1)}, u32[]{:S(2)}, u32[]{:S(2)}) collective-permute-start(bf16[2,128,2560]{1,2,0:T(8,128)(2,1)} %collective-permute-done), channel_id=1, source_target_pairs={{0,8},{8,16},{16,24},{24,32},{32,40},{40,48},{48,56},{56,64},{64,7... | collective-permute-start | bytes 3932168 | tf_op jit(solution)/shard_map/ppermute | solution.py:15
  38.7 15.2 %copy-start.1 = (f32[20,128,128]{1,2,0:T(8,128)}, f32[20,128,128]{1,2,0:T(8,128)S(1)}, u32[]{:S(2)}) copy-start(f32[20,128,128]{1,2,0:T(8,128)S(1)} %get-tuple-element.28) | copy-start | bytes 3932164
  50.8 4.5 copy-start.2
  75.2 1.7 copy-start.10
  75.3 1.7 copy-start.12
  78.6 2.3 copy-start.17
  78.6 2.3 copy-start.19
  80.9 2.5 copy-start.16
  80.9 2.5 copy-start.18
  82.1 33.2 %collective-permute-start.3 = (bf16[2,128,2560]{2,1,0:T(8,128)(2,1)}, bf16[2,128,2560]{2,1,0:T(8,128)(2,1)}, u32[]{:S(2)}, u32[]{:S(2)}) collective-permute-start(bf16[2,128,2560]{2,1,0:T(8,128)(2,1)} %pad_maximum_fusion.2), channel_id=1, source_target_pairs={{16,0},{24,8},{32,16},{40,24},{48,32},{56,40},{64,48},{72,56},{80,... | collective-permute-start | bytes 3932168 | tf_op jit(solution)/shard_map/ppermute | solution.py:15
  84.7 45.5 %collective-permute-start.2 = (bf16[2,128,2560]{2,1,0:T(8,128)(2,1)}, bf16[2,128,2560]{2,1,0:T(8,128)(2,1)}, u32[]{:S(2)}, u32[]{:S(2)}) collective-permute-start(bf16[2,128,2560]{2,1,0:T(8,128)(2,1)} %pad_maximum_fusion.1), channel_id=1, source_target_pairs={{8,0},{16,8},{24,16},{32,24},{40,32},{48,40},{56,48},{64,56},{72,6... | collective-permute-start | bytes 3932168 | tf_op jit(solution)/shard_map/ppermute | solution.py:15
  87.6 467.8 %all-reduce.5.cloned.1.call-start = ((), (), s32[]{:S(2)}) async-start(), calls=%async_computation.1 | async-start | bytes 1310720 | tf_op jit(solution)/shard_map/psum | solution.py:119
  90.5 1.7 copy-start.4
  94.0 1.8 copy-start.15
  (9 other events, 9.9 us)
Sparse Core Ops, SparseCore 0:
  87.7 194.1 all-reduce.2
  287.4 267.9 all-reduce.4
where the time goes:
time: 567 us; the launch traced here: 566 us
  waiting for transfers between devices  470 us (83%)
  matrix products  25 us (4%)
  local copies, waits for them, and re-layouts  24.9 us (4%)
  between operations  16.5 us (3%)
  other arithmetic  16 us (3%)
  starting transfers between devices  13.2 us (2%)
    psum x1, waiting for transfers between devices, local(): up_total = lax.psum(up_term, ('dp', 'context', 'embodime'))  274 us
    psum x1, waiting for transfers between devices, local(): adapter_total = lax.psum(adapter_term, ('dp', 'context'))  148 us
    ppermute x4, waiting for transfers between devices, from_behind(): return lax.ppermute(shard, axis, pairs)  48.6 us
    ppermute x4, starting transfers between devices, from_behind(): return lax.ppermute(shard, axis, pairs)  12.9 us
    another operation x6, local copies, waits for them, and re-layouts, local(): jnp.stack([key_part.reshape(tokens_here, width), value_part.reshape(token...  12 us
  transfers between devices with their start and end apart: 6, of which 6 were waited for; matrix products, arithmetic and copies ran while one was open for 5% of the time, Pallas kernels for 0%

commit v1 on v0

v1 whole, which is shorter than its diff:
```python
import functools
import math

import jax
import jax.numpy as jnp
from jax import lax
from jax.experimental import pallas as pl
from jax.experimental.pallas import tpu as pltpu
from jax.sharding import Mesh, PartitionSpec as P

HEAD = 128
TOK = 128
RANK = 64
STEP_HEADS = 2
LOW = -1e30
SCALE = HEAD**-0.5
SCALE2 = SCALE * math.log2(math.e)
F32 = jnp.float32
BF16 = jnp.bfloat16
GROUP = ("dp", "x", "z")


def dot(a, b, ca, cb):
    return lax.dot_general(a, b, (((ca,), (cb,)), ((), ())), preferred_element_type=F32)


def clip_of(frame, lengths, robots, clips):
    begin = jnp.int32(0)
    start = jnp.int32(0)
    robot = jnp.int32(0)
    for i in range(clips):
        size = lengths[i]
        inside = jnp.logical_and(frame >= begin, frame < begin + size)
        start = jnp.where(inside, begin, start)
        robot = jnp.where(inside, robots[i], robot)
        begin = begin + size
    return start, robot


def attend_kernel(
    clips, steps, place, lengths, robots,
    act_own, act_oth, adapters, up,
    q_own, g_own, k_own, v_own,
    q_oth, g_oth, k_oth, v_oth,
    k_str, v_str, k_crs, v_crs,
    mine, other, back_str, back_crs, payload,
    adapted, adapted_t, agrad_t,
):
    step = pl.program_id(0)
    core = place[0]
    first = core == 0
    frame_a = 2 * place[1]
    frame_b = frame_a + 1
    start_a, robot_a = clip_of(frame_a, lengths, robots, clips)
    start_b, robot_b = clip_of(frame_b, lengths, robots, clips)

    def bias(valid):
        return jnp.where(valid, jnp.float32(0), jnp.float32(LOW))

    bias_a = (bias(frame_a - 2 >= start_a), bias(frame_a - 1 >= start_a), jnp.float32(0))
    bias_b = (bias(frame_b - 2 >= start_b), bias(frame_b - 1 >= start_b), jnp.float32(0))

    def pick(one, two):
        return jnp.where(first, one, two)

    @pl.when(step == 0)
    def _():
        for n, robot in enumerate((robot_a, robot_b)):
            act = pick(act_own[...], act_oth[...]) if n == 0 else pick(act_oth[...], act_own[...])
            table = adapters[robot]
            adapted[n * TOK:(n + 1) * TOK, :] = dot(act, table, 1, 0).astype(BF16)
            adapted_t[:, n * TOK:(n + 1) * TOK] = dot(table, act, 0, 1).astype(BF16)
        agrad_t[...] = jnp.zeros_like(agrad_t)

    def soften(raw, prod, biases):
        scores = [raw[n * TOK:(n + 1) * TOK] * SCALE2 + b for n, b in enumerate(biases)]
        top = functools.reduce(jnp.maximum, scores)
        top = jnp.max(top, 0, keepdims=True)
        weights = [jnp.exp2(s - top) for s in scores]
        prods = [prod[n * TOK:(n + 1) * TOK] for n in range(len(biases))]
        total = jnp.sum(functools.reduce(jnp.add, weights), 0, keepdims=True)
        mixed = [w * p for w, p in zip(weights, prods)]
        moment = jnp.sum(functools.reduce(jnp.add, mixed), 0, keepdims=True)
        inverse = 1.0 / total
        delta = moment * inverse
        scaled = inverse * SCALE
        prob = [(w * inverse).astype(BF16) for w in weights]
        dscore = [((w * scaled) * (p - delta)).astype(BF16) for w, p in zip(weights, prods)]
        return prob, dscore

    none = jnp.zeros((TOK, TOK), BF16)
    for h in range(STEP_HEADS):
        cols = slice(h * HEAD, (h + 1) * HEAD)
        up_h = up[:, cols]
        shift = dot(adapted[...], up_h, 1, 0)
        q_tok = jnp.concatenate(
            [pick(q_own[:, cols], q_oth[:, cols]), pick(q_oth[:, cols], q_own[:, cols])], 0
        )
        query = (q_tok.astype(F32) + shift).astype(BF16)
        grad = jnp.concatenate(
            [pick(g_own[:, cols], g_oth[:, cols]), pick(g_oth[:, cols], g_own[:, cols])], 0
        )
        keys = jnp.concatenate(
            [
                pick(k_str[:, cols], k_crs[:, cols]), pick(k_crs[:, cols], k_str[:, cols]),
                pick(k_own[:, cols], k_oth[:, cols]), pick(k_oth[:, cols], k_own[:, cols]),
            ],
            0,
        )
        values = jnp.concatenate(
            [
                pick(v_str[:, cols], v_crs[:, cols]), pick(v_crs[:, cols], v_str[:, cols]),
                pick(v_own[:, cols], v_oth[:, cols]), pick(v_oth[:, cols], v_own[:, cols]),
            ],
            0,
        )
        raw = dot(keys, query, 1, 1)
        prod = dot(values, grad, 1, 1)
        prob_a, dscore_a = soften(raw[: 3 * TOK, :TOK], prod[: 3 * TOK, :TOK], bias_a)
        prob_b, dscore_b = soften(raw[TOK:, TOK:], prod[TOK:, TOK:], bias_b)
        prob = jnp.concatenate(
            [jnp.concatenate(prob_a + [none], 0), jnp.concatenate([none] + prob_b, 0)], 1
        )
        dscore = jnp.concatenate(
            [jnp.concatenate(dscore_a + [none], 0), jnp.concatenate([none] + dscore_b, 0)], 1
        )
        query_grad = dot(keys, dscore, 0, 0)
        high = query_grad.astype(BF16)
        low = (query_grad - high.astype(F32)).astype(BF16)
        agrad_t[...] += dot(up_h, high, 1, 0) + dot(up_h, low, 1, 0)
        up_term = dot(adapted_t[...], high, 1, 1) + dot(adapted_t[...], low, 1, 1)
        payload[pl.ds(2 * (step * STEP_HEADS + h), 2)] = up_term.reshape(2, 32, HEAD).astype(BF16)
        for n, part in enumerate((dot(dscore, query, 1, 0), dot(prob, grad, 1, 0))):
            p0, p1 = part[:TOK].astype(BF16), part[TOK:2 * TOK].astype(BF16)
            a, b = part[2 * TOK:3 * TOK], part[3 * TOK:]
            back_str[n, :, cols] = pick(p0, p1)
            back_crs[n, :, cols] = pick(p1, p0)
            mine[n, :, cols] = pick(a, b)
            other[n, :, cols] = pick(b, a).astype(BF16)

    @pl.when(step == steps - 1)
    def _():
        terms = []
        for n in range(2):
            act = pick(act_own[...], act_oth[...]) if n == 0 else pick(act_oth[...], act_own[...])
            whole = agrad_t[:, n * TOK:(n + 1) * TOK]
            high = whole.astype(BF16)
            low = (whole - high.astype(F32)).astype(BF16)
            terms.append(dot(high, act, 1, 0) + dot(low, act, 1, 0))
        zero = jnp.zeros((RANK, HEAD), F32)
        base = 2 * steps * STEP_HEADS
        for s in range(4):
            term = jnp.where(robot_a == s, terms[0], zero) + jnp.where(robot_b == s, terms[1], zero)
            payload[base + 2 * s:base + 2 * s + 2] = term.reshape(2, 32, HEAD).astype(BF16)
        rest = payload.shape[0] - base - 8
        payload[base + 8:] = jnp.zeros((rest, 32, HEAD), BF16)


def attend(place, lengths, robots, act_own, act_oth, adapters, up, own, oth, straight, cross):
    half = straight.shape[2]
    width = STEP_HEADS * HEAD
    steps = half // width
    own_spec = pl.BlockSpec((TOK, width), lambda j, place, *_: (0, place[0] * steps + j))

    def layer(n):
        return pl.BlockSpec((None, TOK, width), lambda j, *_: (n, 0, j))

    def whole(shape):
        return pl.BlockSpec(shape, lambda j, *_: (0,) * len(shape))

    pair = pl.BlockSpec((2, TOK, width), lambda j, *_: (0, 0, j))
    grid_spec = pltpu.PrefetchScalarGridSpec(
        num_scalar_prefetch=3,
        grid=(steps,),
        in_specs=[whole((TOK, HEAD)), whole((TOK, HEAD)), whole(adapters.shape)]
        + [pl.BlockSpec((RANK, width), lambda j, place, *_: (0, place[0] * steps + j))]
        + [own_spec] * 4
        + [layer(n) for n in range(4)]
        + [layer(0), layer(1), layer(0), layer(1)],
        out_specs=[pair, pair, pair, pair, whole((32, 32, HEAD))],
        scratch_shapes=[
            pltpu.VMEM((2 * TOK, RANK), BF16),
            pltpu.VMEM((RANK, 2 * TOK), BF16),
            pltpu.VMEM((RANK, 2 * TOK), F32),
        ],
    )
    shape = (2, TOK, half)
    return pl.pallas_call(
        functools.partial(attend_kernel, lengths.shape[0], steps),
        grid_spec=grid_spec,
        out_shape=[
            jax.ShapeDtypeStruct(shape, F32),
            jax.ShapeDtypeStruct(shape, BF16),
            jax.ShapeDtypeStruct(shape, BF16),
            jax.ShapeDtypeStruct(shape, BF16),
            jax.ShapeDtypeStruct((32, 32, HEAD), BF16),
        ],
        compiler_params=pltpu.CompilerParams(
            dimension_semantics=("arbitrary",), vmem_limit_bytes=32 * 1024 * 1024
        ),
        cost_estimate=pl.CostEstimate(
            flops=2 * 10 * 5 * 512 * 256 * 128, bytes_accessed=12 * 1024 * 1024, transcendentals=10 * 512 * 256
        ),
        name="attend",
    )(place, lengths, robots, act_own, act_oth, adapters, up, *own, oth, oth, oth, oth, straight, straight, cross, cross)


def finish_kernel(heads, gathered, up_grad, adapter_grad):
    per_core = heads // 2
    for core in range(2):
        for h in range(per_core):
            at = (core * per_core + h) * HEAD
            for part in range(2):
                up_grad[part * 32:(part + 1) * 32, at:at + HEAD] = gathered[2 * (2 * h + part) + core].astype(F32)
    for s in range(4):
        chunk = 2 * per_core + 2 * s
        term = jnp.concatenate([gathered[2 * chunk], gathered[2 * chunk + 2]], 0).astype(F32)
        adapter_grad[s] = term.T


def finish(gathered, heads, adapters_shape):
    return pl.pallas_call(
        functools.partial(finish_kernel, heads),
        out_shape=[
            jax.ShapeDtypeStruct((RANK, heads * HEAD), F32),
            jax.ShapeDtypeStruct(adapters_shape, F32),
        ],
        name="finish",
    )(gathered)


def local(
    query_tokens, key_tokens, value_tokens, out_grad, actions, clip_lengths, clip_robots, adapters, up_proj,
):
    q, k, v, g = (t[0, 0] for t in (query_tokens, key_tokens, value_tokens, out_grad))
    act = actions[0, 0]
    width = q.shape[1]
    half = width // 2
    core = lax.axis_index("core")
    nz = lax.axis_size("z")
    chips = lax.axis_size("x") * nz
    chip = lax.axis_index("x") * nz + lax.axis_index("z")
    chain = ("x", "z", "core")

    def near(array):
        return lax.dynamic_slice_in_dim(array, core * half, half, 1)

    def far(array):
        return lax.dynamic_slice_in_dim(array, (1 - core) * half, half, 1)

    def chip_step(by, flip):
        return [
            (2 * c + i, 2 * (c + by) + ((1 - i) if flip else i))
            for c in range(chips)
            for i in range(2)
            if 0 <= c + by < chips
        ]

    swap = [(0, 1), (1, 0)]
    near_pair = jnp.stack([near(k), near(v)])
    far_all = jnp.stack([far(q), far(g), far(k), far(v)])
    straight = lax.ppermute(near_pair, chain, chip_step(1, False))
    cross = lax.ppermute(far_all[2:], chain, chip_step(1, True))
    oth = lax.ppermute(far_all, "core", swap)
    act_oth = lax.ppermute(act, "core", swap)
    place = jnp.stack([core, chip]).astype(jnp.int32)
    mine, other, back_str, back_crs, payload = attend(
        place, clip_lengths[0, 0], clip_robots[0, 0], act, act_oth, adapters[0], up_proj,
        (q, g, k, v), oth, straight, cross,
    )

    pieces = lax.all_to_all(payload, GROUP, 0, 0, tiled=True)
    chunk = jnp.sum(pieces.astype(F32), 0)
    index = (lax.axis_index("dp") * lax.axis_size("x") + lax.axis_index("x")) * nz + lax.axis_index("z")
    is_up = index < 2 * (half // HEAD)
    ny = lax.axis_size("y")
    spread = jnp.broadcast_to(chunk.astype(BF16)[None], (2 * ny, 32, HEAD))
    shared = lax.all_to_all(spread, ("core", "y"), 0, 0, tiled=True)
    from_core = jnp.arange(2 * ny, dtype=jnp.int32) // ny
    from_y = jnp.arange(2 * ny, dtype=jnp.int32) % ny
    keep = jnp.where(is_up, from_core == core, from_y == lax.axis_index("y"))
    total = jnp.sum(jnp.where(keep[:, None, None], shared.astype(F32), 0.0), 0)
    spread = jnp.broadcast_to(total.astype(BF16)[None], (64, 32, HEAD))
    gathered = lax.all_to_all(spread, GROUP + ("core",), 0, 0, tiled=True)
    up_total, adapter_total = finish(gathered, width // HEAD, adapters.shape[1:])

    ret_str = lax.ppermute(back_str, chain, chip_step(-1, False))
    ret_crs = lax.ppermute(back_crs, chain, chip_step(-1, True))
    other_in = lax.ppermute(other, "core", swap)
    near_out = (mine + ret_str.astype(F32)).astype(BF16)
    far_out = (other_in.astype(F32) + ret_crs.astype(F32)).astype(BF16)
    first = core == 0
    out = jnp.concatenate([jnp.where(first, near_out, far_out), jnp.where(first, far_out, near_out)], 2)
    return out[0][None, None], out[1][None, None], adapter_total[None], up_total


def solution(mesh):
    sizes = dict(mesh.shape)
    wide = Mesh(
        mesh.devices.reshape(sizes["dp"], 2, sizes["context"] // 4, 2, sizes["embodime"]),
        ("dp", "x", "z", "core", "y"),
    )
    frames = P("dp", "y", ("x", "z", "core"), None)
    rows = P("dp", "y", None)
    return jax.shard_map(
        local,
        mesh=wide,
        in_specs=(frames,) * 5 + (rows, rows, P("y", None, None, None), P()),
        out_specs=(frames, frames, P("y", None, None, None), P()),
        check_vma=False,
    )
```

time: 567 us -> 134 us (0.24)
  waiting for transfers between devices: 470 us -> 49.4 us
  starting transfers between devices: 13.2 us -> 48.7 us
  matrix products: 25 us -> 0 us
  between operations: 16.5 us -> 0.85 us
  Pallas kernels: 0 us -> 13.8 us
  local copies, waits for them, and re-layouts: 24.9 us -> 14.3 us
  other arithmetic: 16 us -> 5.84 us
    psum x2 -> x0, waiting for transfers between devices: 422 us -> none  [the longest x1 274 us: local(): up_total = lax.psum(up_term, ('dp', 'context', 'embodime'))]
    all_to_all x0 -> x3, starting transfers between devices: none -> 28.6 us  [the longest x1 10.9 us: local(): pieces = lax.all_to_all(payload, GROUP, 0, 0, tiled=True)]
    all_to_all x0 -> x3, waiting for transfers between devices: none -> 25.7 us  [the longest x1 14.7 us: local(): gathered = lax.all_to_all(spread, GROUP + ('core',), 0, 0, tiled=True)]
    ppermute x4 -> x7, waiting for transfers between devices: 48.6 us -> 23.6 us  [the longest x1 14 us: local(): straight = lax.ppermute(near_pair, chain, chip_step(1, False))]
    dot_general x21 -> x0, matrix products: 25 us -> none  [the longest x3 6.68 us: local(): jnp.einsum('hqk,qhe->khe', dscore, query3, preferred_element_type=jnp.flo...]
    pallas_call x0 -> x2, Pallas kernels: none -> 13.8 us  [the longest x1 11.8 us: attend(): pl.pallas_call(functools.partial(attend_kernel, lengths.shape[0], steps),...]
    another operation x7 -> x2, local copies, waits for them, and re-layouts: 12.1 us -> 1.3 us  [the longest x1 1.22 us: local(): far_all = jnp.stack([far(q), far(g), far(k), far(v)])]
    ppermute x4 -> x7, starting transfers between devices: 12.9 us -> 20.1 us  [the longest x1 8.92 us: local(): oth = lax.ppermute(far_all, 'core', swap)]
  transfers between devices with their start and end apart: 6 -> 10, of which waited for: 6 -> 6; matrix products, arithmetic and copies ran while one was open for 5% -> 5% of each run, Pallas kernels for 0% -> 0%
where the time goes in v1:
time: 134 us; the launch traced here: 133 us
  waiting for transfers between devices  49.4 us (37%)
  starting transfers between devices  48.7 us (36%)
  local copies, waits for them, and re-layouts  14.3 us (11%)
  Pallas kernels  13.8 us (10%)
  other arithmetic  5.84 us (4%)
    all_to_all x1, waiting for transfers between devices, local(): gathered = lax.all_to_all(spread, GROUP + ('core',), 0, 0, tiled=True)  14.7 us
    ppermute x1, waiting for transfers between devices, local(): straight = lax.ppermute(near_pair, chain, chip_step(1, False))  14 us
    pallas_call x1, Pallas kernels, attend(): pl.pallas_call(functools.partial(attend_kernel, lengths.shape[0], steps),...  11.8 us
    unnamed x36, local copies, waits for them, and re-layouts  11.5 us
    all_to_all x1, starting transfers between devices, local(): pieces = lax.all_to_all(payload, GROUP, 0, 0, tiled=True)  10.9 us
    all_to_all x1, starting transfers between devices, local(): shared = lax.all_to_all(spread, ('core', 'y'), 0, 0, tiled=True)  10.7 us
    ppermute x1, waiting for transfers between devices, local(): cross = lax.ppermute(far_all[2:], chain, chip_step(1, True))  8.95 us
    ppermute x1, starting transfers between devices, local(): oth = lax.ppermute(far_all, 'core', swap)  8.92 us
  transfers between devices with their start and end apart: 10, of which 6 were waited for; matrix products, arithmetic and copies ran while one was open for 5% of the time, Pallas kernels for 0%

profile of v1, /device:TPU:1, one launch (start us, length us, event | category | flops | bytes accessed | tf_op | source)
XLA Modules:
  0.0 132.9 jit_solution(1602865734534409722)
XLA Ops:
  0.7 1.2 dynamic-slice_bitcast_fusion.4
  2.2 1.3 pad_maximum_fusion
  3.5 8.9 %collective-permute-start.1 = (bf16[4,128,1280]{2,1,0:T(8,128)(2,1)}, bf16[4,128,1280]{2,1,0:T(8,128)(2,1)S(1)}, u32[]{:S(2)}, u32[]{:S(2)}) collective-permute-start(bf16[4,128,1280]{2,1,0:T(8,128)(2,1)} %pad_maximum_fusion), channel_id=1, source_target_pairs={{0,8},{8,0},{1,9},{9,1},{2,10},{10,2},{3,11},{11,3},{4,12},{12,4},... | collective-permute-start | bytes 3932168 | tf_op jit(solution)/shard_map/ppermute | solution.py:264
  13.3 1.3 collective-permute-start.3
  15.5 1.3 collective-permute-start.2
  16.9 2.6 %collective-permute-start = (bf16[128,128]{1,0:T(8,128)(2,1)S(1)}, bf16[128,128]{1,0:T(8,128)(2,1)S(1)}, u32[]{:S(2)}, u32[]{:S(2)}) collective-permute-start(bf16[128,128]{1,0:T(8,128)(2,1)S(1)} %bitcast.32), channel_id=1, source_target_pairs={{0,8},{8,0},{1,9},{9,1},{2,10},{10,2},{3,11},{11,3},{4,12},{12,4},... | collective-permute-start | bytes 98312 | tf_op jit(solution)/shard_map/ppermute | solution.py:265
  20.3 8.9 %collective-permute-done.3.k_crs.v_crs = bf16[2,128,1280]{2,1,0:T(8,128)(2,1)S(1)} collective-permute-done((bf16[2,128,1280]{2,1,0:T(8,128)(2,1)}, bf16[2,128,1280]{2,1,0:T(8,128)(2,1)S(1)}, u32[]{:S(2)}, u32[]{:S(2)}) %collective-permute-start.3) | collective-permute-done | bytes 655392 | tf_op jit(solution)/shard_map/ppermute | solution.py:263
  29.2 14.0 %collective-permute-done.2.k_str.v_str = bf16[2,128,1280]{2,1,0:T(8,128)(2,1)S(1)} collective-permute-done((bf16[2,128,1280]{2,1,0:T(8,128)(2,1)}, bf16[2,128,1280]{2,1,0:T(8,128)(2,1)S(1)}, u32[]{:S(2)}, u32[]{:S(2)}) %collective-permute-start.2) | collective-permute-done | bytes 655392 | tf_op jit(solution)/shard_map/ppermute | solution.py:262
  44.4 1.1 copy-done.3
  45.5 1.1 copy-done.4
  47.5 11.8 %attend.1 = (f32[2,128,1280]{2,1,0:T(8,128)S(1)}, bf16[2,128,1280]{2,1,0:T(8,128)(2,1)S(1)}, bf16[2,128,1280]{2,1,0:T(8,128)(2,1)S(1)}, bf16[2,128,1280]{2,1,0:T(8,128)(2,1)S(1)}, bf16[32,32,128]{2,1,0:T(8,128)(2,1)S(1)}) custom-call(s32[2]{0:T(128)S(1)} %pad_add_fusion.place, s32[16]{0:T(128)S(1)} %bitcast.34, s32[16]{0:T(128)S(1)} %bitcast.35, ...), custom_call_target="tpu_custom_call" | custom-call | flops 1677721600 | bytes 12582912 | tf_op jit(solution)/shard_map/attend/pallas_call | solution.py:188
  63.7 10.9 %all-to-all-start = ((bf16[32,32,128]{2,1,0:T(8,128)(2,1)}), bf16[32,32,128]{2,1,0:T(8,128)(2,1)S(1)}, u32[]{:S(2)}, u32[]{:S(2)}) async-start(bf16[32,32,128]{2,1,0:T(8,128)(2,1)} %copy-done.8), calls=%async_computation | async-start | bytes 524288 | tf_op jit(solution)/shard_map/all_to_all | solution.py:272
  74.5 1.4 %collective-permute-start.4 = (bf16[2,128,1280]{2,1,0:T(8,128)(2,1)}, bf16[2,128,1280]{2,1,0:T(8,128)(2,1)S(1)}, u32[]{:S(2)}, u32[]{:S(2)}) collective-permute-start(bf16[2,128,1280]{2,1,0:T(8,128)(2,1)} %copy-done.14), channel_id=1, source_target_pairs={{16,0},{24,8},{32,16},{40,24},{48,32},{56,40},{64,48},{72,56},{80,... | collective-permute-start | bytes 1966088 | tf_op jit(solution)/shard_map/ppermute | solution.py:287
  76.0 3.2 %collective-permute-start.5 = (bf16[2,128,1280]{2,1,0:T(8,128)(2,1)}, bf16[2,128,1280]{2,1,0:T(8,128)(2,1)S(1)}, u32[]{:S(2)}, u32[]{:S(2)}) collective-permute-start(bf16[2,128,1280]{2,1,0:T(8,128)(2,1)} %copy-done.13), channel_id=1, source_target_pairs={{0,8},{8,0},{1,9},{9,1},{2,10},{10,2},{3,11},{11,3},{4,12},{12,4},... | collective-permute-start | bytes 1966088 | tf_op jit(solution)/shard_map/ppermute | solution.py:289
  79.2 1.3 collective-permute-start.6
  80.5 3.7 %all-to-all-done = bf16[32,32,128]{2,1,0:T(8,128)(2,1)S(1)} async-done(((bf16[32,32,128]{2,1,0:T(8,128)(2,1)}), bf16[32,32,128]{2,1,0:T(8,128)(2,1)S(1)}, u32[]{:S(2)}, u32[]{:S(2)}) %all-to-all-start) | async-done | bytes 262176 | tf_op jit(solution)/shard_map/all_to_all | solution.py:272
  85.0 10.7 %all-to-all-start.1 = ((bf16[16,32,128]{2,1,0:T(8,128)(2,1)}), bf16[16,32,128]{2,1,0:T(8,128)(2,1)S(1)}, u32[]{:S(2)}, u32[]{:S(2)}) async-start(bf16[16,32,128]{2,1,0:T(8,128)(2,1)} %broadcast_in_dim.29), calls=%async_computation.1 | async-start | bytes 262144 | tf_op jit(solution)/shard_map/all_to_all | solution.py:278
  95.7 7.3 %all-to-all-done.1 = bf16[16,32,128]{2,1,0:T(8,128)(2,1)S(1)} async-done(((bf16[16,32,128]{2,1,0:T(8,128)(2,1)}), bf16[16,32,128]{2,1,0:T(8,128)(2,1)S(1)}, u32[]{:S(2)}, u32[]{:S(2)}) %all-to-all-start.1) | async-done | bytes 131104 | tf_op jit(solution)/shard_map/all_to_all | solution.py:278
  103.9 7.1 %all-to-all-start.2 = ((bf16[64,32,128]{2,1,0:T(8,128)(2,1)}), bf16[64,32,128]{2,1,0:T(8,128)(2,1)S(1)}, u32[]{:S(2)}, u32[]{:S(2)}) async-start(bf16[64,32,128]{2,1,0:T(8,128)(2,1)} %broadcast_in_dim.31), calls=%async_computation.2 | async-start | bytes 1048576 | tf_op jit(solution)/shard_map/all_to_all | solution.py:284
  111.0 1.4 %broadcast_select_fusion = (bf16[2,128,1280]{2,1,0:T(8,128)(2,1)S(1)}, bf16[2,128,1280]{2,1,0:T(8,128)(2,1)S(1)}) fusion(pred[]{:T(512)S(6)} %eq.25, bf16[2,128,1280]{2,1,0:T(8,128)(2,1)} %collective-permute-done.6, bf16[2,128,1280]{2,1,0:T(8,128)(2,1)S(1)} %collective-permute-done.5, f32[2,128,1280]{2,1,0:T(8,128)S(1)} %copy-done.6, ...), kind=kLoop, calls=%fused_computation.11 | loop fusion | flops 2949120 | bytes 4587521 | tf_op jit(solution)/shard_map/jit(_where)/select_n | solution.py:293
  112.5 1.1 fusion.2
  113.6 14.7 %all-to-all-done.2.gathered = bf16[64,32,128]{2,1,0:T(8,128)(2,1)S(1)} async-done(((bf16[64,32,128]{2,1,0:T(8,128)(2,1)}), bf16[64,32,128]{2,1,0:T(8,128)(2,1)S(1)}, u32[]{:S(2)}, u32[]{:S(2)}) %all-to-all-start.2) | async-done | bytes 524320 | tf_op jit(solution)/shard_map/all_to_all | solution.py:284
  129.1 2.0 %finish.1 = (f32[64,2560]{1,0:T(8,128)}, f32[4,128,64]{2,1,0:T(8,128)}) custom-call(bf16[64,32,128]{2,1,0:T(8,128)(2,1)} %copy-done.15), custom_call_target="tpu_custom_call" | custom-call | tf_op jit(solution)/shard_map/finish/pallas_call | solution.py:222
  131.2 1.7 %copy.16 = f32[1,4,128,64]{2,3,1,0:T(8,128)} copy(f32[1,4,128,64]{3,2,1,0:T(8,128)} %bitcast.36) | data formatting | bytes 262144
  (47 shorter events, 11.8 us)
Async XLA Ops:
  0.6 1.3 copy-start.1
  0.6 1.5 %copy-start = (bf16[1,1,128,2560]{3,2,1,0:T(8,128)(2,1)S(1)}, bf16[1,1,128,2560]{3,2,1,0:T(8,128)(2,1)}, u32[]{:S(2)}) copy-start(bf16[1,1,128,2560]{3,2,1,0:T(8,128)(2,1)} %param.10) | copy-start | bytes 1966084
  3.5 13.4 %copy-start.9 = (bf16[1,1,128,128]{3,2,1,0:T(8,128)(2,1)S(1)}, bf16[1,1,128,128]{3,2,1,0:T(8,128)(2,1)}, u32[]{:S(2)}) copy-start(bf16[1,1,128,128]{3,2,1,0:T(8,128)(2,1)} %param.13) | copy-start | bytes 98308
  3.5 16.1 %copy-start.16 = (bf16[1,4,128,64]{2,3,1,0:T(8,128)(2,1)S(1)}, bf16[1,4,128,64]{2,3,1,0:T(8,128)(2,1)}, u32[]{:S(2)}) copy-start(bf16[1,4,128,64]{2,3,1,0:T(8,128)(2,1)} %param.16) | copy-start | bytes 196612
  3.5 39.8 %copy-start.10 = (s32[1,1,16]{2,1,0:T(1,128)S(1)}, s32[1,1,16]{2,1,0:T(1,128)}, u32[]{:S(2)}) copy-start(s32[1,1,16]{2,1,0:T(1,128)} %param.14) | copy-start | bytes 196
  3.5 39.8 %copy-start.11 = (s32[1,1,16]{2,1,0:T(1,128)S(1)}, s32[1,1,16]{2,1,0:T(1,128)}, u32[]{:S(2)}) copy-start(s32[1,1,16]{2,1,0:T(1,128)} %param.15) | copy-start | bytes 196
  3.5 39.8 %collective-permute-start.1 = (bf16[4,128,1280]{2,1,0:T(8,128)(2,1)}, bf16[4,128,1280]{2,1,0:T(8,128)(2,1)S(1)}, u32[]{:S(2)}, u32[]{:S(2)}) collective-permute-start(bf16[4,128,1280]{2,1,0:T(8,128)(2,1)} %pad_maximum_fusion), channel_id=1, source_target_pairs={{0,8},{8,0},{1,9},{9,1},{2,10},{10,2},{3,11},{11,3},{4,12},{12,4},... | collective-permute-start | bytes 3932168 | tf_op jit(solution)/shard_map/ppermute | solution.py:264
  13.3 15.9 %collective-permute-start.3 = (bf16[2,128,1280]{2,1,0:T(8,128)(2,1)}, bf16[2,128,1280]{2,1,0:T(8,128)(2,1)S(1)}, u32[]{:S(2)}, u32[]{:S(2)}) collective-permute-start(bf16[2,128,1280]{2,1,0:T(8,128)(2,1)} %pad_maximum_fusion.3), channel_id=1, source_target_pairs={{0,24},{8,16},{16,40},{24,32},{32,56},{40,48},{48,72},{56,64},{64,... | collective-permute-start | bytes 1966088 | tf_op jit(solution)/shard_map/ppermute | solution.py:263
  15.5 27.8 %collective-permute-start.2 = (bf16[2,128,1280]{2,1,0:T(8,128)(2,1)}, bf16[2,128,1280]{2,1,0:T(8,128)(2,1)S(1)}, u32[]{:S(2)}, u32[]{:S(2)}) collective-permute-start(bf16[2,128,1280]{2,1,0:T(8,128)(2,1)} %pad_maximum_fusion.2), channel_id=1, source_target_pairs={{0,16},{8,24},{16,32},{24,40},{32,48},{40,56},{48,64},{56,72},{64,... | collective-permute-start | bytes 1966088 | tf_op jit(solution)/shard_map/ppermute | solution.py:262
  16.9 3.4 %collective-permute-start = (bf16[128,128]{1,0:T(8,128)(2,1)S(1)}, bf16[128,128]{1,0:T(8,128)(2,1)S(1)}, u32[]{:S(2)}, u32[]{:S(2)}) collective-permute-start(bf16[128,128]{1,0:T(8,128)(2,1)S(1)} %bitcast.32), channel_id=1, source_target_pairs={{0,8},{8,0},{1,9},{9,1},{2,10},{10,2},{3,11},{11,3},{4,12},{12,4},... | collective-permute-start | bytes 98312 | tf_op jit(solution)/shard_map/ppermute | solution.py:265
  43.3 1.1 copy-start.2
  44.4 1.1 copy-start.3
  45.5 1.1 copy-start.4
  46.6 1.0 copy-start.7
  59.3 1.1 copy-start.5
  61.1 0.8 copy-start.12
  62.0 0.8 copy-start.13
  63.7 20.6 %all-to-all-start = ((bf16[32,32,128]{2,1,0:T(8,128)(2,1)}), bf16[32,32,128]{2,1,0:T(8,128)(2,1)S(1)}, u32[]{:S(2)}, u32[]{:S(2)}) async-start(bf16[32,32,128]{2,1,0:T(8,128)(2,1)} %copy-done.8), calls=%async_computation | async-start | bytes 524288 | tf_op jit(solution)/shard_map/all_to_all | solution.py:272
  74.5 36.5 %copy-start.6 = (f32[2,128,1280]{2,1,0:T(8,128)S(1)}, f32[2,128,1280]{2,1,0:T(8,128)}, u32[]{:S(2)}) copy-start(f32[2,128,1280]{2,1,0:T(8,128)} %copy-done.5) | copy-start | bytes 3932164
  74.5 36.5 %collective-permute-start.4 = (bf16[2,128,1280]{2,1,0:T(8,128)(2,1)}, bf16[2,128,1280]{2,1,0:T(8,128)(2,1)S(1)}, u32[]{:S(2)}, u32[]{:S(2)}) collective-permute-start(bf16[2,128,1280]{2,1,0:T(8,128)(2,1)} %copy-done.14), channel_id=1, source_target_pairs={{16,0},{24,8},{32,16},{40,24},{48,32},{56,40},{64,48},{72,56},{80,... | collective-permute-start | bytes 1966088 | tf_op jit(solution)/shard_map/ppermute | solution.py:287
  76.0 35.0 %collective-permute-start.5 = (bf16[2,128,1280]{2,1,0:T(8,128)(2,1)}, bf16[2,128,1280]{2,1,0:T(8,128)(2,1)S(1)}, u32[]{:S(2)}, u32[]{:S(2)}) collective-permute-start(bf16[2,128,1280]{2,1,0:T(8,128)(2,1)} %copy-done.13), channel_id=1, source_target_pairs={{0,8},{8,0},{1,9},{9,1},{2,10},{10,2},{3,11},{11,3},{4,12},{12,4},... | collective-permute-start | bytes 1966088 | tf_op jit(solution)/shard_map/ppermute | solution.py:289
  79.2 31.8 %collective-permute-start.6 = (bf16[2,128,1280]{2,1,0:T(8,128)(2,1)}, bf16[2,128,1280]{2,1,0:T(8,128)(2,1)}, u32[]{:S(2)}, u32[]{:S(2)}) collective-permute-start(bf16[2,128,1280]{2,1,0:T(8,128)(2,1)} %copy-done.12), channel_id=1, source_target_pairs={{16,8},{24,0},{32,24},{40,16},{48,40},{56,32},{64,56},{72,48},{80,... | collective-permute-start | bytes 1966088 | tf_op jit(solution)/shard_map/ppermute | solution.py:288
  85.0 18.0 %all-to-all-start.1 = ((bf16[16,32,128]{2,1,0:T(8,128)(2,1)}), bf16[16,32,128]{2,1,0:T(8,128)(2,1)S(1)}, u32[]{:S(2)}, u32[]{:S(2)}) async-start(bf16[16,32,128]{2,1,0:T(8,128)(2,1)} %broadcast_in_dim.29), calls=%async_computation.1 | async-start | bytes 262144 | tf_op jit(solution)/shard_map/all_to_all | solution.py:278
  103.9 24.4 %all-to-all-start.2 = ((bf16[64,32,128]{2,1,0:T(8,128)(2,1)}), bf16[64,32,128]{2,1,0:T(8,128)(2,1)S(1)}, u32[]{:S(2)}, u32[]{:S(2)}) async-start(bf16[64,32,128]{2,1,0:T(8,128)(2,1)} %broadcast_in_dim.31), calls=%async_computation.2 | async-start | bytes 1048576 | tf_op jit(solution)/shard_map/all_to_all | solution.py:284
  (3 other events, 2.4 us)

commit v2 on v1

v2 whole, which is shorter than its diff:
```python
import functools
import math

import jax
import jax.numpy as jnp
from jax import lax
from jax.experimental import pallas as pl
from jax.experimental.pallas import tpu as pltpu
from jax.sharding import Mesh, PartitionSpec as P

HEAD = 128
TOK = 128
RANK = 64
FIRST = 8
LOW = -1e30
SCALE = HEAD**-0.5
SCALE2 = SCALE * math.log2(math.e)
F32 = jnp.float32
BF16 = jnp.bfloat16
GROUP = ("dp", "x", "z")


def dot(a, b, ca, cb):
    return lax.dot_general(a, b, (((ca,), (cb,)), ((), ())), preferred_element_type=F32)


def clip_of(frame, lengths, robots, clips):
    begin = jnp.int32(0)
    start = jnp.int32(0)
    robot = jnp.int32(0)
    for i in range(clips):
        size = lengths[i]
        inside = jnp.logical_and(frame >= begin, frame < begin + size)
        start = jnp.where(inside, begin, start)
        robot = jnp.where(inside, robots[i], robot)
        begin = begin + size
    return start, robot


def attend_kernel(
    clips, heads, offset, chunks, place, lengths, robots,
    act_own, adapters, oth, straight, cross, early, agrad_in,
    q_hbm, g_hbm, k_hbm, v_hbm, up_hbm, *refs,
):
    last = early is not None
    refs = refs[4:] if last else refs
    mine_hbm, other_hbm, str_hbm, crs_hbm, payload, agrad_out = refs[:6]
    own, up, mine, other, back_str, back_crs, adapted, adapted_t, agrad_t, sem_in, sem_out = refs[6:]
    core = place[0]
    first = core == 0
    half = oth.shape[1] // 4 // HEAD * HEAD
    width = heads * HEAD
    far = pl.ds(pl.multiple_of(core * half + offset * HEAD, HEAD), width)
    loads = [
        pltpu.make_async_copy(x.at[:, far], own.at[n], sem_in.at[n])
        for n, x in enumerate((q_hbm, g_hbm, k_hbm, v_hbm))
    ]
    loads.append(pltpu.make_async_copy(up_hbm.at[:, far], up, sem_in.at[4]))
    for load in loads:
        load.start()
    frame_a = 2 * place[1]
    frame_b = frame_a + 1
    start_a, robot_a = clip_of(frame_a, lengths, robots, clips)
    start_b, robot_b = clip_of(frame_b, lengths, robots, clips)

    def bias(valid):
        return jnp.where(valid, jnp.float32(0), jnp.float32(LOW))

    bias_a = (bias(frame_a - 2 >= start_a), bias(frame_a - 1 >= start_a), jnp.float32(0))
    bias_b = (bias(frame_b - 2 >= start_b), bias(frame_b - 1 >= start_b), jnp.float32(0))

    def pick(one, two):
        return jnp.where(first, one, two)

    def pair(one, two):
        return [pick(one, two), pick(two, one)]

    acts = pair(act_own[...], oth[:, 4 * half:])
    for n, (act, robot) in enumerate(zip(acts, (robot_a, robot_b))):
        table = adapters[robot]
        adapted[n * TOK:(n + 1) * TOK, :] = dot(act, table, 1, 1).astype(BF16)
        adapted_t[:, n * TOK:(n + 1) * TOK] = dot(table, act, 1, 1).astype(BF16)
    agrad_t[...] = agrad_in[...] if last else jnp.zeros_like(agrad_t)
    for load in loads:
        load.wait()

    def soften(raw, prod, biases):
        scores = [raw[n * TOK:(n + 1) * TOK] * SCALE2 + b for n, b in enumerate(biases)]
        top = functools.reduce(jnp.maximum, scores)
        top = jnp.max(top, 0, keepdims=True)
        weights = [jnp.exp2(s - top) for s in scores]
        prods = [prod[n * TOK:(n + 1) * TOK] for n in range(len(biases))]
        total = jnp.sum(functools.reduce(jnp.add, weights), 0, keepdims=True)
        mixed = [w * p for w, p in zip(weights, prods)]
        moment = jnp.sum(functools.reduce(jnp.add, mixed), 0, keepdims=True)
        inverse = 1.0 / total
        delta = moment * inverse
        scaled = inverse * SCALE
        prob = [(w * inverse).astype(BF16) for w in weights]
        dscore = [((w * scaled) * (p - delta)).astype(BF16) for w, p in zip(weights, prods)]
        return prob, dscore

    none = jnp.zeros((TOK, TOK), BF16)

    def one_head(h):
        at = pl.multiple_of(h * HEAD, HEAD)
        cols = pl.ds(at, HEAD)

        def theirs(n):
            return oth[:, pl.ds(pl.multiple_of(n * half + offset * HEAD + at, HEAD), HEAD)]

        up_h = up[:, cols]
        shift = dot(adapted[...], up_h, 1, 0)
        q_tok = jnp.concatenate(pair(own[0, :, cols], theirs(0)), 0)
        query = (q_tok.astype(F32) + shift).astype(BF16)
        grad = jnp.concatenate(pair(own[1, :, cols], theirs(1)), 0)
        keys = jnp.concatenate(pair(straight[0, :, cols], cross[0, :, cols]) + pair(own[2, :, cols], theirs(2)), 0)
        values = jnp.concatenate(pair(straight[1, :, cols], cross[1, :, cols]) + pair(own[3, :, cols], theirs(3)), 0)
        raw = dot(keys, query, 1, 1)
        prod = dot(values, grad, 1, 1)
        prob_a, dscore_a = soften(raw[: 3 * TOK, :TOK], prod[: 3 * TOK, :TOK], bias_a)
        prob_b, dscore_b = soften(raw[TOK:, TOK:], prod[TOK:, TOK:], bias_b)
        prob = jnp.concatenate(
            [jnp.concatenate(prob_a + [none], 0), jnp.concatenate([none] + prob_b, 0)], 1
        )
        dscore = jnp.concatenate(
            [jnp.concatenate(dscore_a + [none], 0), jnp.concatenate([none] + dscore_b, 0)], 1
        )
        query_grad = dot(keys, dscore, 0, 0)
        high = query_grad.astype(BF16)
        low = (query_grad - high.astype(F32)).astype(BF16)
        agrad_t[...] += dot(up_h, high, 1, 0) + dot(up_h, low, 1, 0)
        up_term = dot(adapted_t[...], high, 1, 1) + dot(adapted_t[...], low, 1, 1)
        chunk = 2 * h + (2 * offset if last else 0)
        payload[pl.ds(chunk, 2)] = up_term.reshape(2, 32, HEAD).astype(BF16)
        for n, part in enumerate((dot(dscore, query, 1, 0), dot(prob, grad, 1, 0))):
            p0, p1 = part[:TOK].astype(BF16), part[TOK:2 * TOK].astype(BF16)
            a, b = part[2 * TOK:3 * TOK], part[3 * TOK:]
            back_str[n, :, cols] = pick(p0, p1)
            back_crs[n, :, cols] = pick(p1, p0)
            mine[n, :, cols] = pick(a, b)
            other[n, :, cols] = pick(b, a).astype(BF16)

    if heads <= 2:
        for h in range(heads):
            one_head(h)
    else:
        @pl.loop(0, heads // 2)
        def _(j):
            one_head(2 * j)
            one_head(2 * j + 1)

    span = pl.ds(offset * HEAD, width)
    stores = [
        pltpu.make_async_copy(x, y.at[:, :, span], sem_out.at[n])
        for n, (x, y) in enumerate(
            ((back_str, str_hbm), (back_crs, crs_hbm), (other, other_hbm), (mine, mine_hbm))
        )
    ]
    for store in stores:
        store.start()
    if last:
        payload[: early.shape[0]] = early[...]
        terms = []
        for n, act in enumerate(acts):
            whole = agrad_t[:, n * TOK:(n + 1) * TOK]
            high = whole.astype(BF16)
            low = (whole - high.astype(F32)).astype(BF16)
            terms.append(dot(high, act, 1, 0) + dot(low, act, 1, 0))
        zero = jnp.zeros((RANK, HEAD), F32)
        base = 2 * (offset + heads)
        for s in range(4):
            term = jnp.where(robot_a == s, terms[0], zero) + jnp.where(robot_b == s, terms[1], zero)
            payload[base + 2 * s:base + 2 * s + 2] = term.reshape(2, 32, HEAD).astype(BF16)
        payload[base + 8:] = jnp.zeros((chunks - base - 8, 32, HEAD), BF16)
    else:
        agrad_out[...] = agrad_t[...]
    for store in stores:
        store.wait()


def attend(scalars, act_own, adapters, oth, straight, cross, own, up, offset, before=None):
    heads = straight.shape[2] // HEAD
    half = own[0].shape[1] // 2
    last = before is not None
    chunks = 32 if last else 2 * heads
    smem = pl.BlockSpec(memory_space=pltpu.SMEM)
    vmem = pl.BlockSpec(memory_space=pltpu.VMEM)
    hbm = pl.BlockSpec(memory_space=pl.ANY)
    shape = (2, TOK, half)
    part = (2, TOK, heads * HEAD)

    def fixed(x):
        return pltpu.with_memory_space_constraint(x, pltpu.HBM)

    inputs = [*scalars, act_own, adapters, oth, straight, cross]
    specs = [smem] * 3 + [vmem] * 5
    aliases = {}
    if last:
        inputs += [before[4], before[5]]
        specs += [vmem] * 2
    inputs += [fixed(x) for x in (*own, up)]
    specs += [hbm] * 5
    if last:
        aliases = {len(inputs) + n: n for n in range(4)}
        inputs += [fixed(x) for x in before[:4]]
        specs += [hbm] * 4
    body = functools.partial(attend_kernel, scalars[1].shape[0], heads, offset, chunks)

    def kernel(*refs):
        refs = list(refs)
        if not last:
            refs[8:8] = [None, None]
        if last:
            refs.insert(len(inputs) + 5, None)
        body(*refs)

    out_shape = [
        pltpu.HBM(shape, F32), pltpu.HBM(shape, BF16), pltpu.HBM(shape, BF16), pltpu.HBM(shape, BF16),
        jax.ShapeDtypeStruct((chunks, 32, HEAD), BF16),
    ]
    out_specs = [hbm] * 4 + [vmem]
    if not last:
        out_shape.append(jax.ShapeDtypeStruct((RANK, 2 * TOK), F32))
        out_specs.append(vmem)
    return pl.pallas_call(
        kernel,
        in_specs=specs,
        out_specs=out_specs,
        out_shape=out_shape,
        input_output_aliases=aliases,
        scratch_shapes=[
            pltpu.VMEM((4, TOK, heads * HEAD), BF16),
            pltpu.VMEM((RANK, heads * HEAD), BF16),
            pltpu.VMEM(part, F32),
            pltpu.VMEM(part, BF16),
            pltpu.VMEM(part, BF16),
            pltpu.VMEM(part, BF16),
            pltpu.VMEM((2 * TOK, RANK), BF16),
            pltpu.VMEM((RANK, 2 * TOK), BF16),
            pltpu.VMEM((RANK, 2 * TOK), F32),
            pltpu.SemaphoreType.DMA((5,)),
            pltpu.SemaphoreType.DMA((4,)),
        ],
        compiler_params=pltpu.CompilerParams(vmem_limit_bytes=24 * 1024 * 1024),
        cost_estimate=pl.CostEstimate(
            flops=2 * heads * 5 * 512 * 256 * 128, bytes_accessed=heads * 1024 * 1024, transcendentals=heads * 512 * 256
        ),
        name="attend_last" if last else "attend_first",
    )(*inputs)


def finish_kernel(heads, place, gathered, swapped, up_grad, adapter_grad):
    per_core = heads // 2
    for n, part in enumerate((gathered, swapped)):
        side = place[0] if n == 0 else 1 - place[0]
        for h in range(per_core):
            cols = pl.ds(pl.multiple_of((side * per_core + h) * HEAD, HEAD), HEAD)
            up_grad[:32, cols] = part[2 * h].astype(F32)
            up_grad[32:, cols] = part[2 * h + 1].astype(F32)
    for s in range(4):
        for n in range(2):
            at = 2 * per_core + 2 * s + n
            adapter_grad[s, n * 32:(n + 1) * 32] = gathered[at].astype(F32) + swapped[at].astype(F32)


def finish(place, gathered, swapped, heads):
    vmem = pl.BlockSpec(memory_space=pltpu.VMEM)
    return pl.pallas_call(
        functools.partial(finish_kernel, heads),
        in_specs=[pl.BlockSpec(memory_space=pltpu.SMEM), vmem, vmem],
        out_specs=[vmem, vmem],
        out_shape=[
            jax.ShapeDtypeStruct((RANK, heads * HEAD), F32),
            jax.ShapeDtypeStruct((4, RANK, HEAD), F32),
        ],
        compiler_params=pltpu.CompilerParams(vmem_limit_bytes=4 * 1024 * 1024),
        name="finish",
    )(place, gathered, swapped)


def local(
    query_tokens, key_tokens, value_tokens, out_grad, actions, clip_lengths, clip_robots, adapters, up_proj,
):
    q, k, v, g = (t[0, 0] for t in (query_tokens, key_tokens, value_tokens, out_grad))
    act = actions[0, 0]
    width = q.shape[1]
    half = width // 2
    core = lax.axis_index("core")
    nz = lax.axis_size("z")
    chips = lax.axis_size("x") * nz
    chip = lax.axis_index("x") * nz + lax.axis_index("z")
    chain = ("x", "z", "core")

    def cut(array, side, begin, size):
        return lax.dynamic_slice_in_dim(array, side * half + begin, size, 1)

    def chip_step(by, flip):
        return [
            (2 * c + i, 2 * (c + by) + ((1 - i) if flip else i))
            for c in range(chips)
            for i in range(2)
            if 0 <= c + by < chips
        ]

    swap = [(0, 1), (1, 0)]
    split = FIRST * HEAD
    moved = []
    for begin, size in ((0, split), (split, half - split)):
        for side, flip in ((core, False), (1 - core, True)):
            both = jnp.stack([cut(k, side, begin, size), cut(v, side, begin, size)])
            moved.append(lax.ppermute(both, chain, chip_step(1, flip)))
    oth = lax.ppermute(
        jnp.concatenate([cut(t, 1 - core, 0, half) for t in (q, g, k, v)] + [act], 1), "core", swap
    )
    place = jnp.stack([core, chip]).astype(jnp.int32)
    scalars = (place, clip_lengths[0, 0], clip_robots[0, 0])
    table = jnp.swapaxes(adapters[0], 1, 2)
    own = (q, g, k, v)
    before = attend(scalars, act, table, oth, moved[0], moved[1], own, up_proj, 0)
    mine, other, back_str, back_crs, payload = attend(
        scalars, act, table, oth, moved[2], moved[3], own, up_proj, FIRST, before
    )

    pieces = lax.all_to_all(payload, GROUP, 0, 0, tiled=True)
    chunk = jnp.sum(pieces.astype(F32), 0)
    index = (lax.axis_index("dp") * lax.axis_size("x") + lax.axis_index("x")) * nz + lax.axis_index("z")
    is_up = index < 2 * (half // HEAD)
    ny = lax.axis_size("y")
    shared = lax.all_to_all(jnp.broadcast_to(chunk.astype(BF16)[None], (ny, 32, HEAD)), "y", 0, 0, tiled=True)
    keep = jnp.logical_or(is_up, jnp.arange(ny, dtype=jnp.int32) == lax.axis_index("y"))
    total = jnp.sum(jnp.where(keep[:, None, None], shared.astype(F32), 0.0), 0)
    gathered = lax.all_to_all(jnp.broadcast_to(total.astype(BF16)[None], (32, 32, HEAD)), GROUP, 0, 0, tiled=True)
    swapped = lax.ppermute(gathered, "core", swap)
    up_total, adapter_total = finish(place, gathered, swapped, width // HEAD)
    adapter_total = jnp.swapaxes(adapter_total, 1, 2)

    ret_str = lax.ppermute(back_str, chain, chip_step(-1, False))
    ret_crs = lax.ppermute(back_crs, chain, chip_step(-1, True))
    other_in = lax.ppermute(other, "core", swap)
    near_out = (mine + ret_str.astype(F32)).astype(BF16)
    far_out = (other_in.astype(F32) + ret_crs.astype(F32)).astype(BF16)
    first = core == 0
    out = jnp.concatenate([jnp.where(first, near_out, far_out), jnp.where(first, far_out, near_out)], 2)
    return out[0][None, None], out[1][None, None], adapter_total[None], up_total


def solution(mesh):
    sizes = dict(mesh.shape)
    wide = Mesh(
        mesh.devices.reshape(sizes["dp"], 2, sizes["context"] // 4, 2, sizes["embodime"]),
        ("dp", "x", "z", "core", "y"),
    )
    frames = P("dp", "y", ("x", "z", "core"), None)
    rows = P("dp", "y", None)
    return jax.shard_map(
        local,
        mesh=wide,
        in_specs=(frames,) * 5 + (rows, rows, P("y", None, None, None), P()),
        out_specs=(frames, frames, P("y", None, None, None), P()),
        check_vma=False,
    )
```

time: 134 us -> 120 us (0.90)
  waiting for transfers between devices: 49.4 us -> 30.8 us
  starting transfers between devices: 48.7 us -> 56.9 us
  local copies, waits for them, and re-layouts: 14.3 us -> 8.15 us
  Pallas kernels: 13.8 us -> 17.8 us
    ppermute x4 -> x6, waiting for transfers between devices: 23.6 us -> 10.1 us  [the longest x4 10.1 us: local(): moved.append(lax.ppermute(both, chain, chip_step(1, flip)))]
    ppermute x4 -> x6, starting transfers between devices: 14.1 us -> 27.3 us  [the longest x4 12.4 us: local(): moved.append(lax.ppermute(both, chain, chip_step(1, flip)))]
    all_to_all x2, waiting for transfers between devices: 22 us -> 10.3 us  [the longest x1 7.22 us: local(): lax.all_to_all(jnp.broadcast_to(chunk.astype(BF16)[None], (ny, 32, HEAD))...]
    unnamed x36 -> x22, local copies, waits for them, and re-layouts: 11.5 us -> 5.15 us
    all_to_all x2, starting transfers between devices: 17.8 us -> 13 us  [the longest x1 6.83 us: local(): lax.all_to_all(jnp.broadcast_to(chunk.astype(BF16)[None], (ny, 32, HEAD))...]
    ppermute x1, waiting for transfers between devices: 0.01 us -> 4.61 us  [local(): ret_crs = lax.ppermute(back_crs, chain, chip_step(-1, True))]
    pallas_call x2 -> x3, Pallas kernels: 13.8 us -> 17.8 us  [the longest x2 16.3 us: attend(): pl.pallas_call(kernel, in_specs=specs, out_specs=out_specs, out_shape=out...]
    all_to_all x1, waiting for transfers between devices: 3.75 us -> 5.78 us  [local(): pieces = lax.all_to_all(payload, GROUP, 0, 0, tiled=True)]
  transfers between devices with their start and end apart: 10 -> 12, of which waited for: 6 -> 5; matrix products, arithmetic and copies ran while one was open for 5% -> 6% of each run, Pallas kernels for 0% -> 9%
where the time goes in v2:
time: 120 us; the launch traced here: 119 us
  starting transfers between devices  56.9 us (47%)
  waiting for transfers between devices  30.8 us (26%)
  Pallas kernels  17.8 us (15%)
  local copies, waits for them, and re-layouts  8.15 us (7%)
  other arithmetic  4.94 us (4%)
    pallas_call x2, Pallas kernels, attend(): pl.pallas_call(kernel, in_specs=specs, out_specs=out_specs, out_shape=out...  16.3 us
    ppermute x4, starting transfers between devices, local(): moved.append(lax.ppermute(both, chain, chip_step(1, flip)))  12.4 us
    all_to_all x1, starting transfers between devices, local(): pieces = lax.all_to_all(payload, GROUP, 0, 0, tiled=True)  11.8 us
    ppermute x4, waiting for transfers between devices, local(): moved.append(lax.ppermute(both, chain, chip_step(1, flip)))  10.1 us
    ppermute x1, starting transfers between devices, local(): lax.ppermute(jnp.concatenate([cut(t, 1 - core, 0, half) for t in (q, g, k...  8.77 us
    all_to_all x1, waiting for transfers between devices, local(): lax.all_to_all(jnp.broadcast_to(chunk.astype(BF16)[None], (ny, 32, HEAD))...  7.22 us
    all_to_all x1, starting transfers between devices, local(): lax.all_to_all(jnp.broadcast_to(chunk.astype(BF16)[None], (ny, 32, HEAD))...  6.83 us
    all_to_all x1, starting transfers between devices, local(): lax.all_to_all(jnp.broadcast_to(total.astype(BF16)[None], (32, 32, HEAD))...  6.21 us
  transfers between devices with their start and end apart: 12, of which 5 were waited for; matrix products, arithmetic and copies ran while one was open for 6% of the time, Pallas kernels for 9%

profile of v2, /device:TPU:1, one launch (start us, length us, event | category | flops | bytes accessed | tf_op | source)
XLA Modules:
  0.0 119.4 jit_solution(7796143463774503270)
XLA Ops:
  0.7 1.8 %bitcast_dynamic-update-slice_fusion.3 = bf16[128,5248]{1,0:T(8,128)(2,1)} fusion(bf16[1,1,128,2560]{3,2,1,0:T(8,128)(2,1)} %param.9, s32[]{:T(128)S(6)} %select_n.37), kind=kLoop, calls=%fused_computation.15 | loop fusion | bytes 655364
  2.5 1.7 %bitcast_dynamic-update-slice_fusion.2 = bf16[128,5248]{1,0:T(8,128)(2,1)} fusion(bf16[128,5248]{1,0:T(8,128)(2,1)} %bitcast_dynamic-update-slice_fusion.3, bf16[1,1,128,2560]{3,2,1,0:T(8,128)(2,1)} %param.12, s32[]{:T(128)S(6)} %select_n.37), kind=kLoop, calls=%fused_computation.14 | loop fusion | bytes 655364
  6.4 8.8 %collective-permute-start = (bf16[128,5248]{1,0:T(8,128)(2,1)}, bf16[128,5248]{1,0:T(8,128)(2,1)S(1)}, u32[]{:S(2)}, u32[]{:S(2)}) collective-permute-start(bf16[128,5248]{1,0:T(8,128)(2,1)} %constant_dynamic-update-slice_fusion), channel_id=1, source_target_pairs={{0,8},{8,0},{1,9},{9,1},{2,10},{10,2},{3,11},{11,3},{4,12},{12,4},... | collective-permute-start | bytes 4030472 | tf_op jit(solution)/shard_map/ppermute | solution.py:313
  16.2 1.3 %collective-permute-start.3 = (bf16[2,128,1024]{2,1,0:T(8,128)(2,1)}, bf16[2,128,1024]{2,1,0:T(8,128)(2,1)S(1)}, u32[]{:S(2)}, u32[]{:S(2)}) collective-permute-start(bf16[2,128,1024]{2,1,0:T(8,128)(2,1)} %pad_maximum_fusion.1), channel_id=1, source_target_pairs={{0,16},{8,24},{16,32},{24,40},{32,48},{40,56},{48,64},{56,72},{64,... | collective-permute-start | bytes 1572872 | tf_op jit(solution)/shard_map/ppermute | solution.py:312
  18.3 1.5 %collective-permute-start.4 = (bf16[2,128,1024]{2,1,0:T(8,128)(2,1)}, bf16[2,128,1024]{2,1,0:T(8,128)(2,1)S(1)}, u32[]{:S(2)}, u32[]{:S(2)}) collective-permute-start(bf16[2,128,1024]{2,1,0:T(8,128)(2,1)} %pad_maximum_fusion.2), channel_id=1, source_target_pairs={{0,24},{8,16},{16,40},{24,32},{32,56},{40,48},{48,72},{56,64},{64,... | collective-permute-start | bytes 1572872 | tf_op jit(solution)/shard_map/ppermute | solution.py:312
  20.8 4.0 %collective-permute-start.1 = (bf16[2,128,256]{2,1,0:T(8,128)(2,1)S(1)}, bf16[2,128,256]{2,1,0:T(8,128)(2,1)S(1)}, u32[]{:S(2)}, u32[]{:S(2)}) collective-permute-start(bf16[2,128,256]{2,1,0:T(8,128)(2,1)S(1)} %pad_maximum_fusion.3), channel_id=1, source_target_pairs={{0,16},{8,24},{16,32},{24,40},{32,48},{40,56},{48,64},{56,72},{64,... | collective-permute-start | bytes 393224 | tf_op jit(solution)/shard_map/ppermute | solution.py:312
  24.8 5.6 %collective-permute-start.2 = (bf16[2,128,256]{2,1,0:T(8,128)(2,1)S(1)}, bf16[2,128,256]{2,1,0:T(8,128)(2,1)S(1)}, u32[]{:S(2)}, u32[]{:S(2)}) collective-permute-start(bf16[2,128,256]{2,1,0:T(8,128)(2,1)S(1)} %pad_maximum_fusion.4), channel_id=1, source_target_pairs={{0,24},{8,16},{16,40},{24,32},{32,56},{40,48},{48,72},{56,64},{64,... | collective-permute-start | bytes 393224 | tf_op jit(solution)/shard_map/ppermute | solution.py:312
  30.5 10.1 %collective-permute-done.4.refs_7_ = bf16[2,128,1024]{2,1,0:T(8,128)(2,1)S(1)} collective-permute-done((bf16[2,128,1024]{2,1,0:T(8,128)(2,1)}, bf16[2,128,1024]{2,1,0:T(8,128)(2,1)S(1)}, u32[]{:S(2)}, u32[]{:S(2)}) %collective-permute-start.4) | collective-permute-done | bytes 524320 | tf_op jit(solution)/shard_map/ppermute | solution.py:312
  40.5 11.1 %attend_first.1 = (f32[2,128,1280]{2,1,0:T(8,128)}, bf16[2,128,1280]{2,1,0:T(8,128)(2,1)}, bf16[2,128,1280]{2,1,0:T(8,128)(2,1)}, bf16[2,128,1280]{2,1,0:T(8,128...) custom-call(s32[2]{0:T(128)S(1)} %pad_add_fusion.refs_0_.place, s32[16]{0:T(128)S(1)} %bitcast.48, ...), custom_call_target="tpu_custom_call" | custom-call | flops 1342177280 | bytes 8388608 | tf_op jit(solution)/shard_map/attend_first/pallas_call | solution.py:226
  51.6 5.2 %attend_last.1 = (f32[2,128,1280]{2,1,0:T(8,128)}, bf16[2,128,1280]{2,1,0:T(8,128)(2,1)}, bf16[2,128,1280]{2,1,0:T(8,128)(2,1)}, bf16[2,128,1280]{2,1,0:T(8,128)(2,1)}, bf16[32,32,128]{2,1,0:T(8,128)(2,1)}) custom-call(s32[2]{0:T(128)S(1)} %pad_add_fusion.refs_0_.place, ...), custom_call_target="tpu_custom_call", output_to_operand_aliasing={{0}: (15, {}), {1}: (16, {}), {2}: (17, {}), {3}: (18, {})} | custom-call | flops 335544320 | bytes 2097152 | tf_op jit(solution)/shard_map/attend_last/pallas_call | solution.py:226
  56.9 11.8 %all-to-all-start = ((bf16[32,32,128]{2,1,0:T(8,128)(2,1)}), bf16[32,32,128]{2,1,0:T(8,128)(2,1)S(1)}, u32[]{:S(2)}, u32[]{:S(2)}) async-start(bf16[32,32,128]{2,1,0:T(8,128)(2,1)} %get-tuple-element.27), calls=%async_computation | async-start | bytes 524288 | tf_op jit(solution)/shard_map/all_to_all | solution.py:325
  68.7 1.3 %collective-permute-start.5 = (bf16[2,128,1280]{2,1,0:T(8,128)(2,1)}, bf16[2,128,1280]{2,1,0:T(8,128)(2,1)S(1)}, u32[]{:S(2)}, u32[]{:S(2)}) collective-permute-start(bf16[2,128,1280]{2,1,0:T(8,128)(2,1)} %get-tuple-element.24), channel_id=1, source_target_pairs={{16,0},{24,8},{32,16},{40,24},{48,32},{56,40},{64,48},{72,56},{80,... | collective-permute-start | bytes 1966088 | tf_op jit(solution)/shard_map/ppermute | solution.py:338
  70.0 2.1 %collective-permute-start.6 = (bf16[2,128,1280]{2,1,0:T(8,128)(2,1)}, bf16[2,128,1280]{2,1,0:T(8,128)(2,1)S(1)}, u32[]{:S(2)}, u32[]{:S(2)}) collective-permute-start(bf16[2,128,1280]{2,1,0:T(8,128)(2,1)} %get-tuple-element.25), channel_id=1, source_target_pairs={{0,8},{8,0},{1,9},{9,1},{2,10},{10,2},{3,11},{11,3},{4,12},{12,4},... | collective-permute-start | bytes 1966088 | tf_op jit(solution)/shard_map/ppermute | solution.py:340
  72.1 1.3 %collective-permute-start.7 = (bf16[2,128,1280]{2,1,0:T(8,128)(2,1)}, bf16[2,128,1280]{2,1,0:T(8,128)(2,1)}, u32[]{:S(2)}, u32[]{:S(2)}) collective-permute-start(bf16[2,128,1280]{2,1,0:T(8,128)(2,1)} %get-tuple-element.26), channel_id=1, source_target_pairs={{16,8},{24,0},{32,24},{40,16},{48,40},{56,32},{64,56},{72,48},{80,... | collective-permute-start | bytes 1966088 | tf_op jit(solution)/shard_map/ppermute | solution.py:339
  73.4 5.8 %all-to-all-done = bf16[32,32,128]{2,1,0:T(8,128)(2,1)S(1)} async-done(((bf16[32,32,128]{2,1,0:T(8,128)(2,1)}), bf16[32,32,128]{2,1,0:T(8,128)(2,1)S(1)}, u32[]{:S(2)}, u32[]{:S(2)}) %all-to-all-start) | async-done | bytes 262176 | tf_op jit(solution)/shard_map/all_to_all | solution.py:325
  79.9 6.8 %all-to-all-start.1 = ((bf16[8,32,128]{2,1,0:T(8,128)(2,1)}), bf16[8,32,128]{2,1,0:T(8,128)(2,1)S(1)}, u32[]{:S(2)}, u32[]{:S(2)}) async-start(bf16[8,32,128]{2,1,0:T(8,128)(2,1)} %broadcast_in_dim.29), calls=%async_computation.1 | async-start | bytes 131072 | tf_op jit(solution)/shard_map/all_to_all | solution.py:330
  86.7 7.2 %all-to-all-done.1 = bf16[8,32,128]{2,1,0:T(8,128)(2,1)S(1)} async-done(((bf16[8,32,128]{2,1,0:T(8,128)(2,1)}), bf16[8,32,128]{2,1,0:T(8,128)(2,1)S(1)}, u32[]{:S(2)}, u32[]{:S(2)}) %all-to-all-start.1) | async-done | bytes 65568 | tf_op jit(solution)/shard_map/all_to_all | solution.py:330
  94.8 6.2 %all-to-all-start.2 = ((bf16[32,32,128]{2,1,0:T(8,128)(2,1)}), bf16[32,32,128]{2,1,0:T(8,128)(2,1)S(1)}, u32[]{:S(2)}, u32[]{:S(2)}) async-start(bf16[32,32,128]{2,1,0:T(8,128)(2,1)} %broadcast_in_dim.31), calls=%async_computation.2 | async-start | bytes 524288 | tf_op jit(solution)/shard_map/all_to_all | solution.py:333
  101.1 4.6 %collective-permute-done.7 = bf16[2,128,1280]{2,1,0:T(8,128)(2,1)} collective-permute-done((bf16[2,128,1280]{2,1,0:T(8,128)(2,1)}, bf16[2,128,1280]{2,1,0:T(8,128)(2,1)}, u32[]{:S(2)}, u32[]{:S(2)}) %collective-permute-start.7) | collective-permute-done | bytes 655392 | tf_op jit(solution)/shard_map/ppermute | solution.py:339
  105.7 1.9 %broadcast_select_fusion = (bf16[2,128,1280]{2,1,0:T(8,128)(2,1)S(1)}, bf16[2,128,1280]{2,1,0:T(8,128)(2,1)S(1)}) fusion(pred[]{:T(512)S(6)} %eq.13, bf16[2,128,1280]{2,1,0:T(8,128)(2,1)} %collective-permute-done.7, bf16[2,128,1280]{2,1,0:T(8,128)(2,1)} %copy-done.8, f32[2,128,1280]{2,1,0:T(8,128)S(1)} %copy-done.6, bf16[2,128,1280]{2,1,0:T(8,128)(2,1)} %copy-done.7), kind=kLoop, calls=%fused_computation.8 | loop fusion | flops 2949120 | bytes 4587521 | tf_op jit(solution)/shard_map/jit(_where)/select_n | solution.py:344
  107.5 3.1 %all-to-all-done.2.gathered = bf16[32,32,128]{2,1,0:T(8,128)(2,1)S(1)} async-done(((bf16[32,32,128]{2,1,0:T(8,128)(2,1)}), bf16[32,32,128]{2,1,0:T(8,128)(2,1)S(1)}, u32[]{:S(2)}, u32[]{:S(2)}) %all-to-all-start.2) | async-done | bytes 262176 | tf_op jit(solution)/shard_map/all_to_all | solution.py:333
  110.7 6.2 %collective-permute-start.8 = (bf16[32,32,128]{2,1,0:T(8,128)(2,1)S(1)}, bf16[32,32,128]{2,1,0:T(8,128)(2,1)S(1)}, u32[]{:S(2)}, u32[]{:S(2)}) collective-permute-start(bf16[32,32,128]{2,1,0:T(8,128)(2,1)S(1)} %all-to-all-done.2.gathered), channel_id=1, source_target_pairs={{0,8},{8,0},{1,9},{9,1},{2,10},{10,2},{3,11},{11,3},{4,12},{12,4},... | collective-permute-start | bytes 786440 | tf_op jit(solution)/shard_map/ppermute | solution.py:334
  116.8 1.1 fusion.2
  118.0 1.5 %finish.1 = (f32[64,2560]{1,0:T(8,128)}, f32[4,64,128]{2,1,0:T(8,128)}) custom-call(s32[2]{0:T(128)S(1)} %pad_add_fusion.refs_0_.place, bf16[32,32,128]{2,1,0:T(8,128)(2,1)S(1)} %all-to-all-done.2.gathered, bf16[32,32,128]{2,1,0:T(8,128)(2,1)S(1)} %collective-permute-done.8.swapped), custom_call_target="tpu_custom_call" | custom-call | tf_op jit(solution)/shard_map/finish/pallas_call | solution.py:269
  (40 shorter events, 6.5 us)
Async XLA Ops:
  0.6 3.6 %copy-start.4 = (bf16[1,1,128,2560]{3,2,1,0:T(8,128)(2,1)S(1)}, bf16[1,1,128,2560]{3,2,1,0:T(8,128)(2,1)}, u32[]{:S(2)}) copy-start(bf16[1,1,128,2560]{3,2,1,0:T(8,128)(2,1)} %param.10) | copy-start | bytes 1966084
  0.6 4.4 %copy-start.5 = (bf16[1,1,128,2560]{3,2,1,0:T(8,128)(2,1)S(1)}, bf16[1,1,128,2560]{3,2,1,0:T(8,128)(2,1)}, u32[]{:S(2)}) copy-start(bf16[1,1,128,2560]{3,2,1,0:T(8,128)(2,1)} %param.11) | copy-start | bytes 1966084
  0.7 5.1 %copy-start = (bf16[1,1,128,128]{3,2,1,0:T(8,128)(2,1)S(1)}, bf16[1,1,128,128]{3,2,1,0:T(8,128)(2,1)}, u32[]{:S(2)}) copy-start(bf16[1,1,128,128]{3,2,1,0:T(8,128)(2,1)} %param.13) | copy-start | bytes 98308
  6.4 34.1 %collective-permute-start = (bf16[128,5248]{1,0:T(8,128)(2,1)}, bf16[128,5248]{1,0:T(8,128)(2,1)S(1)}, u32[]{:S(2)}, u32[]{:S(2)}) collective-permute-start(bf16[128,5248]{1,0:T(8,128)(2,1)} %constant_dynamic-update-slice_fusion), channel_id=1, source_target_pairs={{0,8},{8,0},{1,9},{9,1},{2,10},{10,2},{3,11},{11,3},{4,12},{12,4},... | collective-permute-start | bytes 4030472 | tf_op jit(solution)/shard_map/ppermute | solution.py:313
  15.3 25.2 %copy-start.1 = (bf16[1,4,128,64]{2,3,1,0:T(8,128)(2,1)S(1)}, bf16[1,4,128,64]{2,3,1,0:T(8,128)(2,1)}, u32[]{:S(2)}) copy-start(bf16[1,4,128,64]{2,3,1,0:T(8,128)(2,1)} %param.16) | copy-start | bytes 196612
  15.3 25.2 %copy-start.2 = (s32[1,1,16]{2,1,0:T(1,128)S(1)}, s32[1,1,16]{2,1,0:T(1,128)}, u32[]{:S(2)}) copy-start(s32[1,1,16]{2,1,0:T(1,128)} %param.14) | copy-start | bytes 196
  15.3 25.2 %copy-start.3 = (s32[1,1,16]{2,1,0:T(1,128)S(1)}, s32[1,1,16]{2,1,0:T(1,128)}, u32[]{:S(2)}) copy-start(s32[1,1,16]{2,1,0:T(1,128)} %param.15) | copy-start | bytes 196
  16.2 14.3 %collective-permute-start.3 = (bf16[2,128,1024]{2,1,0:T(8,128)(2,1)}, bf16[2,128,1024]{2,1,0:T(8,128)(2,1)S(1)}, u32[]{:S(2)}, u32[]{:S(2)}) collective-permute-start(bf16[2,128,1024]{2,1,0:T(8,128)(2,1)} %pad_maximum_fusion.1), channel_id=1, source_target_pairs={{0,16},{8,24},{16,32},{24,40},{32,48},{40,56},{48,64},{56,72},{64,... | collective-permute-start | bytes 1572872 | tf_op jit(solution)/shard_map/ppermute | solution.py:312
  18.3 22.2 %collective-permute-start.4 = (bf16[2,128,1024]{2,1,0:T(8,128)(2,1)}, bf16[2,128,1024]{2,1,0:T(8,128)(2,1)S(1)}, u32[]{:S(2)}, u32[]{:S(2)}) collective-permute-start(bf16[2,128,1024]{2,1,0:T(8,128)(2,1)} %pad_maximum_fusion.2), channel_id=1, source_target_pairs={{0,24},{8,16},{16,40},{24,32},{32,56},{40,48},{48,72},{56,64},{64,... | collective-permute-start | bytes 1572872 | tf_op jit(solution)/shard_map/ppermute | solution.py:312
  20.8 30.8 %collective-permute-start.1 = (bf16[2,128,256]{2,1,0:T(8,128)(2,1)S(1)}, bf16[2,128,256]{2,1,0:T(8,128)(2,1)S(1)}, u32[]{:S(2)}, u32[]{:S(2)}) collective-permute-start(bf16[2,128,256]{2,1,0:T(8,128)(2,1)S(1)} %pad_maximum_fusion.3), channel_id=1, source_target_pairs={{0,16},{8,24},{16,32},{24,40},{32,48},{40,56},{48,64},{56,72},{64,... | collective-permute-start | bytes 393224 | tf_op jit(solution)/shard_map/ppermute | solution.py:312
  24.8 26.9 %collective-permute-start.2 = (bf16[2,128,256]{2,1,0:T(8,128)(2,1)S(1)}, bf16[2,128,256]{2,1,0:T(8,128)(2,1)S(1)}, u32[]{:S(2)}, u32[]{:S(2)}) collective-permute-start(bf16[2,128,256]{2,1,0:T(8,128)(2,1)S(1)} %pad_maximum_fusion.4), channel_id=1, source_target_pairs={{0,24},{8,16},{16,40},{24,32},{32,56},{40,48},{48,72},{56,64},{64,... | collective-permute-start | bytes 393224 | tf_op jit(solution)/shard_map/ppermute | solution.py:312
  56.9 48.8 %copy-start.6 = (f32[2,128,1280]{2,1,0:T(8,128)S(1)}, f32[2,128,1280]{2,1,0:T(8,128)}, u32[]{:S(2)}) copy-start(f32[2,128,1280]{2,1,0:T(8,128)} %get-tuple-element.23) | copy-start | bytes 3932164
  56.9 22.3 %all-to-all-start = ((bf16[32,32,128]{2,1,0:T(8,128)(2,1)}), bf16[32,32,128]{2,1,0:T(8,128)(2,1)S(1)}, u32[]{:S(2)}, u32[]{:S(2)}) async-start(bf16[32,32,128]{2,1,0:T(8,128)(2,1)} %get-tuple-element.27), calls=%async_computation | async-start | bytes 524288 | tf_op jit(solution)/shard_map/all_to_all | solution.py:325
  68.7 32.3 %collective-permute-start.5 = (bf16[2,128,1280]{2,1,0:T(8,128)(2,1)}, bf16[2,128,1280]{2,1,0:T(8,128)(2,1)S(1)}, u32[]{:S(2)}, u32[]{:S(2)}) collective-permute-start(bf16[2,128,1280]{2,1,0:T(8,128)(2,1)} %get-tuple-element.24), channel_id=1, source_target_pairs={{16,0},{24,8},{32,16},{40,24},{48,32},{56,40},{64,48},{72,56},{80,... | collective-permute-start | bytes 1966088 | tf_op jit(solution)/shard_map/ppermute | solution.py:338
  70.0 31.0 %collective-permute-start.6 = (bf16[2,128,1280]{2,1,0:T(8,128)(2,1)}, bf16[2,128,1280]{2,1,0:T(8,128)(2,1)S(1)}, u32[]{:S(2)}, u32[]{:S(2)}) collective-permute-start(bf16[2,128,1280]{2,1,0:T(8,128)(2,1)} %get-tuple-element.25), channel_id=1, source_target_pairs={{0,8},{8,0},{1,9},{9,1},{2,10},{10,2},{3,11},{11,3},{4,12},{12,4},... | collective-permute-start | bytes 1966088 | tf_op jit(solution)/shard_map/ppermute | solution.py:340
  72.1 33.5 %collective-permute-start.7 = (bf16[2,128,1280]{2,1,0:T(8,128)(2,1)}, bf16[2,128,1280]{2,1,0:T(8,128)(2,1)}, u32[]{:S(2)}, u32[]{:S(2)}) collective-permute-start(bf16[2,128,1280]{2,1,0:T(8,128)(2,1)} %get-tuple-element.26), channel_id=1, source_target_pairs={{16,8},{24,0},{32,24},{40,16},{48,40},{56,32},{64,56},{72,48},{80,... | collective-permute-start | bytes 1966088 | tf_op jit(solution)/shard_map/ppermute | solution.py:339
  79.9 14.1 %all-to-all-start.1 = ((bf16[8,32,128]{2,1,0:T(8,128)(2,1)}), bf16[8,32,128]{2,1,0:T(8,128)(2,1)S(1)}, u32[]{:S(2)}, u32[]{:S(2)}) async-start(bf16[8,32,128]{2,1,0:T(8,128)(2,1)} %broadcast_in_dim.29), calls=%async_computation.1 | async-start | bytes 131072 | tf_op jit(solution)/shard_map/all_to_all | solution.py:330
  94.8 15.9 %all-to-all-start.2 = ((bf16[32,32,128]{2,1,0:T(8,128)(2,1)}), bf16[32,32,128]{2,1,0:T(8,128)(2,1)S(1)}, u32[]{:S(2)}, u32[]{:S(2)}) async-start(bf16[32,32,128]{2,1,0:T(8,128)(2,1)} %broadcast_in_dim.31), calls=%async_computation.2 | async-start | bytes 524288 | tf_op jit(solution)/shard_map/all_to_all | solution.py:333
  101.0 4.6 %copy-start.7 = (bf16[2,128,1280]{2,1,0:T(8,128)(2,1)}, bf16[2,128,1280]{2,1,0:T(8,128)(2,1)S(1)}, u32[]{:S(2)}) copy-start(bf16[2,128,1280]{2,1,0:T(8,128)(2,1)S(1)} %collective-permute-done.5) | copy-start | bytes 1966084
  101.0 4.6 %copy-start.8 = (bf16[2,128,1280]{2,1,0:T(8,128)(2,1)}, bf16[2,128,1280]{2,1,0:T(8,128)(2,1)S(1)}, u32[]{:S(2)}) copy-start(bf16[2,128,1280]{2,1,0:T(8,128)(2,1)S(1)} %collective-permute-done.6) | copy-start | bytes 1966084
  110.7 7.3 %collective-permute-start.8 = (bf16[32,32,128]{2,1,0:T(8,128)(2,1)S(1)}, bf16[32,32,128]{2,1,0:T(8,128)(2,1)S(1)}, u32[]{:S(2)}, u32[]{:S(2)}) collective-permute-start(bf16[32,32,128]{2,1,0:T(8,128)(2,1)S(1)} %all-to-all-done.2.gathered), channel_id=1, source_target_pairs={{0,8},{8,0},{1,9},{9,1},{2,10},{10,2},{3,11},{11,3},{4,12},{12,4},... | collective-permute-start | bytes 786440 | tf_op jit(solution)/shard_map/ppermute | solution.py:334

commit v3 on v2

v3 whole, which is shorter than its diff:
```python
import functools
import math

import jax
import jax.numpy as jnp
from jax import lax
from jax.experimental import pallas as pl
from jax.experimental.pallas import tpu as pltpu
from jax.sharding import Mesh, PartitionSpec as P

HEAD = 128
TOK = 128
RANK = 64
SPLIT = 3
LOW = -1e30
SCALE = HEAD**-0.5
SCALE2 = SCALE * math.log2(math.e)
F32 = jnp.float32
BF16 = jnp.bfloat16
GROUP = ("dp", "x", "z")
MIB = 1024 * 1024


def dot(a, b, ca, cb):
    return lax.dot_general(a, b, (((ca,), (cb,)), ((), ())), preferred_element_type=F32)


def clip_of(frame, lengths, robots, clips):
    begin = jnp.int32(0)
    start = jnp.int32(0)
    robot = jnp.int32(0)
    for i in range(clips):
        size = lengths[i]
        inside = jnp.logical_and(frame >= begin, frame < begin + size)
        start = jnp.where(inside, begin, start)
        robot = jnp.where(inside, robots[i], robot)
        begin = begin + size
    return start, robot


def smem():
    return pl.BlockSpec(memory_space=pltpu.SMEM)


def vmem():
    return pl.BlockSpec(memory_space=pltpu.VMEM)


def hbm():
    return pl.BlockSpec(memory_space=pl.ANY)


def fixed(x):
    return pltpu.with_memory_space_constraint(x, pltpu.HBM)


def take_kernel(far, place, q, g, k, v, act, out, sems):
    half = q.shape[1] // 2
    side = 1 - place[0] if far else place[0]
    copies = [
        pltpu.make_async_copy(
            x.at[:, pl.ds(pl.multiple_of(side * half, HEAD), half)], out.at[:, pl.ds(n * half, half)], sems.at[n]
        )
        for n, x in enumerate((q, g, k, v))
    ]
    copies.append(pltpu.make_async_copy(act, out.at[:, pl.ds(4 * half, HEAD)], sems.at[4]))
    for copy in copies:
        copy.start()
    for copy in copies:
        copy.wait()


def take_half(place, own, act, far):
    half = own[0].shape[1] // 2
    return pl.pallas_call(
        functools.partial(take_kernel, far),
        in_specs=[smem()] + [hbm()] * 5,
        out_specs=vmem(),
        out_shape=pltpu.VMEM((TOK, 4 * half + HEAD), BF16),
        scratch_shapes=[pltpu.SemaphoreType.DMA((5,))],
        compiler_params=pltpu.CompilerParams(vmem_limit_bytes=8 * MIB),
        cost_estimate=pl.CostEstimate(flops=0, bytes_accessed=4 * MIB, transcendentals=0),
        name="take_far" if far else "take_near",
    )(place, *(fixed(x) for x in own), fixed(act))


def pack_kernel(clips, begin, heads, place, lengths, robots, near, oth, up, down):
    half = near.shape[1] // 4 // HEAD * HEAD
    quarter = half // 2
    first = place[0] == 0
    frame_a = 2 * place[1]
    start_n, _ = clip_of(frame_a + 2, lengths, robots, clips)
    wide = start_n == frame_a
    width = heads * HEAD

    def frame(is_a, array, group):
        at = array * half + group * quarter + begin * HEAD
        one, two = near[:, at:at + width], oth[:, at:at + width]
        return jnp.where(first, one, two) if is_a else jnp.where(first, two, one)

    for n, array in enumerate((2, 3)):
        up[:, n * width:(n + 1) * width] = frame(False, array, 0)
        up[:, (2 + n) * width:(3 + n) * width] = jnp.where(wide, frame(True, array, 0), frame(False, array, 1))
    for n in range(4):
        down[:, n * width:(n + 1) * width] = frame(True, n, 1)
    one, two = near[:, 4 * half:], oth[:, 4 * half:]
    down[:, 4 * width:] = jnp.where(first, one, two)


def pack(scalars, near, oth, begin, heads):
    width = heads * HEAD
    return pl.pallas_call(
        functools.partial(pack_kernel, scalars[1].shape[0], begin, heads),
        in_specs=[smem()] * 3 + [vmem()] * 2,
        out_specs=[vmem()] * 2,
        out_shape=[
            jax.ShapeDtypeStruct((TOK, 4 * width), BF16),
            jax.ShapeDtypeStruct((TOK, 4 * width + HEAD), BF16),
        ],
        compiler_params=pltpu.CompilerParams(vmem_limit_bytes=8 * MIB),
        cost_estimate=pl.CostEstimate(flops=0, bytes_accessed=4 * MIB, transcendentals=0),
        name="pack",
    )(*scalars, near, oth)


def attend_kernel(
    clips, begin, heads, place, lengths, robots,
    adapters, near, oth, below, above, early, agrad_in, up_hbm, *refs,
):
    last = early is not None
    refs = refs[4:] if last else refs
    sum_a, sum_b, ret_down, ret_up, payload, agrad_out = refs[:6]
    up, keep_a, keep_b, keep_down, keep_up, adapted, adapted_t, agrad_t, sem_in, sem_out = refs[6:]
    core = place[0]
    first = core == 0
    half = near.shape[1] // 4 // HEAD * HEAD
    quarter = half // 2
    five = quarter // HEAD
    width = heads * HEAD
    loads = [
        pltpu.make_async_copy(
            up_hbm.at[:, pl.ds(pl.multiple_of(core * half + n * quarter + begin * HEAD, HEAD), width)],
            up.at[n], sem_in.at[n],
        )
        for n in range(2)
    ]
    for load in loads:
        load.start()
    frame_a = 2 * place[1]
    start_a, robot_a = clip_of(frame_a, lengths, robots, clips)
    start_b, robot_b = clip_of(frame_a + 1, lengths, robots, clips)
    start_n, robot_n = clip_of(frame_a + 2, lengths, robots, clips)
    wide_below = start_a == frame_a - 2
    wide_above = start_n == frame_a

    def bias(valid):
        return jnp.where(valid, jnp.float32(0), jnp.float32(LOW))

    zero = jnp.float32(0)
    bias_a = (bias(wide_below), bias(start_a <= frame_a - 1), zero)
    bias_b = (bias(start_b <= frame_a - 1), bias(start_b <= frame_a), zero)
    scale_a = jnp.where(wide_below, 0.0, 1.0).astype(F32)
    scale_n = jnp.where(wide_above, 1.0, 0.0).astype(F32)

    def pick(one, two):
        return jnp.where(first, one, two)

    def pair(one, two):
        return [pick(one, two), pick(two, one)]

    acts = pair(near[:, 4 * half:], oth[:, 4 * half:]) + [above[:, 4 * width:]]
    for n, (act, robot) in enumerate(zip(acts, (robot_a, robot_b, robot_n))):
        table = adapters[robot]
        adapted[n * TOK:(n + 1) * TOK, :] = dot(act, table, 1, 1).astype(BF16)
        adapted_t[:, n * TOK:(n + 1) * TOK] = dot(table, act, 1, 1).astype(BF16)
    agrad_t[...] = agrad_in[...] if last else jnp.zeros_like(agrad_t)
    for load in loads:
        load.wait()

    def soften(raw, prods, biases, keep=None):
        scores = [r * SCALE2 + b for r, b in zip(raw, biases)]
        top = jnp.max(functools.reduce(jnp.maximum, scores), 0, keepdims=True)
        weights = [jnp.exp2(s - top) for s in scores]
        total = jnp.sum(functools.reduce(jnp.add, weights), 0, keepdims=True)
        mixed = [w * p for w, p in zip(weights, prods)]
        moment = jnp.sum(functools.reduce(jnp.add, mixed), 0, keepdims=True)
        inverse = 1.0 / total
        if keep is not None:
            inverse = inverse * keep
        delta = moment * inverse
        scaled = inverse * SCALE
        prob = [(w * inverse).astype(BF16) for w in weights]
        dscore = [((w * scaled) * (p - delta)).astype(BF16) for w, p in zip(weights, prods)]
        return prob, dscore

    def block(x, i, j):
        return x[i * TOK:(i + 1) * TOK, j * TOK:(j + 1) * TOK]

    def column(blocks):
        return jnp.concatenate(blocks, 0)

    none = jnp.zeros((TOK, TOK), BF16)

    def sums(keys, dscore, up_h, rows, where):
        query_grad = dot(keys, dscore, 0, 0)
        high = query_grad.astype(BF16)
        low = (query_grad - high.astype(F32)).astype(BF16)
        agrad_t[:, :rows] += dot(up_h, high, 1, 0) + dot(up_h, low, 1, 0)
        term = dot(adapted_t[:, :rows], high, 1, 1) + dot(adapted_t[:, :rows], low, 1, 1)
        payload[pl.ds(where, 2)] = term.reshape(2, 32, HEAD).astype(BF16)

    def one_pair(j):
        at = pl.multiple_of(j * HEAD, HEAD)
        cols = pl.ds(at, HEAD)

        def there(n, group):
            return pl.ds(pl.multiple_of(n * half + group * quarter + begin * HEAD + at, HEAD), HEAD)

        def both(n, group):
            return pair(near[:, there(n, group)], oth[:, there(n, group)])

        def lower(n):
            return below[:, pl.ds(pl.multiple_of(n * width + at, HEAD), HEAD)]

        def upper(n):
            return above[:, pl.ds(pl.multiple_of(n * width + at, HEAD), HEAD)]

        up_h = up[0, :, cols]
        shift = dot(adapted[: 2 * TOK], up_h, 1, 0)
        query = (column(both(0, 0)).astype(F32) + shift).astype(BF16)
        grad = column(both(1, 0))
        keys = column([lower(2), lower(0)] + both(2, 0))
        values = column([lower(3), lower(1)] + both(3, 0))
        raw = dot(keys, query, 1, 1)
        prod = dot(values, grad, 1, 1)
        prob_a, dscore_a = soften([block(raw, i, 0) for i in range(3)], [block(prod, i, 0) for i in range(3)], bias_a)
        prob_b, dscore_b = soften(
            [block(raw, i, 1) for i in range(1, 4)], [block(prod, i, 1) for i in range(1, 4)], bias_b
        )
        prob = jnp.concatenate([column(prob_a + [none]), column([none] + prob_b)], 1)
        dscore = jnp.concatenate([column(dscore_a + [none]), column([none] + dscore_b)], 1)
        sums(keys, dscore, up_h, 2 * TOK, 2 * j + (2 * begin if last else 0))
        wide_parts = []
        for n, part in enumerate((dot(dscore, query, 1, 0), dot(prob, grad, 1, 0))):
            wide_parts.append(part[:TOK])
            keep_down[n, :, cols] = part[TOK:2 * TOK].astype(BF16)
            keep_a[n, 0, :, cols] = part[2 * TOK:3 * TOK]
            keep_b[n, 0, :, cols] = part[3 * TOK:]

        up_h = up[1, :, cols]
        shift = dot(adapted[...], up_h, 1, 0)
        query = (column(both(0, 1) + [upper(0)]).astype(F32) + shift).astype(BF16)
        grad = column(both(1, 1) + [upper(1)])
        keys = column([lower(2)] + both(2, 1) + [upper(2)])
        values = column([lower(3)] + both(3, 1) + [upper(3)])
        raw = dot(keys[: 3 * TOK], query[: 2 * TOK], 1, 1)
        prod = dot(values[: 3 * TOK], grad[: 2 * TOK], 1, 1)
        raw_n = dot(keys[TOK:], query[2 * TOK:], 1, 1)
        prod_n = dot(values[TOK:], grad[2 * TOK:], 1, 1)
        prob_a, dscore_a = soften(
            [block(raw, i, 0) for i in range(2)], [block(prod, i, 0) for i in range(2)], bias_a[1:], scale_a
        )
        prob_b, dscore_b = soften([block(raw, i, 1) for i in range(3)], [block(prod, i, 1) for i in range(3)], bias_b)
        prob_n, dscore_n = soften(
            [block(raw_n, i, 0) for i in range(3)], [block(prod_n, i, 0) for i in range(3)], (zero, zero, zero), scale_n
        )
        prob = jnp.concatenate([column(prob_a + [none, none]), column(prob_b + [none]), column([none] + prob_n)], 1)
        dscore = jnp.concatenate(
            [column(dscore_a + [none, none]), column(dscore_b + [none]), column([none] + dscore_n)], 1
        )
        sums(keys, dscore, up_h, 3 * TOK, 2 * j + (2 * (five + begin) if last else 2 * heads))
        for n, part in enumerate((dot(dscore, query, 1, 0), dot(prob, grad, 1, 0))):
            keep_down[2 + n, :, cols] = jnp.where(wide_below, wide_parts[n], part[:TOK]).astype(BF16)
            keep_a[n, 1, :, cols] = part[TOK:2 * TOK]
            keep_b[n, 1, :, cols] = part[2 * TOK:3 * TOK]
            keep_up[n, :, cols] = part[3 * TOK:].astype(BF16)

    for j in range(heads):
        one_pair(j)

    span = pl.ds(begin * HEAD, width)
    stores = [
        pltpu.make_async_copy(x, y, sem_out.at[n])
        for n, (x, y) in enumerate(
            (
                (keep_down, ret_down.at[:, :, span]), (keep_up, ret_up.at[:, :, span]),
                (keep_a, sum_a.at[:, :, :, span]), (keep_b, sum_b.at[:, :, :, span]),
            )
        )
    ]
    for store in stores:
        store.start()
    if last:
        payload[: 2 * begin] = early[: 2 * begin]
        payload[2 * five:2 * (five + begin)] = early[2 * begin:]
        terms = []
        for n, act in enumerate(acts):
            whole = agrad_t[:, n * TOK:(n + 1) * TOK]
            high = whole.astype(BF16)
            low = (whole - high.astype(F32)).astype(BF16)
            terms.append(dot(high, act, 1, 0) + dot(low, act, 1, 0))
        blank = jnp.zeros((RANK, HEAD), F32)
        base = 4 * five
        for s in range(4):
            term = jnp.where(robot_a == s, terms[0], blank) + jnp.where(robot_b == s, terms[1], blank)
            term = term + jnp.where(robot_n == s, terms[2], blank)
            payload[base + 2 * s:base + 2 * s + 2] = term.reshape(2, 32, HEAD).astype(BF16)
        payload[base + 8:] = jnp.zeros((payload.shape[0] - base - 8, 32, HEAD), BF16)
    else:
        agrad_out[...] = agrad_t[...]
    for store in stores:
        store.wait()


def attend(scalars, adapters, near, oth, below, above, up, begin, before=None):
    width = below.shape[1] // 4
    heads = width // HEAD
    quarter = up.shape[1] // 4
    last = before is not None
    chunks = 32 if last else 4 * heads
    inputs = [*scalars, adapters, near, oth, below, above]
    specs = [smem()] * 3 + [vmem()] * 5
    if last:
        inputs += [before[4], before[5]]
        specs += [vmem()] * 2
    inputs.append(fixed(up))
    specs.append(hbm())
    plain = len(inputs)
    aliases = {}
    if last:
        aliases = {plain + n: n for n in range(4)}
        inputs += [fixed(x) for x in before[:4]]
        specs += [hbm()] * 4
    body = functools.partial(attend_kernel, scalars[1].shape[0], begin, heads)

    def kernel(*refs):
        refs = list(refs)
        if last:
            refs.insert(plain + 9, None)
        else:
            refs[8:8] = [None, None]
        body(*refs)

    out_shape = [
        pltpu.HBM((2, 2, TOK, quarter), F32), pltpu.HBM((2, 2, TOK, quarter), F32),
        pltpu.HBM((4, TOK, quarter), BF16), pltpu.HBM((2, TOK, quarter), BF16),
        jax.ShapeDtypeStruct((chunks, 32, HEAD), BF16),
    ]
    out_specs = [hbm()] * 4 + [vmem()]
    if not last:
        out_shape.append(jax.ShapeDtypeStruct((RANK, 3 * TOK), F32))
        out_specs.append(vmem())
    return pl.pallas_call(
        kernel,
        in_specs=specs,
        out_specs=out_specs,
        out_shape=out_shape,
        input_output_aliases=aliases,
        scratch_shapes=[
            pltpu.VMEM((2, RANK, width), BF16),
            pltpu.VMEM((2, 2, TOK, width), F32),
            pltpu.VMEM((2, 2, TOK, width), F32),
            pltpu.VMEM((4, TOK, width), BF16),
            pltpu.VMEM((2, TOK, width), BF16),
            pltpu.VMEM((3 * TOK, RANK), BF16),
            pltpu.VMEM((RANK, 3 * TOK), BF16),
            pltpu.VMEM((RANK, 3 * TOK), F32),
            pltpu.SemaphoreType.DMA((2,)),
            pltpu.SemaphoreType.DMA((4,)),
        ],
        compiler_params=pltpu.CompilerParams(vmem_limit_bytes=24 * MIB),
        cost_estimate=pl.CostEstimate(
            flops=2 * heads * 12 * 512 * 256 * 128, bytes_accessed=heads * 2 * MIB, transcendentals=heads * 1024 * 256
        ),
        name="attend_last" if last else "attend_first",
    )(*inputs)


def finish_kernel(heads, place, gathered, swapped, up_grad, adapter_grad):
    per_core = heads // 2
    for n, part in enumerate((gathered, swapped)):
        side = place[0] if n == 0 else 1 - place[0]
        for h in range(per_core):
            cols = pl.ds(pl.multiple_of((side * per_core + h) * HEAD, HEAD), HEAD)
            up_grad[:32, cols] = part[2 * h].astype(F32)
            up_grad[32:, cols] = part[2 * h + 1].astype(F32)
    for s in range(4):
        for n in range(2):
            at = 2 * per_core + 2 * s + n
            adapter_grad[s, n * 32:(n + 1) * 32] = gathered[at].astype(F32) + swapped[at].astype(F32)


def finish(place, gathered, swapped, heads):
    return pl.pallas_call(
        functools.partial(finish_kernel, heads),
        in_specs=[smem(), vmem(), vmem()],
        out_specs=[vmem(), vmem()],
        out_shape=[
            jax.ShapeDtypeStruct((RANK, heads * HEAD), F32),
            jax.ShapeDtypeStruct((4, RANK, HEAD), F32),
        ],
        compiler_params=pltpu.CompilerParams(vmem_limit_bytes=4 * MIB),
        name="finish",
    )(place, gathered, swapped)


def local(
    query_tokens, key_tokens, value_tokens, out_grad, actions, clip_lengths, clip_robots, adapters, up_proj,
):
    q, k, v, g = (t[0, 0] for t in (query_tokens, key_tokens, value_tokens, out_grad))
    act = actions[0, 0]
    width = q.shape[1]
    half = width // 2
    quarter = half // 2
    core = lax.axis_index("core")
    nz = lax.axis_size("z")
    chips = lax.axis_size("x") * nz
    chip = lax.axis_index("x") * nz + lax.axis_index("z")
    column = ("x", "z")
    swap = [(0, 1), (1, 0)]
    upward = [(c, c + 1) for c in range(chips - 1)]
    downward = [(c + 1, c) for c in range(chips - 1)]
    place = jnp.stack([core, chip]).astype(jnp.int32)
    lengths = clip_lengths[0, 0]
    scalars = (place, lengths, clip_robots[0, 0])
    own = (q, g, k, v)
    oth = lax.ppermute(take_half(place, own, act, True), "core", swap)
    near = take_half(place, own, act, False)
    five = quarter // HEAD
    table = jnp.swapaxes(adapters[0], 1, 2)
    moved = []
    for begin, heads in ((0, SPLIT), (SPLIT, five - SPLIT)):
        up_msg, down_msg = pack(scalars, near, oth, begin, heads)
        moved.append((lax.ppermute(up_msg, column, upward), lax.ppermute(down_msg, column, downward)))
    before = attend(scalars, table, near, oth, *moved[0], up_proj, 0)
    sum_a, sum_b, ret_down, ret_up, payload = attend(
        scalars, table, near, oth, *moved[1], up_proj, SPLIT, before
    )

    pieces = lax.all_to_all(payload, GROUP, 0, 0, tiled=True)
    chunk = jnp.sum(pieces.astype(F32), 0)
    index = (lax.axis_index("dp") * lax.axis_size("x") + lax.axis_index("x")) * nz + lax.axis_index("z")
    is_up = index < 2 * (half // HEAD)
    ny = lax.axis_size("y")
    shared = lax.all_to_all(jnp.broadcast_to(chunk.astype(BF16)[None], (ny, 32, HEAD)), "y", 0, 0, tiled=True)
    keep = jnp.logical_or(is_up, jnp.arange(ny, dtype=jnp.int32) == lax.axis_index("y"))
    total = jnp.sum(jnp.where(keep[:, None, None], shared.astype(F32), 0.0), 0)
    gathered = lax.all_to_all(jnp.broadcast_to(total.astype(BF16)[None], (32, 32, HEAD)), GROUP, 0, 0, tiled=True)
    swapped = lax.ppermute(gathered, "core", swap)
    up_total, adapter_total = finish(place, gathered, swapped, width // HEAD)
    adapter_total = jnp.swapaxes(adapter_total, 1, 2)

    ends = jnp.cumsum(lengths)
    after = 2 * chip + 2
    wide_above = jnp.sum(jnp.where((ends - lengths <= after) & (after < ends), ends - lengths, 0)) == 2 * chip
    wide_above = jnp.logical_and(wide_above, after < ends[-1])
    from_above = lax.ppermute(ret_down, column, downward).astype(F32)
    from_below = lax.ppermute(ret_up, column, upward).astype(F32)
    second = from_above[2:]
    a1 = sum_a[:, 0] + jnp.where(wide_above, second, 0.0)
    a2 = sum_a[:, 1] + from_below
    b1 = sum_b[:, 0] + from_above[:2]
    b2 = sum_b[:, 1] + jnp.where(wide_above, 0.0, second)
    first = core == 0
    mine = [jnp.where(first, x, y).astype(BF16) for x, y in ((a1, b1), (a2, b2))]
    theirs = jnp.stack([jnp.where(first, y, x).astype(BF16) for x, y in ((a1, b1), (a2, b2))])
    other = lax.ppermute(theirs, "core", swap)
    out = jnp.concatenate(
        [jnp.where(first, mine[0], other[0]), jnp.where(first, mine[1], other[1])]
        + [jnp.where(first, other[0], mine[0]), jnp.where(first, other[1], mine[1])],
        2,
    )
    return out[0][None, None], out[1][None, None], adapter_total[None], up_total


def solution(mesh):
    sizes = dict(mesh.shape)
    wide = Mesh(
        mesh.devices.reshape(sizes["dp"], 2, sizes["context"] // 4, 2, sizes["embodime"]),
        ("dp", "x", "z", "core", "y"),
    )
    frames = P("dp", "y", ("x", "z", "core"), None)
    rows = P("dp", "y", None)
    return jax.shard_map(
        local,
        mesh=wide,
        in_specs=(frames,) * 5 + (rows, rows, P("y", None, None, None), P()),
        out_specs=(frames, frames, P("y", None, None, None), P()),
        check_vma=False,
    )
```

time: 120 us -> 119 us (level)
  waiting for transfers between devices: 30.8 us -> 11.4 us
  blocking collectives: 0 us -> 16.5 us
  local copies, waits for them, and re-layouts: 8.15 us -> 2.44 us
  Pallas kernels: 17.8 us -> 23 us
  other arithmetic: 4.94 us -> 6.99 us
  between operations: 0.92 us -> 2.24 us
    all_to_all x0 -> x1, blocking collectives: none -> 16.5 us  [local(): lax.all_to_all(jnp.broadcast_to(total.astype(BF16)[None], (32, 32, HEAD))...]
    ppermute x8, waiting for transfers between devices: 14.7 us -> 2.63 us  [the longest x2 1.8 us: local(): lax.ppermute(up_msg, column, upward)]
    all_to_all x1, waiting for transfers between devices: 7.22 us -> 0.01 us  [local(): lax.all_to_all(jnp.broadcast_to(chunk.astype(BF16)[None], (ny, 32, HEAD))...]
    all_to_all x1 -> x0, starting transfers between devices: 6.21 us -> none  [local(): lax.all_to_all(jnp.broadcast_to(total.astype(BF16)[None], (32, 32, HEAD))...]
    unnamed x22 -> x10, local copies, waits for them, and re-layouts: 5.15 us -> 0.03 us
    pallas_call x1 -> x5, Pallas kernels: 1.47 us -> 6.57 us  [the longest x2 3.72 us: take_half(): pl.pallas_call(functools.partial(take_kernel, far), in_specs=[smem()] + [...]
    ppermute x8, starting transfers between devices: 25.8 us -> 30.6 us  [the longest x1 8.79 us: local(): oth = lax.ppermute(take_half(place, own, act, True), 'core', swap)]
    all_to_all x1 -> x0, waiting for transfers between devices: 3.12 us -> none  [local(): lax.all_to_all(jnp.broadcast_to(total.astype(BF16)[None], (32, 32, HEAD))...]
  transfers between devices with their start and end apart: 12 -> 11, of which waited for: 5 -> 3; matrix products, arithmetic and copies ran while one was open for 6% -> 8% of each run, Pallas kernels for 9% -> 10%
where the time goes in v3:
time: 119 us
  starting transfers between devices  56 us (47%)
  Pallas kernels  23 us (19%)
  blocking collectives  16.5 us (14%)
  waiting for transfers between devices  11.4 us (10%)
  other arithmetic  6.99 us (6%)
  local copies, waits for them, and re-layouts  2.44 us (2%)
  between operations  2.24 us (2%)
    all_to_all x1, blocking collectives, local(): lax.all_to_all(jnp.broadcast_to(total.astype(BF16)[None], (32, 32, HEAD))...  16.5 us
    pallas_call x2, Pallas kernels, attend(): pl.pallas_call(kernel, in_specs=specs, out_specs=out_specs, out_shape=out...  16.4 us
    all_to_all x1, starting transfers between devices, local(): pieces = lax.all_to_all(payload, GROUP, 0, 0, tiled=True)  12.4 us
    ppermute x1, starting transfers between devices, local(): oth = lax.ppermute(take_half(place, own, act, True), 'core', swap)  8.79 us
    all_to_all x1, waiting for transfers between devices, local(): pieces = lax.all_to_all(payload, GROUP, 0, 0, tiled=True)  8.72 us
    ppermute x2, starting transfers between devices, local(): lax.ppermute(up_msg, column, upward)  8.14 us
    all_to_all x1, starting transfers between devices, local(): lax.all_to_all(jnp.broadcast_to(chunk.astype(BF16)[None], (ny, 32, HEAD))...  6.82 us
    ppermute x1, starting transfers between devices, local(): other = lax.ppermute(theirs, 'core', swap)  6.55 us
  transfers between devices with their start and end apart: 11, of which 3 were waited for; matrix products, arithmetic and copies ran while one was open for 8% of the time, Pallas kernels for 10%

profile of v3, /device:TPU:1, one launch (start us, length us, event | category | flops | bytes accessed | tf_op | source)
XLA Modules:
  0.0 118.5 jit_solution(1786507872550513604)
XLA Ops:
  0.7 1.9 %take_far.1 = bf16[128,5248]{1,0:T(8,128)(2,1)S(1)} custom-call(s32[2]{0:T(128)S(1)} %pad_add_fusion.place.refs_0_, bf16[128,2560]{1,0:T(8,128)(2,1)} %bitcast.87, bf16[128,2560]{1,0:T(8,128)(2,1)} %bitcast.89, bf16[128,2560]{1,0:T(8,128)(2,1)} %bitcast.91, bf16[128,2560]{1,0:T(8,128)(2,1)} %bitcast.93, bf16[128,128]{1,0:T(8,128)(2,1)} %bitcast.95), custom_call_target="tpu_custom_call" | custom-call | bytes 4194304 | tf_op jit(solution)/shard_map/take_far/pallas_call | solution.py:75
  2.6 8.8 %collective-permute-start = (bf16[128,5248]{1,0:T(8,128)(2,1)S(1)}, bf16[128,5248]{1,0:T(8,128)(2,1)S(1)}, u32[]{:S(2)}, u32[]{:S(2)}) collective-permute-start(bf16[128,5248]{1,0:T(8,128)(2,1)S(1)} %take_far.1), channel_id=1, source_target_pairs={{0,8},{8,0},{1,9},{9,1},{2,10},{10,2},{3,11},{11,3},{4,12},{12,4},... | collective-permute-start | bytes 4030472 | tf_op jit(solution)/shard_map/ppermute | solution.py:427
  11.4 1.9 %take_near.1.near.refs_4_ = bf16[128,5248]{1,0:T(8,128)(2,1)S(1)} custom-call(s32[2]{0:T(128)S(1)} %pad_add_fusion.place.refs_0_, bf16[128,2560]{1,0:T(8,128)(2,1)} %bitcast.88, bf16[128,2560]{1,0:T(8,128)(2,1)} %bitcast.90, bf16[128,2560]{1,0:T(8,128)(2,1)} %bitcast.92, bf16[128,2560]{1,0:T(8,128)(2,1)} %bitcast.94, bf16[128,128]{1,0:T(8,128)(2,1)} %bitcast.96), custom_call_target="tpu_custom_call" | custom-call | bytes 4194304 | tf_op jit(solution)/shard_map/take_near/pallas_call | solution.py:75
  14.8 1.3 %collective-permute-start.4 = (bf16[128,1664]{1,0:T(8,128)(2,1)S(1)}, bf16[128,1664]{1,0:T(8,128)(2,1)S(1)}, u32[]{:S(2)}, u32[]{:S(2)}) collective-permute-start(bf16[128,1664]{1,0:T(8,128)(2,1)S(1)} %get-tuple-element.24), channel_id=1, source_target_pairs={{16,0},{32,16},{48,32},{64,48},{80,64},{96,80},{112,96},{128,112},... | collective-permute-start | bytes 1277960 | tf_op jit(solution)/shard_map/ppermute | solution.py:434
  16.1 4.1 %collective-permute-start.3 = (bf16[128,1536]{1,0:T(8,128)(2,1)S(1)}, bf16[128,1536]{1,0:T(8,128)(2,1)S(1)}, u32[]{:S(2)}, u32[]{:S(2)}) collective-permute-start(bf16[128,1536]{1,0:T(8,128)(2,1)S(1)} %get-tuple-element.23), channel_id=1, source_target_pairs={{0,16},{16,32},{32,48},{48,64},{64,80},{80,96},{96,112},{112,128},... | collective-permute-start | bytes 1179656 | tf_op jit(solution)/shard_map/ppermute | solution.py:434
  21.0 1.3 %collective-permute-start.2 = (bf16[128,1152]{1,0:T(8,128)(2,1)S(1)}, bf16[128,1152]{1,0:T(8,128)(2,1)S(1)}, u32[]{:S(2)}, u32[]{:S(2)}) collective-permute-start(bf16[128,1152]{1,0:T(8,128)(2,1)S(1)} %get-tuple-element.22), channel_id=1, source_target_pairs={{16,0},{32,16},{48,32},{64,48},{80,64},{96,80},{112,96},{128,112},... | collective-permute-start | bytes 884744 | tf_op jit(solution)/shard_map/ppermute | solution.py:434
  22.3 4.0 %collective-permute-start.1 = (bf16[128,1024]{1,0:T(8,128)(2,1)S(1)}, bf16[128,1024]{1,0:T(8,128)(2,1)S(1)}, u32[]{:S(2)}, u32[]{:S(2)}) collective-permute-start(bf16[128,1024]{1,0:T(8,128)(2,1)S(1)} %get-tuple-element.21), channel_id=1, source_target_pairs={{0,16},{16,32},{32,48},{48,64},{64,80},{80,96},{96,112},{112,128},... | collective-permute-start | bytes 786440 | tf_op jit(solution)/shard_map/ppermute | solution.py:434
  26.3 1.8 %collective-permute-done.3.refs_6_ = bf16[128,1536]{1,0:T(8,128)(2,1)S(1)} collective-permute-done((bf16[128,1536]{1,0:T(8,128)(2,1)S(1)}, bf16[128,1536]{1,0:T(8,128)(2,1)S(1)}, u32[]{:S(2)}, u32[]{:S(2)}) %collective-permute-start.3) | collective-permute-done | bytes 393248 | tf_op jit(solution)/shard_map/ppermute | solution.py:434
  28.1 9.0 %attend_first.1 = (f32[2,2,128,640]{3,2,1,0:T(8,128)}, f32[2,2,128,640]{3,2,1,0:T(8,128)}, bf16[4,128,640]{2,1,0:T(8,128)(2,1)}, bf16[2,128,640]{2,1,0:T(8,128)(...) custom-call(s32[2]{0:T(128)S(1)} %pad_add_fusion.place.refs_0_, s32[16]{0:T(128)S(1)} %bitcast.80, ...), custom_call_target="tpu_custom_call" | custom-call | flops 1207959552 | bytes 6291456 | tf_op jit(solution)/shard_map/attend_first/pallas_call | solution.py:353
  37.1 7.4 %attend_last.1 = (f32[2,2,128,640]{3,2,1,0:T(8,128)}, f32[2,2,128,640]{3,2,1,0:T(8,128)}, bf16[4,128,640]{2,1,0:T(8,128)(2,1)}, bf16[2,128,640]{2,1,0:T(8,128)(2,1)}, bf16[32,32,128]{2,1,0:T(8,128)(2,1)}) custom-call(s32[2]{0:T(128)S(1)} %pad_add_fusion.place.refs_0_, ...), custom_call_target="tpu_custom_call", output_to_operand_aliasing={{0}: (11, {}), {1}: (12, {}), {2}: (13, {}), {3}: (14, {})} | custom-call | flops 805306368 | bytes 4194304 | tf_op jit(solution)/shard_map/attend_last/pallas_call | solution.py:353
  44.5 1.3 %collective-permute-start.5 = (bf16[4,128,640]{2,1,0:T(8,128)(2,1)}, bf16[4,128,640]{2,1,0:T(8,128)(2,1)}, u32[]{:S(2)}, u32[]{:S(2)}) collective-permute-start(bf16[4,128,640]{2,1,0:T(8,128)(2,1)} %get-tuple-element.32), channel_id=1, source_target_pairs={{16,0},{32,16},{48,32},{64,48},{80,64},{96,80},{112,96},{128,112},... | collective-permute-start | bytes 1966088 | tf_op jit(solution)/shard_map/ppermute | solution.py:457
  45.8 12.4 %all-to-all-start = ((bf16[32,32,128]{2,1,0:T(8,128)(2,1)}), bf16[32,32,128]{2,1,0:T(8,128)(2,1)S(1)}, u32[]{:S(2)}, u32[]{:S(2)}) async-start(bf16[32,32,128]{2,1,0:T(8,128)(2,1)} %get-tuple-element.35), calls=%async_computation | async-start | bytes 524288 | tf_op jit(solution)/shard_map/all_to_all | solution.py:440
  58.3 3.3 %collective-permute-start.6 = (bf16[2,128,640]{2,1,0:T(8,128)(2,1)}, bf16[2,128,640]{2,1,0:T(8,128)(2,1)S(1)}, u32[]{:S(2)}, u32[]{:S(2)}) collective-permute-start(bf16[2,128,640]{2,1,0:T(8,128)(2,1)} %get-tuple-element.34), channel_id=1, source_target_pairs={{0,16},{16,32},{32,48},{48,64},{64,80},{80,96},{96,112},{112,128},... | collective-permute-start | bytes 983048 | tf_op jit(solution)/shard_map/ppermute | solution.py:458
  64.3 8.7 %all-to-all-done = bf16[32,32,128]{2,1,0:T(8,128)(2,1)S(1)} async-done(((bf16[32,32,128]{2,1,0:T(8,128)(2,1)}), bf16[32,32,128]{2,1,0:T(8,128)(2,1)S(1)}, u32[]{:S(2)}, u32[]{:S(2)}) %all-to-all-start) | async-done | bytes 262176 | tf_op jit(solution)/shard_map/all_to_all | solution.py:440
  73.7 6.8 %all-to-all-start.1 = ((bf16[8,32,128]{2,1,0:T(8,128)(2,1)}), bf16[8,32,128]{2,1,0:T(8,128)(2,1)S(1)}, u32[]{:S(2)}, u32[]{:S(2)}) async-start(bf16[8,32,128]{2,1,0:T(8,128)(2,1)} %broadcast_in_dim.41), calls=%async_computation.1 | async-start | bytes 131072 | tf_op jit(solution)/shard_map/all_to_all | solution.py:445
  80.5 1.2 convert_element_type.30
  81.7 1.8 %fusion.3 = (bf16[1,2,128,640]{3,2,1,0:T(8,128)(2,1)S(1)}, bf16[1,2,128,640]{3,2,1,0:T(8,128)(2,1)S(1)}) fusion(pred[]{:T(512)S(6)} %eq.16, f32[4,128,640]{2,1,0:T(8,128)S(1)} %convert_element_type.30, pred[]{:T(512)S(6)} %and.12, bf16[2,128,640]{2,1,0:T(8,128)(2,1)S(1)} %collective-permute-done.6, f32[2,2,128,640]{3,2,1,0:T(8,128)S(1)} %copy-done.3, ...), kind=kLoop, calls=%fused_computation.16 | loop fusion | flops 1802240 | bytes 4915202 | tf_op jit(solution)/shard_map/stack | solution.py:466
  83.5 0.9 pad_maximum_fusion.1
  84.4 6.5 %collective-permute-start.7 = (bf16[2,2,128,640]{3,2,1,0:T(8,128)(2,1)}, bf16[2,2,128,640]{3,2,1,0:T(8,128)(2,1)S(1)}, u32[]{:S(2)}, u32[]{:S(2)}) collective-permute-start(bf16[2,2,128,640]{3,2,1,0:T(8,128)(2,1)} %pad_maximum_fusion.1), channel_id=1, source_target_pairs={{0,8},{8,0},{1,9},{9,1},{2,10},{10,2},{3,11},{11,3},{4,12},{12,4},... | collective-permute-start | bytes 1966088 | tf_op jit(solution)/shard_map/ppermute | solution.py:467
  91.1 16.5 %all_to_all.15.gathered = bf16[32,32,128]{2,1,0:T(8,128)(2,1)S(1)} all-to-all(bf16[32,32,128]{2,1,0:T(8,128)(2,1)S(1)} %broadcast_in_dim.43), channel_id=1, replica_groups=mesh['dp'=2,'x'=2,'z'=8,'core'=2,'y'=8] {'dp','x','z'}, dimensions={0} | all-to-all | bytes 524288 | tf_op jit(solution)/shard_map/all_to_all | solution.py:448
  107.6 6.1 %collective-permute-start.8 = (bf16[32,32,128]{2,1,0:T(8,128)(2,1)S(1)}, bf16[32,32,128]{2,1,0:T(8,128)(2,1)S(1)}, u32[]{:S(2)}, u32[]{:S(2)}) collective-permute-start(bf16[32,32,128]{2,1,0:T(8,128)(2,1)S(1)} %all_to_all.15.gathered), channel_id=1, source_target_pairs={{0,8},{8,0},{1,9},{9,1},{2,10},{10,2},{3,11},{11,3},{4,12},{12,4},... | collective-permute-start | bytes 786440 | tf_op jit(solution)/shard_map/ppermute | solution.py:449
  113.8 1.9 %broadcast_select_fusion.3 = (bf16[2,128,640]{2,1,0:T(8,128)(2,1)S(1)}, bf16[2,128,640]{2,1,0:T(8,128)(2,1)S(1)}, bf16[2,128,640]{2,1,0:T(8,128)(2,1)S(1)}, bf16[2,128,640]{2,1,0:T(8,128)(2,1)S(1)}) fusion(pred[]{:T(512)S(6)} %eq.16, bf16[2,2,128,640]{3,2,1,0:T(8,128)(2,1)S(1)} %collective-permute-done.7, f32[4,128,640]{2,1,0:T(8,128)S(1)} %convert_element_type.30, ...), kind=kLoop, calls=%fused_computation.23 | loop fusion | flops 2129920 | bytes 6225922 | tf_op jit(solution)/shard_map/jit(_where)/select_n | solution.py:469
  115.9 1.1 slice_bitcast_fusion
  117.0 1.5 %finish.1 = (f32[64,2560]{1,0:T(8,128)}, f32[4,64,128]{2,1,0:T(8,128)}) custom-call(s32[2]{0:T(128)S(1)} %pad_add_fusion.place.refs_0_, bf16[32,32,128]{2,1,0:T(8,128)(2,1)S(1)} %all_to_all.15.gathered, bf16[32,32,128]{2,1,0:T(8,128)(2,1)S(1)} %collective-permute-done.8.swapped), custom_call_target="tpu_custom_call" | custom-call | tf_op jit(solution)/shard_map/finish/pallas_call | solution.py:394
  (34 shorter events, 4.7 us)
Async XLA Ops:
  2.6 11.5 %copy-start.1 = (s32[1,1,16]{2,1,0:T(1,128)S(1)}, s32[1,1,16]{2,1,0:T(1,128)}, u32[]{:S(2)}) copy-start(s32[1,1,16]{2,1,0:T(1,128)} %param.14) | copy-start | bytes 196
  2.6 11.5 %copy-start.2 = (s32[1,1,16]{2,1,0:T(1,128)S(1)}, s32[1,1,16]{2,1,0:T(1,128)}, u32[]{:S(2)}) copy-start(s32[1,1,16]{2,1,0:T(1,128)} %param.15) | copy-start | bytes 196
  2.6 11.5 %collective-permute-start = (bf16[128,5248]{1,0:T(8,128)(2,1)S(1)}, bf16[128,5248]{1,0:T(8,128)(2,1)S(1)}, u32[]{:S(2)}, u32[]{:S(2)}) collective-permute-start(bf16[128,5248]{1,0:T(8,128)(2,1)S(1)} %take_far.1), channel_id=1, source_target_pairs={{0,8},{8,0},{1,9},{9,1},{2,10},{10,2},{3,11},{11,3},{4,12},{12,4},... | collective-permute-start | bytes 4030472 | tf_op jit(solution)/shard_map/ppermute | solution.py:427
  14.8 13.2 %collective-permute-start.4 = (bf16[128,1664]{1,0:T(8,128)(2,1)S(1)}, bf16[128,1664]{1,0:T(8,128)(2,1)S(1)}, u32[]{:S(2)}, u32[]{:S(2)}) collective-permute-start(bf16[128,1664]{1,0:T(8,128)(2,1)S(1)} %get-tuple-element.24), channel_id=1, source_target_pairs={{16,0},{32,16},{48,32},{64,48},{80,64},{96,80},{112,96},{128,112},... | collective-permute-start | bytes 1277960 | tf_op jit(solution)/shard_map/ppermute | solution.py:434
  16.1 11.9 %copy-start = (bf16[1,4,128,64]{2,3,1,0:T(8,128)(2,1)S(1)}, bf16[1,4,128,64]{2,3,1,0:T(8,128)(2,1)}, u32[]{:S(2)}) copy-start(bf16[1,4,128,64]{2,3,1,0:T(8,128)(2,1)} %param.16) | copy-start | bytes 196612
  16.1 11.9 %collective-permute-start.3 = (bf16[128,1536]{1,0:T(8,128)(2,1)S(1)}, bf16[128,1536]{1,0:T(8,128)(2,1)S(1)}, u32[]{:S(2)}, u32[]{:S(2)}) collective-permute-start(bf16[128,1536]{1,0:T(8,128)(2,1)S(1)} %get-tuple-element.23), channel_id=1, source_target_pairs={{0,16},{16,32},{32,48},{48,64},{64,80},{80,96},{96,112},{112,128},... | collective-permute-start | bytes 1179656 | tf_op jit(solution)/shard_map/ppermute | solution.py:434
  21.0 16.2 %collective-permute-start.2 = (bf16[128,1152]{1,0:T(8,128)(2,1)S(1)}, bf16[128,1152]{1,0:T(8,128)(2,1)S(1)}, u32[]{:S(2)}, u32[]{:S(2)}) collective-permute-start(bf16[128,1152]{1,0:T(8,128)(2,1)S(1)} %get-tuple-element.22), channel_id=1, source_target_pairs={{16,0},{32,16},{48,32},{64,48},{80,64},{96,80},{112,96},{128,112},... | collective-permute-start | bytes 884744 | tf_op jit(solution)/shard_map/ppermute | solution.py:434
  22.3 14.9 %collective-permute-start.1 = (bf16[128,1024]{1,0:T(8,128)(2,1)S(1)}, bf16[128,1024]{1,0:T(8,128)(2,1)S(1)}, u32[]{:S(2)}, u32[]{:S(2)}) collective-permute-start(bf16[128,1024]{1,0:T(8,128)(2,1)S(1)} %get-tuple-element.21), channel_id=1, source_target_pairs={{0,16},{16,32},{32,48},{48,64},{64,80},{80,96},{96,112},{112,128},... | collective-permute-start | bytes 786440 | tf_op jit(solution)/shard_map/ppermute | solution.py:434
  44.5 36.0 %collective-permute-start.5 = (bf16[4,128,640]{2,1,0:T(8,128)(2,1)}, bf16[4,128,640]{2,1,0:T(8,128)(2,1)}, u32[]{:S(2)}, u32[]{:S(2)}) collective-permute-start(bf16[4,128,640]{2,1,0:T(8,128)(2,1)} %get-tuple-element.32), channel_id=1, source_target_pairs={{16,0},{32,16},{48,32},{64,48},{80,64},{96,80},{112,96},{128,112},... | collective-permute-start | bytes 1966088 | tf_op jit(solution)/shard_map/ppermute | solution.py:457
  45.8 27.2 %all-to-all-start = ((bf16[32,32,128]{2,1,0:T(8,128)(2,1)}), bf16[32,32,128]{2,1,0:T(8,128)(2,1)S(1)}, u32[]{:S(2)}, u32[]{:S(2)}) async-start(bf16[32,32,128]{2,1,0:T(8,128)(2,1)} %get-tuple-element.35), calls=%async_computation | async-start | bytes 524288 | tf_op jit(solution)/shard_map/all_to_all | solution.py:440
  58.2 23.5 %copy-start.3 = (f32[2,2,128,640]{3,2,1,0:T(8,128)S(1)}, f32[2,2,128,640]{3,2,1,0:T(8,128)}, u32[]{:S(2)}) copy-start(f32[2,2,128,640]{3,2,1,0:T(8,128)} %get-tuple-element.31) | copy-start | bytes 3932164
  58.3 23.4 %collective-permute-start.6 = (bf16[2,128,640]{2,1,0:T(8,128)(2,1)}, bf16[2,128,640]{2,1,0:T(8,128)(2,1)S(1)}, u32[]{:S(2)}, u32[]{:S(2)}) collective-permute-start(bf16[2,128,640]{2,1,0:T(8,128)(2,1)} %get-tuple-element.34), channel_id=1, source_target_pairs={{0,16},{16,32},{32,48},{48,64},{64,80},{80,96},{96,112},{112,128},... | collective-permute-start | bytes 983048 | tf_op jit(solution)/shard_map/ppermute | solution.py:458
  73.7 17.3 %all-to-all-start.1 = ((bf16[8,32,128]{2,1,0:T(8,128)(2,1)}), bf16[8,32,128]{2,1,0:T(8,128)(2,1)S(1)}, u32[]{:S(2)}, u32[]{:S(2)}) async-start(bf16[8,32,128]{2,1,0:T(8,128)(2,1)} %broadcast_in_dim.41), calls=%async_computation.1 | async-start | bytes 131072 | tf_op jit(solution)/shard_map/all_to_all | solution.py:445
  81.7 1.8 %copy-start.4 = (bf16[2,128,640]{2,1,0:T(8,128)(2,1)}, bf16[2,128,640]{2,1,0:T(8,128)(2,1)S(1)}, u32[]{:S(2)}) copy-start(bf16[2,128,640]{2,1,0:T(8,128)(2,1)S(1)} %collective-permute-done.6) | copy-start | bytes 983044
  84.4 29.3 %collective-permute-start.7 = (bf16[2,2,128,640]{3,2,1,0:T(8,128)(2,1)}, bf16[2,2,128,640]{3,2,1,0:T(8,128)(2,1)S(1)}, u32[]{:S(2)}, u32[]{:S(2)}) collective-permute-start(bf16[2,2,128,640]{3,2,1,0:T(8,128)(2,1)} %pad_maximum_fusion.1), channel_id=1, source_target_pairs={{0,8},{8,0},{1,9},{9,1},{2,10},{10,2},{3,11},{11,3},{4,12},{12,4},... | collective-permute-start | bytes 1966088 | tf_op jit(solution)/shard_map/ppermute | solution.py:467
  107.6 9.4 %collective-permute-start.8 = (bf16[32,32,128]{2,1,0:T(8,128)(2,1)S(1)}, bf16[32,32,128]{2,1,0:T(8,128)(2,1)S(1)}, u32[]{:S(2)}, u32[]{:S(2)}) collective-permute-start(bf16[32,32,128]{2,1,0:T(8,128)(2,1)S(1)} %all_to_all.15.gathered), channel_id=1, source_target_pairs={{0,8},{8,0},{1,9},{9,1},{2,10},{10,2},{3,11},{11,3},{4,12},{12,4},... | collective-permute-start | bytes 786440 | tf_op jit(solution)/shard_map/ppermute | solution.py:449

commit v4 on v0

v4 whole, which is shorter than its diff:
```python
import functools
import math

import jax
import jax.numpy as jnp
from jax import lax
from jax.experimental import pallas as pl
from jax.experimental.pallas import tpu as pltpu
from jax.sharding import Mesh, PartitionSpec as P

HEAD = 128
TOK = 128
RANK = 64
LOW = -1e30
SCALE = HEAD**-0.5
SCALE2 = SCALE * math.log2(math.e)
F32 = jnp.float32
BF16 = jnp.bfloat16
ROWS = 16
MIB = 1024 * 1024


def dot(a, b, ca, cb):
    return lax.dot_general(a, b, (((ca,), (cb,)), ((), ())), preferred_element_type=F32)


def clip_of(frame, lengths, robots, clips):
    begin = jnp.int32(0)
    start = jnp.int32(0)
    robot = jnp.int32(0)
    for i in range(clips):
        size = lengths[i]
        inside = jnp.logical_and(frame >= begin, frame < begin + size)
        start = jnp.where(inside, begin, start)
        robot = jnp.where(inside, robots[i], robot)
        begin = begin + size
    return start, robot


def smem():
    return pl.BlockSpec(memory_space=pltpu.SMEM)


def vmem():
    return pl.BlockSpec(memory_space=pltpu.VMEM)


def hbm():
    return pl.BlockSpec(memory_space=pl.ANY)


def fixed(x):
    return pltpu.with_memory_space_constraint(x, pltpu.HBM)


def take_kernel(far, place, q, g, k, v, act, out, sems):
    half = q.shape[1] // 2
    side = 1 - place[0] if far else place[0]
    copies = [
        pltpu.make_async_copy(
            x.at[:, pl.ds(pl.multiple_of(side * half, HEAD), half)], out.at[:, pl.ds(n * half, half)], sems.at[n]
        )
        for n, x in enumerate((q, g, k, v))
    ]
    copies.append(pltpu.make_async_copy(act, out.at[:, pl.ds(4 * half, HEAD)], sems.at[4]))
    for copy in copies:
        copy.start()
    for copy in copies:
        copy.wait()


def take_half(place, own, act, far):
    half = own[0].shape[1] // 2
    return pl.pallas_call(
        functools.partial(take_kernel, far),
        in_specs=[smem()] + [hbm()] * 5,
        out_specs=vmem(),
        out_shape=pltpu.VMEM((TOK, 4 * half + HEAD), BF16),
        scratch_shapes=[pltpu.SemaphoreType.DMA((5,))],
        compiler_params=pltpu.CompilerParams(vmem_limit_bytes=8 * MIB),
        cost_estimate=pl.CostEstimate(flops=0, bytes_accessed=4 * MIB, transcendentals=0),
        name="take_far" if far else "take_near",
    )(place, *(fixed(x) for x in own), fixed(act))


def pack_kernel(clips, place, lengths, robots, near, oth, up, down):
    half = near.shape[1] // 4 // HEAD * HEAD
    quarter = half // 2
    first = place[0] == 0
    frame_a = 2 * place[1]
    start_n, _ = clip_of(frame_a + 2, lengths, robots, clips)
    wide = start_n == frame_a

    def frame(is_a, array, group):
        at = array * half + group * quarter
        one, two = near[:, at:at + quarter], oth[:, at:at + quarter]
        return jnp.where(first, one, two) if is_a else jnp.where(first, two, one)

    for n, array in enumerate((2, 3)):
        up[:, n * quarter:(n + 1) * quarter] = frame(False, array, 0)
        up[:, (2 + n) * quarter:(3 + n) * quarter] = jnp.where(wide, frame(True, array, 0), frame(False, array, 1))
    for n in range(4):
        down[:, n * quarter:(n + 1) * quarter] = frame(True, n, 1)
    one, two = near[:, 4 * half:], oth[:, 4 * half:]
    down[:, 4 * quarter:] = jnp.where(first, one, two)


def pack(scalars, near, oth):
    quarter = near.shape[1] // 4 // HEAD * HEAD // 2
    return pl.pallas_call(
        functools.partial(pack_kernel, scalars[1].shape[0]),
        in_specs=[smem()] * 3 + [vmem()] * 2,
        out_specs=[vmem()] * 2,
        out_shape=[pltpu.VMEM((TOK, 4 * quarter), BF16), pltpu.VMEM((TOK, 4 * quarter + HEAD), BF16)],
        compiler_params=pltpu.CompilerParams(vmem_limit_bytes=8 * MIB),
        cost_estimate=pl.CostEstimate(flops=0, bytes_accessed=4 * MIB, transcendentals=0),
        name="pack",
    )(*scalars, near, oth)


class Views:
    def __init__(self, place, near, oth, below, above):
        self.first = place[0] == 0
        self.near, self.oth, self.below, self.above = near, oth, below, above
        self.half = near.shape[1] // 4 // HEAD * HEAD
        self.quarter = self.half // 2

    def pick(self, one, two):
        return jnp.where(self.first, one, two)

    def pair(self, one, two):
        return [self.pick(one, two), self.pick(two, one)]

    def both(self, n, group, j):
        at = n * self.half + group * self.quarter + j * HEAD
        return self.pair(self.near[:, at:at + HEAD], self.oth[:, at:at + HEAD])

    def lower(self, n, j):
        at = n * self.quarter + j * HEAD
        return self.below[:, at:at + HEAD]

    def upper(self, n, j):
        at = n * self.quarter + j * HEAD
        return self.above[:, at:at + HEAD]

    def actions(self):
        return self.pair(self.near[:, 4 * self.half:], self.oth[:, 4 * self.half:]) + [self.above[:, 4 * self.quarter:]]


def block(x, i, j):
    return x[i * TOK:(i + 1) * TOK, j * TOK:(j + 1) * TOK]


def column(blocks):
    return jnp.concatenate(blocks, 0)


def soften(raw, prods, biases, keep=None):
    scores = [r * SCALE2 + b for r, b in zip(raw, biases)]
    top = jnp.max(functools.reduce(jnp.maximum, scores), 0, keepdims=True)
    weights = [jnp.exp2(s - top) for s in scores]
    total = jnp.sum(functools.reduce(jnp.add, weights), 0, keepdims=True)
    mixed = [w * p for w, p in zip(weights, prods)]
    moment = jnp.sum(functools.reduce(jnp.add, mixed), 0, keepdims=True)
    inverse = 1.0 / total
    if keep is not None:
        inverse = inverse * keep
    delta = moment * inverse
    scaled = inverse * SCALE
    prob = [(w * inverse).astype(BF16) for w in weights]
    dscore = [((w * scaled) * (p - delta)).astype(BF16) for w, p in zip(weights, prods)]
    return prob, dscore


class Masks:
    def __init__(self, clips, place, lengths, robots):
        frame_a = 2 * place[1]
        start_a, robot_a = clip_of(frame_a, lengths, robots, clips)
        start_b, robot_b = clip_of(frame_a + 1, lengths, robots, clips)
        start_n, robot_n = clip_of(frame_a + 2, lengths, robots, clips)
        self.wide_below = start_a == frame_a - 2
        self.wide_above = start_n == frame_a
        self.robots = (robot_a, robot_b, robot_n)

        def bias(valid):
            return jnp.where(valid, jnp.float32(0), jnp.float32(LOW))

        zero = jnp.float32(0)
        self.a = (bias(self.wide_below), bias(start_a <= frame_a - 1), zero)
        self.b = (bias(start_b <= frame_a - 1), bias(start_b <= frame_a), zero)
        self.n = (zero, zero, zero)
        self.scale_a = jnp.where(self.wide_below, 0.0, 1.0).astype(F32)
        self.scale_n = jnp.where(self.wide_above, 1.0, 0.0).astype(F32)


def shifts(view, masks, adapters, adapted, adapted_t):
    for n, (act, robot) in enumerate(zip(view.actions(), masks.robots)):
        table = adapters[robot]
        adapted[n * TOK:(n + 1) * TOK, :] = dot(act, table, 1, 1).astype(BF16)
        if adapted_t is not None:
            adapted_t[:, n * TOK:(n + 1) * TOK] = dot(table, act, 1, 1).astype(BF16)


def narrow_head(view, masks, adapted, up_h, j):
    none = jnp.zeros((TOK, TOK), BF16)
    shift = dot(adapted[: 2 * TOK], up_h, 1, 0)
    query = (column(view.both(0, 0, j)).astype(F32) + shift).astype(BF16)
    grad = column(view.both(1, 0, j))
    keys = column([view.lower(2, j), view.lower(0, j)] + view.both(2, 0, j))
    values = column([view.lower(3, j), view.lower(1, j)] + view.both(3, 0, j))
    raw = dot(keys, query, 1, 1)
    prod = dot(values, grad, 1, 1)
    prob_a, dscore_a = soften([block(raw, i, 0) for i in range(3)], [block(prod, i, 0) for i in range(3)], masks.a)
    prob_b, dscore_b = soften([block(raw, i, 1) for i in range(1, 4)], [block(prod, i, 1) for i in range(1, 4)], masks.b)
    prob = jnp.concatenate([column(prob_a + [none]), column([none] + prob_b)], 1)
    dscore = jnp.concatenate([column(dscore_a + [none]), column([none] + dscore_b)], 1)
    return query, grad, keys, prob, dscore


def wide_head(view, masks, adapted, up_h, j):
    none = jnp.zeros((TOK, TOK), BF16)
    shift = dot(adapted[...], up_h, 1, 0)
    query = (column(view.both(0, 1, j) + [view.upper(0, j)]).astype(F32) + shift).astype(BF16)
    grad = column(view.both(1, 1, j) + [view.upper(1, j)])
    keys = column([view.lower(2, j)] + view.both(2, 1, j) + [view.upper(2, j)])
    values = column([view.lower(3, j)] + view.both(3, 1, j) + [view.upper(3, j)])
    raw = dot(keys[: 3 * TOK], query[: 2 * TOK], 1, 1)
    prod = dot(values[: 3 * TOK], grad[: 2 * TOK], 1, 1)
    raw_n = dot(keys[TOK:], query[2 * TOK:], 1, 1)
    prod_n = dot(values[TOK:], grad[2 * TOK:], 1, 1)
    prob_a, dscore_a = soften(
        [block(raw, i, 0) for i in range(2)], [block(prod, i, 0) for i in range(2)], masks.a[1:], masks.scale_a
    )
    prob_b, dscore_b = soften([block(raw, i, 1) for i in range(3)], [block(prod, i, 1) for i in range(3)], masks.b)
    prob_n, dscore_n = soften(
        [block(raw_n, i, 0) for i in range(3)], [block(prod_n, i, 0) for i in range(3)], masks.n, masks.scale_n
    )
    prob = jnp.concatenate([column(prob_a + [none, none]), column(prob_b + [none]), column([none] + prob_n)], 1)
    dscore = jnp.concatenate([column(dscore_a + [none, none]), column(dscore_b + [none]), column([none] + dscore_n)], 1)
    return query, grad, keys, prob, dscore


def rows_kernel(
    clips, place, lengths, robots, adapters, near, oth, below, above, up_hbm, payload,
    up, adapted, adapted_t, agrad_t, pay, sem,
):
    view = Views(place, near, oth, below, above)
    half, quarter = view.half, view.quarter
    five = quarter // HEAD
    load = pltpu.make_async_copy(
        up_hbm.at[:, pl.ds(pl.multiple_of(place[0] * half, HEAD), half)], up, sem.at[0]
    )
    load.start()
    masks = Masks(clips, place, lengths, robots)
    shifts(view, masks, adapters, adapted, adapted_t)
    agrad_t[...] = jnp.zeros_like(agrad_t)
    pay[:, 2 * five:, :] = jnp.zeros((RANK, ROWS - 2 * five, HEAD), F32)
    load.wait()

    def sums(keys, dscore, up_h, rows, head):
        query_grad = dot(keys, dscore, 0, 0)
        high = query_grad.astype(BF16)
        low = (query_grad - high.astype(F32)).astype(BF16)
        agrad_t[:, :rows] += dot(up_h, high, 1, 0) + dot(up_h, low, 1, 0)
        term = dot(adapted_t[:, :rows], high, 1, 1) + dot(adapted_t[:, :rows], low, 1, 1)
        pay[:, head, :] = term

    for j in range(five):
        up_h = up[:, j * HEAD:(j + 1) * HEAD]
        _, _, keys, _, dscore = narrow_head(view, masks, adapted, up_h, j)
        sums(keys, dscore, up_h, 2 * TOK, j)
        up_h = up[:, quarter + j * HEAD:quarter + (j + 1) * HEAD]
        _, _, keys, _, dscore = wide_head(view, masks, adapted, up_h, j)
        sums(keys, dscore, up_h, 3 * TOK, five + j)

    terms = []
    for n, act in enumerate(view.actions()):
        whole = agrad_t[:, n * TOK:(n + 1) * TOK]
        high = whole.astype(BF16)
        low = (whole - high.astype(F32)).astype(BF16)
        terms.append(dot(high, act, 1, 0) + dot(low, act, 1, 0))
    blank = jnp.zeros((RANK, HEAD), F32)
    for s in range(4):
        pay[:, 2 * five + s, :] = functools.reduce(
            jnp.add, [jnp.where(robot == s, term, blank) for robot, term in zip(masks.robots, terms)]
        )
    payload[...] = pay[...].astype(BF16)


def rows_call(scalars, adapters, near, oth, below, above, up):
    half = up.shape[1] // 2
    five = half // 2 // HEAD
    return pl.pallas_call(
        functools.partial(rows_kernel, scalars[1].shape[0]),
        in_specs=[smem()] * 3 + [vmem()] * 5 + [hbm()],
        out_specs=vmem(),
        out_shape=jax.ShapeDtypeStruct((RANK, ROWS, HEAD), BF16),
        scratch_shapes=[
            pltpu.VMEM((RANK, half), BF16),
            pltpu.VMEM((3 * TOK, RANK), BF16),
            pltpu.VMEM((RANK, 3 * TOK), BF16),
            pltpu.VMEM((RANK, 3 * TOK), F32),
            pltpu.VMEM((RANK, ROWS, HEAD), F32),
            pltpu.SemaphoreType.DMA((1,)),
        ],
        compiler_params=pltpu.CompilerParams(vmem_limit_bytes=16 * MIB),
        cost_estimate=pl.CostEstimate(
            flops=2 * five * 7 * 512 * 256 * 128, bytes_accessed=12 * MIB, transcendentals=five * 1024 * 256
        ),
        name="attend_rows",
    )(*scalars, adapters, near, oth, below, above, fixed(up))


def keys_kernel(
    clips, place, lengths, robots, adapters, oth, below, above, q, g, k, v, act, up_hbm,
    sum_a, sum_b, ret_down, ret_up,
    near, up, adapted, keep_a, keep_b, keep_down, keep_up, sem_in, sem_out,
):
    view = Views(place, near, oth, below, above)
    half, quarter = view.half, view.quarter
    five = quarter // HEAD
    side = pl.ds(pl.multiple_of(place[0] * half, HEAD), half)
    pairs = [(x.at[:, side], near.at[:, pl.ds(n * half, half)]) for n, x in enumerate((q, g, k, v))]
    pairs += [(act, near.at[:, pl.ds(4 * half, HEAD)]), (up_hbm.at[:, side], up)]
    loads = [pltpu.make_async_copy(x, y, sem_in.at[n]) for n, (x, y) in enumerate(pairs)]
    for load in loads:
        load.start()
    masks = Masks(clips, place, lengths, robots)
    for load in loads:
        load.wait()
    shifts(view, masks, adapters, adapted, None)
    stores = []
    for j in range(five):
        cols = slice(j * HEAD, (j + 1) * HEAD)
        query, grad, _, prob, dscore = narrow_head(view, masks, adapted, up[:, cols], j)
        wide_parts = []
        for n, part in enumerate((dot(dscore, query, 1, 0), dot(prob, grad, 1, 0))):
            wide_parts.append(part[:TOK])
            keep_down[n, :, cols] = part[TOK:2 * TOK].astype(BF16)
            keep_a[n, 0, :, cols] = part[2 * TOK:3 * TOK]
            keep_b[n, 0, :, cols] = part[3 * TOK:]
        up_h = up[:, quarter + j * HEAD:quarter + (j + 1) * HEAD]
        query, grad, _, prob, dscore = wide_head(view, masks, adapted, up_h, j)
        for n, part in enumerate((dot(dscore, query, 1, 0), dot(prob, grad, 1, 0))):
            keep_down[2 + n, :, cols] = jnp.where(masks.wide_below, wide_parts[n], part[:TOK]).astype(BF16)
            keep_a[n, 1, :, cols] = part[TOK:2 * TOK]
            keep_b[n, 1, :, cols] = part[2 * TOK:3 * TOK]
            keep_up[n, :, cols] = part[3 * TOK:].astype(BF16)
        span = pl.ds(j * HEAD, HEAD)
        for n, (x, y) in enumerate(((keep_down, ret_down), (keep_up, ret_up), (keep_a, sum_a), (keep_b, sum_b))):
            at = (slice(None),) * (len(x.shape) - 1) + (span,)
            stores.append(pltpu.make_async_copy(x.at[at], y.at[at], sem_out.at[j, n]))
            stores[-1].start()
    for store in stores:
        store.wait()


def keys_call(scalars, adapters, oth, below, above, own, act, up):
    half = up.shape[1] // 2
    quarter = half // 2
    five = quarter // HEAD
    shapes = [((4, TOK, quarter), BF16), ((2, TOK, quarter), BF16)]
    sums = ((2, 2, TOK, quarter), F32)
    return pl.pallas_call(
        functools.partial(keys_kernel, scalars[1].shape[0]),
        in_specs=[smem()] * 3 + [vmem()] * 4 + [hbm()] * 6,
        out_specs=[hbm()] * 4,
        out_shape=[pltpu.HBM(*x) for x in (sums, sums, *shapes)],
        scratch_shapes=[
            pltpu.VMEM((TOK, 4 * half + HEAD), BF16),
            pltpu.VMEM((RANK, half), BF16),
            pltpu.VMEM((3 * TOK, RANK), BF16),
            pltpu.VMEM(*sums),
            pltpu.VMEM(*sums),
            pltpu.VMEM(*shapes[0]),
            pltpu.VMEM(*shapes[1]),
            pltpu.SemaphoreType.DMA((6,)),
            pltpu.SemaphoreType.DMA((five, 4)),
        ],
        compiler_params=pltpu.CompilerParams(vmem_limit_bytes=24 * MIB),
        cost_estimate=pl.CostEstimate(
            flops=2 * five * 9 * 512 * 256 * 128, bytes_accessed=10 * MIB, transcendentals=five * 1024 * 256
        ),
        name="attend_keys",
    )(*scalars, adapters, oth, below, above, *(fixed(x) for x in (*own, act, up)))


def join_kernel(
    clips, place, lengths, robots, sum_a_hbm, sum_b_hbm, above, below, mine, theirs, sum_a, sum_b, sems
):
    loads = [
        pltpu.make_async_copy(x.at[n], y.at[n], sems.at[2 * m + n])
        for m, (x, y) in enumerate(((sum_a_hbm, sum_a), (sum_b_hbm, sum_b)))
        for n in range(2)
    ]
    for load in loads:
        load.start()
    first = place[0] == 0
    frame_a = 2 * place[1]
    start_n, _ = clip_of(frame_a + 2, lengths, robots, clips)
    wide = start_n == frame_a
    quarter = above.shape[2]
    for n in range(2):
        loads[n].wait()
        loads[2 + n].wait()
        for group in range(2):
            second = above[2 + n].astype(F32)
            if group == 0:
                a = sum_a[n, 0] + jnp.where(wide, second, 0.0)
                b = sum_b[n, 0] + above[n].astype(F32)
            else:
                a = sum_a[n, 1] + below[n].astype(F32)
                b = sum_b[n, 1] + jnp.where(wide, 0.0, second)
            cols = slice(group * quarter, (group + 1) * quarter)
            mine[n, :, cols] = jnp.where(first, a, b).astype(BF16)
            theirs[n, :, cols] = jnp.where(first, b, a).astype(BF16)


def join(scalars, sum_a, sum_b, above, below):
    shape = (2, TOK, 2 * above.shape[2])
    return pl.pallas_call(
        functools.partial(join_kernel, scalars[1].shape[0]),
        in_specs=[smem()] * 3 + [hbm()] * 2 + [vmem()] * 2,
        out_specs=[vmem()] * 2,
        out_shape=[pltpu.VMEM(shape, BF16), pltpu.VMEM(shape, BF16)],
        scratch_shapes=[
            pltpu.VMEM(sum_a.shape, F32), pltpu.VMEM(sum_b.shape, F32), pltpu.SemaphoreType.DMA((4,))
        ],
        compiler_params=pltpu.CompilerParams(vmem_limit_bytes=8 * MIB),
        cost_estimate=pl.CostEstimate(flops=MIB, bytes_accessed=6 * MIB, transcendentals=0),
        name="join",
    )(*scalars, fixed(sum_a), fixed(sum_b), above, below)


def place_kernel(place, mine, other, key_grad, value_grad, sems):
    half = mine.shape[2]
    copies = []
    for n, out in enumerate((key_grad, value_grad)):
        for side, source in ((place[0], mine), (1 - place[0], other)):
            cols = pl.ds(pl.multiple_of(side * half, HEAD), half)
            copies.append(pltpu.make_async_copy(source.at[n], out.at[:, cols], sems.at[len(copies)]))
    for copy in copies:
        copy.start()
    for copy in copies:
        copy.wait()


def place_halves(place, mine, other):
    shape = (TOK, 2 * mine.shape[2])
    return pl.pallas_call(
        place_kernel,
        in_specs=[smem()] + [vmem()] * 2,
        out_specs=[hbm()] * 2,
        out_shape=[pltpu.HBM(shape, BF16), pltpu.HBM(shape, BF16)],
        scratch_shapes=[pltpu.SemaphoreType.DMA((4,))],
        compiler_params=pltpu.CompilerParams(vmem_limit_bytes=4 * MIB),
        cost_estimate=pl.CostEstimate(flops=0, bytes_accessed=4 * MIB, transcendentals=0),
        name="place_halves",
    )(place, mine, other)


def first_sum_kernel(nz, ny, pieces, out):
    for y in range(ny):
        total = functools.reduce(jnp.add, [pieces[z * ny + y].astype(F32) for z in range(nz)]).astype(BF16)
        for n in range(out.shape[0]):
            out[n, y] = total


def first_sum(pieces, nz, ny, peers):
    return pl.pallas_call(
        functools.partial(first_sum_kernel, nz, ny),
        in_specs=[vmem()],
        out_specs=vmem(),
        out_shape=pltpu.VMEM((peers, ny, ROWS, HEAD), BF16),
        compiler_params=pltpu.CompilerParams(vmem_limit_bytes=2 * MIB),
        name="first_sum",
    )(pieces)


def second_sum_kernel(nz, ny, up_rows, pieces, out):
    totals = [functools.reduce(jnp.add, [pieces[n, y].astype(F32) for n in range(pieces.shape[0])]) for y in range(ny)]
    everything = functools.reduce(jnp.add, totals)
    is_up = lax.broadcasted_iota(jnp.int32, (ROWS, HEAD), 0) < up_rows
    for y in range(ny):
        message = jnp.where(is_up, everything, totals[y]).astype(BF16)
        for z in range(nz):
            out[z * ny + y] = message


def second_sum(pieces, nz, ny, up_rows):
    return pl.pallas_call(
        functools.partial(second_sum_kernel, nz, ny, up_rows),
        in_specs=[vmem()],
        out_specs=vmem(),
        out_shape=pltpu.VMEM((nz * ny, ROWS, HEAD), BF16),
        compiler_params=pltpu.CompilerParams(vmem_limit_bytes=2 * MIB),
        name="second_sum",
    )(pieces)


def finish_kernel(heads, place, gathered, swapped, up_grad, adapter_grad, one, two):
    per_core = heads // 2
    one[...] = gathered[...].astype(F32)
    two[...] = swapped[...].astype(F32)
    for n, part in enumerate((one, two)):
        side = place[0] if n == 0 else 1 - place[0]
        for h in range(per_core):
            cols = pl.ds(pl.multiple_of((side * per_core + h) * HEAD, HEAD), HEAD)
            up_grad[:, cols] = part[:, h, :]
    for s in range(4):
        adapter_grad[s] = one[:, per_core + s, :] + two[:, per_core + s, :]


def finish(place, gathered, swapped, heads):
    return pl.pallas_call(
        functools.partial(finish_kernel, heads),
        in_specs=[smem(), vmem(), vmem()],
        out_specs=[vmem(), vmem()],
        out_shape=[
            jax.ShapeDtypeStruct((RANK, heads * HEAD), F32),
            jax.ShapeDtypeStruct((4, RANK, HEAD), F32),
        ],
        scratch_shapes=[pltpu.VMEM((RANK, ROWS, HEAD), F32), pltpu.VMEM((RANK, ROWS, HEAD), F32)],
        compiler_params=pltpu.CompilerParams(vmem_limit_bytes=6 * MIB),
        name="finish",
    )(place, gathered, swapped)


def local(
    query_tokens, key_tokens, value_tokens, out_grad, actions, clip_lengths, clip_robots, adapters, up_proj,
):
    q, k, v, g = (t[0, 0] for t in (query_tokens, key_tokens, value_tokens, out_grad))
    act = actions[0, 0]
    heads = q.shape[1] // HEAD
    core = lax.axis_index("core")
    nz, ny = lax.axis_size("z"), lax.axis_size("y")
    chips = lax.axis_size("x") * nz
    chip = lax.axis_index("x") * nz + lax.axis_index("z")
    chain = ("x", "z")
    swap = [(0, 1), (1, 0)]
    upward = [(c, c + 1) for c in range(chips - 1)]
    downward = [(c + 1, c) for c in range(chips - 1)]
    place = jnp.stack([core, chip]).astype(jnp.int32)
    scalars = (place, clip_lengths[0, 0], clip_robots[0, 0])
    own = (q, g, k, v)
    oth = lax.ppermute(take_half(place, own, act, True), "core", swap)
    near = take_half(place, own, act, False)
    up_msg, down_msg = pack(scalars, near, oth)
    below = lax.ppermute(up_msg, chain, upward)
    above = lax.ppermute(down_msg, chain, downward)
    table = jnp.swapaxes(adapters[0], 1, 2)
    payload = rows_call(scalars, table, near, oth, below, above, up_proj)

    plane, line = ("z", "y"), ("dp", "x")
    peers = lax.axis_size("dp") * lax.axis_size("x")
    pieces = lax.all_to_all(payload, plane, 0, 0, tiled=True)
    pieces = lax.all_to_all(first_sum(pieces, nz, ny, peers), line, 0, 0, tiled=True)
    gathered = lax.all_to_all(second_sum(pieces, nz, ny, heads // 2), plane, 0, 0, tiled=True)
    swapped = lax.ppermute(gathered, "core", swap)
    up_total, adapter_total = finish(place, gathered, swapped, heads)
    adapter_total = jnp.swapaxes(adapter_total, 1, 2)

    sum_a, sum_b, ret_down, ret_up = keys_call(scalars, table, oth, below, above, own, act, up_proj)
    from_above = lax.ppermute(ret_down, chain, downward)
    from_below = lax.ppermute(ret_up, chain, upward)
    mine, theirs = join(scalars, sum_a, sum_b, from_above, from_below)
    key_grad, value_grad = place_halves(place, mine, lax.ppermute(theirs, "core", swap))
    return key_grad[None, None], value_grad[None, None], adapter_total[None], up_total


def solution(mesh):
    sizes = dict(mesh.shape)
    wide = Mesh(
        mesh.devices.reshape(sizes["dp"], 2, sizes["context"] // 4, 2, sizes["embodime"]),
        ("dp", "x", "z", "core", "y"),
    )
    frames = P("dp", "y", ("x", "z", "core"), None)
    rows = P("dp", "y", None)
    return jax.shard_map(
        local,
        mesh=wide,
        in_specs=(frames,) * 5 + (rows, rows, P("y", None, None, None), P()),
        out_specs=(frames, frames, P("y", None, None, None), P()),
        check_vma=False,
    )
```

time: 567 us -> 123 us (0.22)
  waiting for transfers between devices: 470 us -> 21.7 us
  starting transfers between devices: 13.2 us -> 49.6 us
  Pallas kernels: 0 us -> 32.6 us
  matrix products: 25 us -> 0 us
  local copies, waits for them, and re-layouts: 24.9 us -> 0.02 us
  blocking collectives: 0 us -> 16.6 us
  other arithmetic: 16 us -> 0.08 us
  between operations: 16.5 us -> 0.83 us
    psum x2 -> x0, waiting for transfers between devices: 422 us -> none  [the longest x1 274 us: local(): up_total = lax.psum(up_term, ('dp', 'context', 'embodime'))]
    ppermute x4 -> x7, waiting for transfers between devices: 48.6 us -> 14.2 us  [the longest x1 13.4 us: local(): below = lax.ppermute(up_msg, chain, upward)]
    pallas_call x0 -> x10, Pallas kernels: none -> 32.6 us  [the longest x1 11.1 us: rows_call(): pl.pallas_call(functools.partial(rows_kernel, scalars[1].shape[0]), in_sp...]
    dot_general x21 -> x0, matrix products: 25 us -> none  [the longest x3 6.68 us: local(): jnp.einsum('hqk,qhe->khe', dscore, query3, preferred_element_type=jnp.flo...]
    all_to_all x0 -> x2, starting transfers between devices: none -> 22.4 us  [the longest x1 13.4 us: local(): pieces = lax.all_to_all(payload, plane, 0, 0, tiled=True)]
    all_to_all x0 -> x1, blocking collectives: none -> 16.6 us  [local(): lax.all_to_all(first_sum(pieces, nz, ny, peers), line, 0, 0, tiled=True)]
    ppermute x4 -> x7, starting transfers between devices: 12.9 us -> 27.2 us  [the longest x1 8.79 us: local(): oth = lax.ppermute(take_half(place, own, act, True), 'core', swap)]
    another operation x7 -> x0, local copies, waits for them, and re-layouts: 12.1 us -> none  [the longest x6 12 us: local(): jnp.stack([key_part.reshape(tokens_here, width), value_part.reshape(token...]
  transfers between devices with their start and end apart: 6 -> 9, of which waited for: 6 -> 3; matrix products, arithmetic and copies ran while one was open for 5% -> 0% of each run, Pallas kernels for 0% -> 14%
where the time goes in v4:
time: 123 us; the launch traced here: 121 us
  starting transfers between devices  49.6 us (40%)
  Pallas kernels  32.6 us (27%)
  waiting for transfers between devices  21.7 us (18%)
  blocking collectives  16.6 us (13%)
    all_to_all x1, blocking collectives, local(): lax.all_to_all(first_sum(pieces, nz, ny, peers), line, 0, 0, tiled=True)  16.6 us
    all_to_all x1, starting transfers between devices, local(): pieces = lax.all_to_all(payload, plane, 0, 0, tiled=True)  13.4 us
    ppermute x1, waiting for transfers between devices, local(): below = lax.ppermute(up_msg, chain, upward)  13.4 us
    pallas_call x1, Pallas kernels, rows_call(): pl.pallas_call(functools.partial(rows_kernel, scalars[1].shape[0]), in_sp...  11.1 us
    pallas_call x1, Pallas kernels, keys_call(): pl.pallas_call(functools.partial(keys_kernel, scalars[1].shape[0]), in_sp...  10.3 us
    all_to_all x1, starting transfers between devices, local(): lax.all_to_all(second_sum(pieces, nz, ny, heads // 2), plane, 0, 0, tiled...  9.06 us
    ppermute x1, starting transfers between devices, local(): oth = lax.ppermute(take_half(place, own, act, True), 'core', swap)  8.79 us
    all_to_all x1, waiting for transfers between devices, local(): lax.all_to_all(second_sum(pieces, nz, ny, heads // 2), plane, 0, 0, tiled...  7.53 us
  transfers between devices with their start and end apart: 9, of which 3 were waited for; matrix products, arithmetic and copies ran while one was open for 0% of the time, Pallas kernels for 14%

profile of v4, /device:TPU:1, one launch (start us, length us, event | category | flops | bytes accessed | tf_op | source)
XLA Modules:
  0.0 121.5 jit_solution(400533768560006349)
XLA Ops:
  0.6 0.1 pad_add_fusion.place
  0.7 1.9 %take_far.1 = bf16[128,5248]{1,0:T(8,128)(2,1)S(1)} custom-call(s32[2]{0:T(128)S(1)} %pad_add_fusion.place, bf16[128,2560]{1,0:T(8,128)(2,1)} %bitcast.27, bf16[128,2560]{1,0:T(8,128)(2,1)} %bitcast.30, bf16[128,2560]{1,0:T(8,128)(2,1)} %bitcast.33, bf16[128,2560]{1,0:T(8,128)(2,1)} %bitcast.36, bf16[128,128]{1,0:T(8,128)(2,1)} %bitcast.39), custom_call_target="tpu_custom_call" | custom-call | bytes 4194304 | tf_op jit(solution)/shard_map/take_far/pallas_call | solution.py:74
  2.6 0.0 copy-start.1
  2.6 8.8 %collective-permute-start = (bf16[128,5248]{1,0:T(8,128)(2,1)S(1)}, bf16[128,5248]{1,0:T(8,128)(2,1)S(1)}, u32[]{:S(2)}, u32[]{:S(2)}) collective-permute-start(bf16[128,5248]{1,0:T(8,128)(2,1)S(1)} %take_far.1), channel_id=1, source_target_pairs={{0,8},{8,0},{1,9},{9,1},{2,10},{10,2},{3,11},{11,3},{4,12},{12,4},... | collective-permute-start | bytes 4030472 | tf_op jit(solution)/shard_map/ppermute | solution.py:546
  11.4 1.9 %take_near.1.near = bf16[128,5248]{1,0:T(8,128)(2,1)S(1)} custom-call(s32[2]{0:T(128)S(1)} %pad_add_fusion.place, bf16[128,2560]{1,0:T(8,128)(2,1)} %bitcast.28, bf16[128,2560]{1,0:T(8,128)(2,1)} %bitcast.31, bf16[128,2560]{1,0:T(8,128)(2,1)} %bitcast.34, bf16[128,2560]{1,0:T(8,128)(2,1)} %bitcast.37, bf16[128,128]{1,0:T(8,128)(2,1)} %bitcast.40), custom_call_target="tpu_custom_call" | custom-call | bytes 4194304 | tf_op jit(solution)/shard_map/take_near/pallas_call | solution.py:74
  13.3 0.8 collective-permute-done.oth
  14.1 0.8 pack.1
  14.9 1.3 %collective-permute-start.2 = (bf16[128,2688]{1,0:T(8,128)(2,1)S(1)}, bf16[128,2688]{1,0:T(8,128)(2,1)S(1)}, u32[]{:S(2)}, u32[]{:S(2)}) collective-permute-start(bf16[128,2688]{1,0:T(8,128)(2,1)S(1)} %get-tuple-element.17), channel_id=1, source_target_pairs={{16,0},{32,16},{48,32},{64,48},{80,64},{96,80},{112,96},{128,112},... | collective-permute-start | bytes 2064392 | tf_op jit(solution)/shard_map/ppermute | solution.py:550
  16.2 4.0 %collective-permute-start.1 = (bf16[128,2560]{1,0:T(8,128)(2,1)S(1)}, bf16[128,2560]{1,0:T(8,128)(2,1)S(1)}, u32[]{:S(2)}, u32[]{:S(2)}) collective-permute-start(bf16[128,2560]{1,0:T(8,128)(2,1)S(1)} %get-tuple-element.16), channel_id=1, source_target_pairs={{0,16},{16,32},{32,48},{48,64},{64,80},{80,96},{96,112},{112,128},... | collective-permute-start | bytes 1966088 | tf_op jit(solution)/shard_map/ppermute | solution.py:549
  20.3 13.4 %collective-permute-done.1.below = bf16[128,2560]{1,0:T(8,128)(2,1)S(1)} collective-permute-done((bf16[128,2560]{1,0:T(8,128)(2,1)S(1)}, bf16[128,2560]{1,0:T(8,128)(2,1)S(1)}, u32[]{:S(2)}, u32[]{:S(2)}) %collective-permute-start.1) | collective-permute-done | bytes 655392 | tf_op jit(solution)/shard_map/ppermute | solution.py:549
  33.6 11.1 %attend_rows.1 = bf16[64,16,128]{2,1,0:T(8,128)(2,1)} custom-call(s32[2]{0:T(128)S(1)} %pad_add_fusion.place, s32[16]{0:T(128)S(1)} %bitcast.20, s32[16]{0:T(128)S(1)} %bitcast.24, bf16[4,64,128]{2,1,0:T(8,128)(2,1)S(1)} %bitcast.17, bf16[128,5248]{1,0:T(8,128)(2,1)S(1)} %take_near.1.near, bf16[128,5248]{1,0:T(8,128)(2,1)S(1)} %collective-permute-done.oth, ...), custom_call_target="tpu_custom_call" | custom-call | flops 1174405120 | bytes 12582912 | tf_op jit(solution)/shard_map/attend_rows/pallas_call | solution.py:293
  44.7 13.4 %all-to-all-start = ((bf16[64,16,128]{2,1,0:T(8,128)(2,1)}), bf16[64,16,128]{2,1,0:T(8,128)(2,1)S(1)}, u32[]{:S(2)}, u32[]{:S(2)}) async-start(bf16[64,16,128]{2,1,0:T(8,128)(2,1)} %attend_rows.1), calls=%async_computation | async-start | bytes 524288 | tf_op jit(solution)/shard_map/all_to_all | solution.py:556
  58.1 10.3 %attend_keys.1 = (f32[2,2,128,640]{3,2,1,0:T(8,128)}, f32[2,2,128,640]{3,2,1,0:T(8,128)}, bf16[4,128,640]{2,1,0:T(8,128)(2,1)}, bf16[2,128,640]{2,1,0:T(8,128)(2,1)}) custom-call(s32[2]{0:T(128)S(1)} %pad_add_fusion.place, s32[16]{0:T(128)S(1)} %bitcast.21, s32[16]{0:T(128)S(1)} %bitcast.25, bf16[4,64,128]{2,1,0:T(8,128)(2,1)S(1)} %bitcast.18, ...), custom_call_target="tpu_custom_call" | custom-call | flops 1509949440 | bytes 10485760 | tf_op jit(solution)/shard_map/attend_keys/pallas_call | solution.py:364
  68.4 1.3 %collective-permute-start.3 = (bf16[4,128,640]{2,1,0:T(8,128)(2,1)}, bf16[4,128,640]{2,1,0:T(8,128)(2,1)S(1)}, u32[]{:S(2)}, u32[]{:S(2)}) collective-permute-start(bf16[4,128,640]{2,1,0:T(8,128)(2,1)} %get-tuple-element.20), channel_id=1, source_target_pairs={{16,0},{32,16},{48,32},{64,48},{80,64},{96,80},{112,96},{128,112},... | collective-permute-start | bytes 1966088 | tf_op jit(solution)/shard_map/ppermute | solution.py:564
  69.7 4.0 %collective-permute-start.4 = (bf16[2,128,640]{2,1,0:T(8,128)(2,1)}, bf16[2,128,640]{2,1,0:T(8,128)(2,1)S(1)}, u32[]{:S(2)}, u32[]{:S(2)}) collective-permute-start(bf16[2,128,640]{2,1,0:T(8,128)(2,1)} %get-tuple-element.21), channel_id=1, source_target_pairs={{0,16},{16,32},{32,48},{48,64},{64,80},{80,96},{96,112},{112,128},... | collective-permute-start | bytes 983048 | tf_op jit(solution)/shard_map/ppermute | solution.py:565
  73.8 16.6 %all_to_all.15.pieces = bf16[4,8,16,128]{3,2,1,0:T(8,128)(2,1)S(1)} all-to-all(bf16[4,8,16,128]{3,2,1,0:T(8,128)(2,1)S(1)} %first_sum.1), channel_id=1, replica_groups=mesh['dp'=2,'x'=2,'z'=8,'core'=2,'y'=8] {'dp','x'}, dimensions={0} | all-to-all | bytes 262144 | tf_op jit(solution)/shard_map/all_to_all | solution.py:557
  90.4 0.7 second_sum.1
  91.1 9.1 %all-to-all-start.2 = ((bf16[64,16,128]{2,1,0:T(8,128)(2,1)}), bf16[64,16,128]{2,1,0:T(8,128)(2,1)S(1)}, u32[]{:S(2)}, u32[]{:S(2)}) async-start(bf16[64,16,128]{2,1,0:T(8,128)(2,1)} %second_sum.1), calls=%async_computation.2 | async-start | bytes 524288 | tf_op jit(solution)/shard_map/all_to_all | solution.py:558
  100.2 2.5 %join.1 = (bf16[2,128,1280]{2,1,0:T(8,128)(2,1)S(1)}, bf16[2,128,1280]{2,1,0:T(8,128)(2,1)S(1)}) custom-call(s32[2]{0:T(128)S(1)} %pad_add_fusion.place, s32[16]{0:T(128)S(1)} %bitcast.22, s32[16]{0:T(128)S(1)} %bitcast.26, f32[2,2,128,640]{3,2,1,0:T(8,128)} %get-tuple-element.18.sum_a_hbm, f32[2,2,128,640]{3,2,1,0:T(8,128)} %get-tuple-element.19.sum_b_hbm, ...), custom_call_target="tpu_custom_call" | custom-call | flops 1048576 | bytes 6291456 | tf_op jit(solution)/shard_map/join/pallas_call | solution.py:421
  102.7 2.8 %collective-permute-start.5 = (bf16[2,128,1280]{2,1,0:T(8,128)(2,1)S(1)}, bf16[2,128,1280]{2,1,0:T(8,128)(2,1)S(1)}, u32[]{:S(2)}, u32[]{:S(2)}) collective-permute-start(bf16[2,128,1280]{2,1,0:T(8,128)(2,1)S(1)} %get-tuple-element.23), channel_id=1, source_target_pairs={{0,8},{8,0},{1,9},{9,1},{2,10},{10,2},{3,11},{11,3},{4,12},{12,4},... | collective-permute-start | bytes 1966088 | tf_op jit(solution)/shard_map/ppermute | solution.py:567
  105.5 7.5 %all-to-all-done.2.gathered = bf16[64,16,128]{2,1,0:T(8,128)(2,1)S(1)} async-done(((bf16[64,16,128]{2,1,0:T(8,128)(2,1)}), bf16[64,16,128]{2,1,0:T(8,128)(2,1)S(1)}, u32[]{:S(2)}, u32[]{:S(2)}) %all-to-all-start.2) | async-done | bytes 262176 | tf_op jit(solution)/shard_map/all_to_all | solution.py:558
  113.0 5.0 %collective-permute-start.6 = (bf16[64,16,128]{2,1,0:T(8,128)(2,1)S(1)}, bf16[64,16,128]{2,1,0:T(8,128)(2,1)S(1)}, u32[]{:S(2)}, u32[]{:S(2)}) collective-permute-start(bf16[64,16,128]{2,1,0:T(8,128)(2,1)S(1)} %all-to-all-done.2.gathered), channel_id=1, source_target_pairs={{0,8},{8,0},{1,9},{9,1},{2,10},{10,2},{3,11},{11,3},{4,12},{12,4},... | collective-permute-start | bytes 786440 | tf_op jit(solution)/shard_map/ppermute | solution.py:559
  118.0 1.6 %place_halves.1 = (bf16[128,2560]{1,0:T(8,128)(2,1)}, bf16[128,2560]{1,0:T(8,128)(2,1)}) custom-call(s32[2]{0:T(128)S(1)} %pad_add_fusion.place, bf16[2,128,1280]{2,1,0:T(8,128)(2,1)S(1)} %get-tuple-element.22.mine, bf16[2,128,1280]{2,1,0:T(8,128)(2,1)S(1)} %collective-permute-done.5.other), custom_call_target="tpu_custom_call" | custom-call | bytes 4194304 | tf_op jit(solution)/shard_map/place_halves/pallas_call | solution.py:450
  119.6 1.8 %finish.1 = (f32[64,2560]{1,0:T(8,128)}, f32[4,64,128]{2,1,0:T(8,128)}) custom-call(s32[2]{0:T(128)S(1)} %pad_add_fusion.place, bf16[64,16,128]{2,1,0:T(8,128)(2,1)S(1)} %all-to-all-done.2.gathered, bf16[64,16,128]{2,1,0:T(8,128)(2,1)S(1)} %collective-permute-done.6.swapped), custom_call_target="tpu_custom_call" | custom-call | tf_op jit(solution)/shard_map/finish/pallas_call | solution.py:515
  (12 shorter events, 0.1 us)
Async XLA Ops:
  2.6 11.5 %copy-start.1 = (s32[1,1,16]{2,1,0:T(1,128)S(1)}, s32[1,1,16]{2,1,0:T(1,128)}, u32[]{:S(2)}) copy-start(s32[1,1,16]{2,1,0:T(1,128)} %param.14) | copy-start | bytes 196
  2.6 11.5 %copy-start.2 = (s32[1,1,16]{2,1,0:T(1,128)S(1)}, s32[1,1,16]{2,1,0:T(1,128)}, u32[]{:S(2)}) copy-start(s32[1,1,16]{2,1,0:T(1,128)} %param.15) | copy-start | bytes 196
  2.6 11.5 %collective-permute-start = (bf16[128,5248]{1,0:T(8,128)(2,1)S(1)}, bf16[128,5248]{1,0:T(8,128)(2,1)S(1)}, u32[]{:S(2)}, u32[]{:S(2)}) collective-permute-start(bf16[128,5248]{1,0:T(8,128)(2,1)S(1)} %take_far.1), channel_id=1, source_target_pairs={{0,8},{8,0},{1,9},{9,1},{2,10},{10,2},{3,11},{11,3},{4,12},{12,4},... | collective-permute-start | bytes 4030472 | tf_op jit(solution)/shard_map/ppermute | solution.py:546
  14.1 19.5 %copy-start = (bf16[1,4,128,64]{2,3,1,0:T(8,128)(2,1)S(1)}, bf16[1,4,128,64]{2,3,1,0:T(8,128)(2,1)}, u32[]{:S(2)}) copy-start(bf16[1,4,128,64]{2,3,1,0:T(8,128)(2,1)} %param.16) | copy-start | bytes 196612
  14.9 18.7 %collective-permute-start.2 = (bf16[128,2688]{1,0:T(8,128)(2,1)S(1)}, bf16[128,2688]{1,0:T(8,128)(2,1)S(1)}, u32[]{:S(2)}, u32[]{:S(2)}) collective-permute-start(bf16[128,2688]{1,0:T(8,128)(2,1)S(1)} %get-tuple-element.17), channel_id=1, source_target_pairs={{16,0},{32,16},{48,32},{64,48},{80,64},{96,80},{112,96},{128,112},... | collective-permute-start | bytes 2064392 | tf_op jit(solution)/shard_map/ppermute | solution.py:550
  16.2 17.4 %collective-permute-start.1 = (bf16[128,2560]{1,0:T(8,128)(2,1)S(1)}, bf16[128,2560]{1,0:T(8,128)(2,1)S(1)}, u32[]{:S(2)}, u32[]{:S(2)}) collective-permute-start(bf16[128,2560]{1,0:T(8,128)(2,1)S(1)} %get-tuple-element.16), channel_id=1, source_target_pairs={{0,16},{16,32},{32,48},{48,64},{64,80},{80,96},{96,112},{112,128},... | collective-permute-start | bytes 1966088 | tf_op jit(solution)/shard_map/ppermute | solution.py:549
  44.7 29.0 %all-to-all-start = ((bf16[64,16,128]{2,1,0:T(8,128)(2,1)}), bf16[64,16,128]{2,1,0:T(8,128)(2,1)S(1)}, u32[]{:S(2)}, u32[]{:S(2)}) async-start(bf16[64,16,128]{2,1,0:T(8,128)(2,1)} %attend_rows.1), calls=%async_computation | async-start | bytes 524288 | tf_op jit(solution)/shard_map/all_to_all | solution.py:556
  68.4 31.8 %collective-permute-start.3 = (bf16[4,128,640]{2,1,0:T(8,128)(2,1)}, bf16[4,128,640]{2,1,0:T(8,128)(2,1)S(1)}, u32[]{:S(2)}, u32[]{:S(2)}) collective-permute-start(bf16[4,128,640]{2,1,0:T(8,128)(2,1)} %get-tuple-element.20), channel_id=1, source_target_pairs={{16,0},{32,16},{48,32},{64,48},{80,64},{96,80},{112,96},{128,112},... | collective-permute-start | bytes 1966088 | tf_op jit(solution)/shard_map/ppermute | solution.py:564
  69.7 30.5 %collective-permute-start.4 = (bf16[2,128,640]{2,1,0:T(8,128)(2,1)}, bf16[2,128,640]{2,1,0:T(8,128)(2,1)S(1)}, u32[]{:S(2)}, u32[]{:S(2)}) collective-permute-start(bf16[2,128,640]{2,1,0:T(8,128)(2,1)} %get-tuple-element.21), channel_id=1, source_target_pairs={{0,16},{16,32},{32,48},{48,64},{64,80},{80,96},{96,112},{112,128},... | collective-permute-start | bytes 983048 | tf_op jit(solution)/shard_map/ppermute | solution.py:565
  91.1 21.9 %all-to-all-start.2 = ((bf16[64,16,128]{2,1,0:T(8,128)(2,1)}), bf16[64,16,128]{2,1,0:T(8,128)(2,1)S(1)}, u32[]{:S(2)}, u32[]{:S(2)}) async-start(bf16[64,16,128]{2,1,0:T(8,128)(2,1)} %second_sum.1), calls=%async_computation.2 | async-start | bytes 524288 | tf_op jit(solution)/shard_map/all_to_all | solution.py:558
  102.7 15.3 %collective-permute-start.5 = (bf16[2,128,1280]{2,1,0:T(8,128)(2,1)S(1)}, bf16[2,128,1280]{2,1,0:T(8,128)(2,1)S(1)}, u32[]{:S(2)}, u32[]{:S(2)}) collective-permute-start(bf16[2,128,1280]{2,1,0:T(8,128)(2,1)S(1)} %get-tuple-element.23), channel_id=1, source_target_pairs={{0,8},{8,0},{1,9},{9,1},{2,10},{10,2},{3,11},{11,3},{4,12},{12,4},... | collective-permute-start | bytes 1966088 | tf_op jit(solution)/shard_map/ppermute | solution.py:567
  113.0 6.7 %collective-permute-start.6 = (bf16[64,16,128]{2,1,0:T(8,128)(2,1)S(1)}, bf16[64,16,128]{2,1,0:T(8,128)(2,1)S(1)}, u32[]{:S(2)}, u32[]{:S(2)}) collective-permute-start(bf16[64,16,128]{2,1,0:T(8,128)(2,1)S(1)} %all-to-all-done.2.gathered), channel_id=1, source_target_pairs={{0,8},{8,0},{1,9},{9,1},{2,10},{10,2},{3,11},{11,3},{4,12},{12,4},... | collective-permute-start | bytes 786440 | tf_op jit(solution)/shard_map/ppermute | solution.py:559

commit v5 on v4

--- a/solution.py
+++ b/solution.py
@@ -156,9 +156,9 @@
 
 
 def soften(raw, prods, biases, keep=None):
-    scores = [r * SCALE2 + b for r, b in zip(raw, biases)]
-    top = jnp.max(functools.reduce(jnp.maximum, scores), 0, keepdims=True)
-    weights = [jnp.exp2(s - top) for s in scores]
+    tops = [jnp.max(r, 0, keepdims=True) + b for r, b in zip(raw, biases)]
+    top = functools.reduce(jnp.maximum, tops)
+    weights = [jnp.exp2(r * SCALE2 + (b - top) * SCALE2) for r, b in zip(raw, biases)]
     total = jnp.sum(functools.reduce(jnp.add, weights), 0, keepdims=True)
     mixed = [w * p for w, p in zip(weights, prods)]
     moment = jnp.sum(functools.reduce(jnp.add, mixed), 0, keepdims=True)
@@ -240,15 +240,16 @@
     return query, grad, keys, prob, dscore
 
 
-def rows_kernel(
-    clips, place, lengths, robots, adapters, near, oth, below, above, up_hbm, payload,
-    up, adapted, adapted_t, agrad_t, pay, sem,
+def attend_kernel(
+    clips, place, lengths, robots, adapters, near, oth, below, above, up_hbm,
+    payload, sum_a, sum_b, ret_down, ret_up,
+    up, adapted, adapted_t, agrad_t, pay, keep_a, keep_b, keep_down, keep_up, sem_in, sem_out,
 ):
     view = Views(place, near, oth, below, above)
     half, quarter = view.half, view.quarter
     five = quarter // HEAD
     load = pltpu.make_async_copy(
-        up_hbm.at[:, pl.ds(pl.multiple_of(place[0] * half, HEAD), half)], up, sem.at[0]
+        up_hbm.at[:, pl.ds(pl.multiple_of(place[0] * half, HEAD), half)], up, sem_in.at[0]
     )
     load.start()
     masks = Masks(clips, place, lengths, robots)
@@ -265,13 +266,31 @@
         term = dot(adapted_t[:, :rows], high, 1, 1) + dot(adapted_t[:, :rows], low, 1, 1)
         pay[:, head, :] = term
 
+    stores = []
     for j in range(five):
-        up_h = up[:, j * HEAD:(j + 1) * HEAD]
-        _, _, keys, _, dscore = narrow_head(view, masks, adapted, up_h, j)
+        cols = slice(j * HEAD, (j + 1) * HEAD)
+        up_h = up[:, cols]
+        query, grad, keys, prob, dscore = narrow_head(view, masks, adapted, up_h, j)
         sums(keys, dscore, up_h, 2 * TOK, j)
+        wide_parts = []
+        for n, part in enumerate((dot(dscore, query, 1, 0), dot(prob, grad, 1, 0))):
+            wide_parts.append(part[:TOK])
+            keep_down[n, :, cols] = part[TOK:2 * TOK].astype(BF16)
+            keep_a[n, 0, :, cols] = part[2 * TOK:3 * TOK]
+            keep_b[n, 0, :, cols] = part[3 * TOK:]
         up_h = up[:, quarter + j * HEAD:quarter + (j + 1) * HEAD]
-        _, _, keys, _, dscore = wide_head(view, masks, adapted, up_h, j)
+        query, grad, keys, prob, dscore = wide_head(view, masks, adapted, up_h, j)
         sums(keys, dscore, up_h, 3 * TOK, five + j)
+        for n, part in enumerate((dot(dscore, query, 1, 0), dot(prob, grad, 1, 0))):
+            keep_down[2 + n, :, cols] = jnp.where(masks.wide_below, wide_parts[n], part[:TOK]).astype(BF16)
+            keep_a[n, 1, :, cols] = part[TOK:2 * TOK]
+            keep_b[n, 1, :, cols] = part[2 * TOK:3 * TOK]
+            keep_up[n, :, cols] = part[3 * TOK:].astype(BF16)
+        span = pl.ds(j * HEAD, HEAD)
+        for n, (x, y) in enumerate(((keep_down, ret_down), (keep_up, ret_up), (keep_a, sum_a), (keep_b, sum_b))):
+            at = (slice(None),) * (len(x.shape) - 1) + (span,)
+            stores.append(pltpu.make_async_copy(x.at[at], y.at[at], sem_out.at[j, n]))
+            stores[-1].start()
 
     terms = []
     for n, act in enumerate(view.actions()):
@@ -285,104 +304,57 @@
             jnp.add, [jnp.where(robot == s, term, blank) for robot, term in zip(masks.robots, terms)]
         )
     payload[...] = pay[...].astype(BF16)
-
-
-def rows_call(scalars, adapters, near, oth, below, above, up):
+    for store in stores:
+        store.wait()
+
+
+def attend(scalars, adapters, near, oth, below, above, up):
     half = up.shape[1] // 2
-    five = half // 2 // HEAD
-    return pl.pallas_call(
-        functools.partial(rows_kernel, scalars[1].shape[0]),
+    quarter = half // 2
+    five = quarter // HEAD
+    shapes = [((4, TOK, quarter), BF16), ((2, TOK, quarter), BF16)]
+    sums = ((2, 2, TOK, quarter), F32)
+    return pl.pallas_call(
+        functools.partial(attend_kernel, scalars[1].shape[0]),
         in_specs=[smem()] * 3 + [vmem()] * 5 + [hbm()],
-        out_specs=vmem(),
-        out_shape=jax.ShapeDtypeStruct((RANK, ROWS, HEAD), BF16),
+        out_specs=[vmem()] + [hbm()] * 4,
+        out_shape=[jax.ShapeDtypeStruct((RANK, ROWS, HEAD), BF16)] + [pltpu.HBM(*x) for x in (sums, sums, *shapes)],
         scratch_shapes=[
             pltpu.VMEM((RANK, half), BF16),
             pltpu.VMEM((3 * TOK, RANK), BF16),
             pltpu.VMEM((RANK, 3 * TOK), BF16),
             pltpu.VMEM((RANK, 3 * TOK), F32),
             pltpu.VMEM((RANK, ROWS, HEAD), F32),
-            pltpu.SemaphoreType.DMA((1,)),
-        ],
-        compiler_params=pltpu.CompilerParams(vmem_limit_bytes=16 * MIB),
-        cost_estimate=pl.CostEstimate(
-            flops=2 * five * 7 * 512 * 256 * 128, bytes_accessed=12 * MIB, transcendentals=five * 1024 * 256
-        ),
-        name="attend_rows",
-    )(*scalars, adapters, near, oth, below, above, fixed(up))
-
-
-def keys_kernel(
-    clips, place, lengths, robots, adapters, oth, below, above, q, g, k, v, act, up_hbm,
-    sum_a, sum_b, ret_down, ret_up,
-    near, up, adapted, keep_a, keep_b, keep_down, keep_up, sem_in, sem_out,
-):
-    view = Views(place, near, oth, below, above)
-    half, quarter = view.half, view.quarter
-    five = quarter // HEAD
-    side = pl.ds(pl.multiple_of(place[0] * half, HEAD), half)
-    pairs = [(x.at[:, side], near.at[:, pl.ds(n * half, half)]) for n, x in enumerate((q, g, k, v))]
-    pairs += [(act, near.at[:, pl.ds(4 * half, HEAD)]), (up_hbm.at[:, side], up)]
-    loads = [pltpu.make_async_copy(x, y, sem_in.at[n]) for n, (x, y) in enumerate(pairs)]
-    for load in loads:
-        load.start()
-    masks = Masks(clips, place, lengths, robots)
-    for load in loads:
-        load.wait()
-    shifts(view, masks, adapters, adapted, None)
-    stores = []
-    for j in range(five):
-        cols = slice(j * HEAD, (j + 1) * HEAD)
-        query, grad, _, prob, dscore = narrow_head(view, masks, adapted, up[:, cols], j)
-        wide_parts = []
-        for n, part in enumerate((dot(dscore, query, 1, 0), dot(prob, grad, 1, 0))):
-            wide_parts.append(part[:TOK])
-            keep_down[n, :, cols] = part[TOK:2 * TOK].astype(BF16)
-            keep_a[n, 0, :, cols] = part[2 * TOK:3 * TOK]
-            keep_b[n, 0, :, cols] = part[3 * TOK:]
-        up_h = up[:, quarter + j * HEAD:quarter + (j + 1) * HEAD]
-        query, grad, _, prob, dscore = wide_head(view, masks, adapted, up_h, j)
-        for n, part in enumerate((dot(dscore, query, 1, 0), dot(prob, grad, 1, 0))):
-            keep_down[2 + n, :, cols] = jnp.where(masks.wide_below, wide_parts[n], part[:TOK]).astype(BF16)
-            keep_a[n, 1, :, cols] = part[TOK:2 * TOK]
-            keep_b[n, 1, :, cols] = part[2 * TOK:3 * TOK]
-            keep_up[n, :, cols] = part[3 * TOK:].astype(BF16)
-        span = pl.ds(j * HEAD, HEAD)
-        for n, (x, y) in enumerate(((keep_down, ret_down), (keep_up, ret_up), (keep_a, sum_a), (keep_b, sum_b))):
-            at = (slice(None),) * (len(x.shape) - 1) + (span,)
-            stores.append(pltpu.make_async_copy(x.at[at], y.at[at], sem_out.at[j, n]))
-            stores[-1].start()
-    for store in stores:
-        store.wait()
-
-
-def keys_call(scalars, adapters, oth, below, above, own, act, up):
-    half = up.shape[1] // 2
-    quarter = half // 2
-    five = quarter // HEAD
-    shapes = [((4, TOK, quarter), BF16), ((2, TOK, quarter), BF16)]
-    sums = ((2, 2, TOK, quarter), F32)
-    return pl.pallas_call(
-        functools.partial(keys_kernel, scalars[1].shape[0]),
-        in_specs=[smem()] * 3 + [vmem()] * 4 + [hbm()] * 6,
-        out_specs=[hbm()] * 4,
-        out_shape=[pltpu.HBM(*x) for x in (sums, sums, *shapes)],
-        scratch_shapes=[
-            pltpu.VMEM((TOK, 4 * half + HEAD), BF16),
-            pltpu.VMEM((RANK, half), BF16),
-            pltpu.VMEM((3 * TOK, RANK), BF16),
             pltpu.VMEM(*sums),
             pltpu.VMEM(*sums),
             pltpu.VMEM(*shapes[0]),
             pltpu.VMEM(*shapes[1]),
-            pltpu.SemaphoreType.DMA((6,)),
+            pltpu.SemaphoreType.DMA((1,)),
             pltpu.SemaphoreType.DMA((five, 4)),
         ],
         compiler_params=pltpu.CompilerParams(vmem_limit_bytes=24 * MIB),
         cost_estimate=pl.CostEstimate(
-            flops=2 * five * 9 * 512 * 256 * 128, bytes_accessed=10 * MIB, transcendentals=five * 1024 * 256
+            flops=2 * five * 12 * 512 * 256 * 128, bytes_accessed=12 * MIB, transcendentals=five * 1024 * 256
         ),
-        name="attend_keys",
-    )(*scalars, adapters, oth, below, above, *(fixed(x) for x in (*own, act, up)))
+        name="attend",
+    )(*scalars, adapters, near, oth, below, above, fixed(up))
+
+
+def hold_kernel(down_in, up_in, down_out, up_out):
+    pass
+
+
+def hold(ret_down, ret_up):
+    return pl.pallas_call(
+        hold_kernel,
+        in_specs=[hbm()] * 2,
+        out_specs=[hbm()] * 2,
+        out_shape=[pltpu.HBM(x.shape, x.dtype) for x in (ret_down, ret_up)],
+        input_output_aliases={0: 0, 1: 1},
+        compiler_params=pltpu.CompilerParams(vmem_limit_bytes=MIB),
+        cost_estimate=pl.CostEstimate(flops=MIB, bytes_accessed=MIB, transcendentals=0),
+        name="hold",
+    )(fixed(ret_down), fixed(ret_up))
 
 
 def join_kernel(
@@ -549,20 +521,19 @@
     below = lax.ppermute(up_msg, chain, upward)
     above = lax.ppermute(down_msg, chain, downward)
     table = jnp.swapaxes(adapters[0], 1, 2)
-    payload = rows_call(scalars, table, near, oth, below, above, up_proj)
+    payload, sum_a, sum_b, ret_down, ret_up = attend(scalars, table, near, oth, below, above, up_proj)
+    ret_down, ret_up = hold(ret_down, ret_up)
 
     plane, line = ("z", "y"), ("dp", "x")
     peers = lax.axis_size("dp") * lax.axis_size("x")
     pieces = lax.all_to_all(payload, plane, 0, 0, tiled=True)
     pieces = lax.all_to_all(first_sum(pieces, nz, ny, peers), line, 0, 0, tiled=True)
+    from_above = lax.ppermute(ret_down, chain, downward)
+    from_below = lax.ppermute(ret_up, chain, upward)
     gathered = lax.all_to_all(second_sum(pieces, nz, ny, heads // 2), plane, 0, 0, tiled=True)
     swapped = lax.ppermute(gathered, "core", swap)
     up_total, adapter_total = finish(place, gathered, swapped, heads)
     adapter_total = jnp.swapaxes(adapter_total, 1, 2)
-
-    sum_a, sum_b, ret_down, ret_up = keys_call(scalars, table, oth, below, above, own, act, up_proj)
-    from_above = lax.ppermute(ret_down, chain, downward)
-    from_below = lax.ppermute(ret_up, chain, upward)
     mine, theirs = join(scalars, sum_a, sum_b, from_above, from_below)
     key_grad, value_grad = place_halves(place, mine, lax.ppermute(theirs, "core", swap))
     return key_grad[None, None], value_grad[None, None], adapter_total[None], up_total

time: 123 us -> 117 us (0.951)
  Pallas kernels: 32.6 us -> 24.9 us
  waiting for transfers between devices: 21.7 us -> 29 us
  blocking collectives: 16.6 us -> 9.62 us
  starting transfers between devices: 49.6 us -> 51.7 us
    pallas_call x2, Pallas kernels: 21.4 us -> 13.7 us  [the longest x1 13.7 us: attend(): pl.pallas_call(functools.partial(attend_kernel, scalars[1].shape[0]), in_...]
    all_to_all x1, waiting for transfers between devices: 0.01 us -> 7.26 us  [local(): pieces = lax.all_to_all(payload, plane, 0, 0, tiled=True)]
    all_to_all x1, blocking collectives: 16.6 us -> 9.62 us  [local(): lax.all_to_all(first_sum(pieces, nz, ny, peers), line, 0, 0, tiled=True)]
    all_to_all x1, starting transfers between devices: 9.06 us -> 11.3 us  [local(): lax.all_to_all(second_sum(pieces, nz, ny, heads // 2), plane, 0, 0, tiled...]
  transfers between devices with their start and end apart: 9 -> 9, of which waited for: 3 -> 4; matrix products, arithmetic and copies ran while one was open for 0% -> 0% of each run, Pallas kernels for 14% -> 6%
where the time goes in v5:
time: 117 us; the launch traced here: 116 us
  starting transfers between devices  51.7 us (44%)
  waiting for transfers between devices  29 us (25%)
  Pallas kernels  24.9 us (21%)
  blocking collectives  9.62 us (8%)
    pallas_call x1, Pallas kernels, attend(): pl.pallas_call(functools.partial(attend_kernel, scalars[1].shape[0]), in_...  13.7 us
    ppermute x1, waiting for transfers between devices, local(): below = lax.ppermute(up_msg, chain, upward)  13.4 us
    all_to_all x1, starting transfers between devices, local(): pieces = lax.all_to_all(payload, plane, 0, 0, tiled=True)  13.2 us
    all_to_all x1, starting transfers between devices, local(): lax.all_to_all(second_sum(pieces, nz, ny, heads // 2), plane, 0, 0, tiled...  11.3 us
    all_to_all x1, blocking collectives, local(): lax.all_to_all(first_sum(pieces, nz, ny, peers), line, 0, 0, tiled=True)  9.62 us
    ppermute x1, starting transfers between devices, local(): oth = lax.ppermute(take_half(place, own, act, True), 'core', swap)  8.79 us
    all_to_all x1, waiting for transfers between devices, local(): lax.all_to_all(second_sum(pieces, nz, ny, heads // 2), plane, 0, 0, tiled...  7.53 us
    all_to_all x1, waiting for transfers between devices, local(): pieces = lax.all_to_all(payload, plane, 0, 0, tiled=True)  7.26 us
  transfers between devices with their start and end apart: 9, of which 4 were waited for; matrix products, arithmetic and copies ran while one was open for 0% of the time, Pallas kernels for 6%

profile of v5, /device:TPU:1, one launch (start us, length us, event | category | flops | bytes accessed | tf_op | source)
XLA Modules:
  0.0 116.1 jit_solution(2064187404896409493)
XLA Ops:
  0.6 0.1 pad_add_fusion.place
  0.7 1.9 %take_far.1 = bf16[128,5248]{1,0:T(8,128)(2,1)S(1)} custom-call(s32[2]{0:T(128)S(1)} %pad_add_fusion.place, bf16[128,2560]{1,0:T(8,128)(2,1)} %bitcast.24, bf16[128,2560]{1,0:T(8,128)(2,1)} %bitcast.26, bf16[128,2560]{1,0:T(8,128)(2,1)} %bitcast.28, bf16[128,2560]{1,0:T(8,128)(2,1)} %bitcast.30, bf16[128,128]{1,0:T(8,128)(2,1)} %bitcast.32), custom_call_target="tpu_custom_call" | custom-call | bytes 4194304 | tf_op jit(solution)/shard_map/take_far/pallas_call | solution.py:74
  2.6 0.0 copy-start
  2.6 8.8 %collective-permute-start = (bf16[128,5248]{1,0:T(8,128)(2,1)S(1)}, bf16[128,5248]{1,0:T(8,128)(2,1)S(1)}, u32[]{:S(2)}, u32[]{:S(2)}) collective-permute-start(bf16[128,5248]{1,0:T(8,128)(2,1)S(1)} %take_far.1), channel_id=1, source_target_pairs={{0,8},{8,0},{1,9},{9,1},{2,10},{10,2},{3,11},{11,3},{4,12},{12,4},... | collective-permute-start | bytes 4030472 | tf_op jit(solution)/shard_map/ppermute | solution.py:518
  11.4 1.9 %take_near.1.near = bf16[128,5248]{1,0:T(8,128)(2,1)S(1)} custom-call(s32[2]{0:T(128)S(1)} %pad_add_fusion.place, bf16[128,2560]{1,0:T(8,128)(2,1)} %bitcast.25, bf16[128,2560]{1,0:T(8,128)(2,1)} %bitcast.27, bf16[128,2560]{1,0:T(8,128)(2,1)} %bitcast.29, bf16[128,2560]{1,0:T(8,128)(2,1)} %bitcast.31, bf16[128,128]{1,0:T(8,128)(2,1)} %bitcast.33), custom_call_target="tpu_custom_call" | custom-call | bytes 4194304 | tf_op jit(solution)/shard_map/take_near/pallas_call | solution.py:74
  13.3 0.8 collective-permute-done.oth
  14.1 0.8 pack.1
  14.9 1.3 %collective-permute-start.2 = (bf16[128,2688]{1,0:T(8,128)(2,1)S(1)}, bf16[128,2688]{1,0:T(8,128)(2,1)S(1)}, u32[]{:S(2)}, u32[]{:S(2)}) collective-permute-start(bf16[128,2688]{1,0:T(8,128)(2,1)S(1)} %get-tuple-element.20), channel_id=1, source_target_pairs={{16,0},{32,16},{48,32},{64,48},{80,64},{96,80},{112,96},{128,112},... | collective-permute-start | bytes 2064392 | tf_op jit(solution)/shard_map/ppermute | solution.py:522
  16.2 4.0 %collective-permute-start.1 = (bf16[128,2560]{1,0:T(8,128)(2,1)S(1)}, bf16[128,2560]{1,0:T(8,128)(2,1)S(1)}, u32[]{:S(2)}, u32[]{:S(2)}) collective-permute-start(bf16[128,2560]{1,0:T(8,128)(2,1)S(1)} %get-tuple-element.19), channel_id=1, source_target_pairs={{0,16},{16,32},{32,48},{48,64},{64,80},{80,96},{96,112},{112,128},... | collective-permute-start | bytes 1966088 | tf_op jit(solution)/shard_map/ppermute | solution.py:521
  20.3 13.4 %collective-permute-done.1.below = bf16[128,2560]{1,0:T(8,128)(2,1)S(1)} collective-permute-done((bf16[128,2560]{1,0:T(8,128)(2,1)S(1)}, bf16[128,2560]{1,0:T(8,128)(2,1)S(1)}, u32[]{:S(2)}, u32[]{:S(2)}) %collective-permute-start.1) | collective-permute-done | bytes 655392 | tf_op jit(solution)/shard_map/ppermute | solution.py:521
  33.6 13.7 %attend.1 = (bf16[64,16,128]{2,1,0:T(8,128)(2,1)}, f32[2,2,128,640]{3,2,1,0:T(8,128)}, f32[2,2,128,640]{3,2,1,0:T(8,128)}, bf16[4,128,640]{2,1,0:T(8,128)(2,1)}, bf16[2,128,640]{2,1,0:T(8,128)(2,1)}) custom-call(s32[2]{0:T(128)S(1)} %pad_add_fusion.place, s32[16]{0:T(128)S(1)} %bitcast.18, s32[16]{0:T(128)S(1)} %bitcast.21, ...), custom_call_target="tpu_custom_call" | custom-call | flops 2013265920 | bytes 12582912 | tf_op jit(solution)/shard_map/attend/pallas_call | solution.py:317
  47.3 13.2 %all-to-all-start = ((bf16[64,16,128]{2,1,0:T(8,128)(2,1)}), bf16[64,16,128]{2,1,0:T(8,128)(2,1)S(1)}, u32[]{:S(2)}, u32[]{:S(2)}) async-start(bf16[64,16,128]{2,1,0:T(8,128)(2,1)} %get-tuple-element.31), calls=%async_computation | async-start | bytes 524288 | tf_op jit(solution)/shard_map/all_to_all | solution.py:529
  60.5 1.3 %collective-permute-start.3 = (bf16[4,128,640]{2,1,0:T(8,128)(2,1)}, bf16[4,128,640]{2,1,0:T(8,128)(2,1)S(1)}, u32[]{:S(2)}, u32[]{:S(2)}) collective-permute-start(bf16[4,128,640]{2,1,0:T(8,128)(2,1)} %get-tuple-element.25), channel_id=1, source_target_pairs={{16,0},{32,16},{48,32},{64,48},{80,64},{96,80},{112,96},{128,112},... | collective-permute-start | bytes 1966088 | tf_op jit(solution)/shard_map/ppermute | solution.py:531
  61.8 4.0 %collective-permute-start.4 = (bf16[2,128,640]{2,1,0:T(8,128)(2,1)}, bf16[2,128,640]{2,1,0:T(8,128)(2,1)S(1)}, u32[]{:S(2)}, u32[]{:S(2)}) collective-permute-start(bf16[2,128,640]{2,1,0:T(8,128)(2,1)} %get-tuple-element.26), channel_id=1, source_target_pairs={{0,16},{16,32},{32,48},{48,64},{64,80},{80,96},{96,112},{112,128},... | collective-permute-start | bytes 983048 | tf_op jit(solution)/shard_map/ppermute | solution.py:532
  65.8 7.3 %all-to-all-done.pieces = bf16[64,16,128]{2,1,0:T(8,128)(2,1)S(1)} async-done(((bf16[64,16,128]{2,1,0:T(8,128)(2,1)}), bf16[64,16,128]{2,1,0:T(8,128)(2,1)S(1)}, u32[]{:S(2)}, u32[]{:S(2)}) %all-to-all-start) | async-done | bytes 262176 | tf_op jit(solution)/shard_map/all_to_all | solution.py:529
  73.1 9.6 %all_to_all.15.pieces = bf16[4,8,16,128]{3,2,1,0:T(8,128)(2,1)S(1)} all-to-all(bf16[4,8,16,128]{3,2,1,0:T(8,128)(2,1)S(1)} %first_sum.1), channel_id=1, replica_groups=mesh['dp'=2,'x'=2,'z'=8,'core'=2,'y'=8] {'dp','x'}, dimensions={0} | all-to-all | bytes 262144 | tf_op jit(solution)/shard_map/all_to_all | solution.py:530
  82.8 0.7 second_sum.1
  83.5 11.3 %all-to-all-start.2 = ((bf16[64,16,128]{2,1,0:T(8,128)(2,1)}), bf16[64,16,128]{2,1,0:T(8,128)(2,1)S(1)}, u32[]{:S(2)}, u32[]{:S(2)}) async-start(bf16[64,16,128]{2,1,0:T(8,128)(2,1)} %second_sum.1), calls=%async_computation.2 | async-start | bytes 524288 | tf_op jit(solution)/shard_map/all_to_all | solution.py:533
  94.9 2.5 %join.1 = (bf16[2,128,1280]{2,1,0:T(8,128)(2,1)S(1)}, bf16[2,128,1280]{2,1,0:T(8,128)(2,1)S(1)}) custom-call(s32[2]{0:T(128)S(1)} %pad_add_fusion.place, s32[16]{0:T(128)S(1)} %bitcast.19, s32[16]{0:T(128)S(1)} %bitcast.22, f32[2,2,128,640]{3,2,1,0:T(8,128)} %get-tuple-element.21.sum_a_hbm, f32[2,2,128,640]{3,2,1,0:T(8,128)} %get-tuple-element.22.sum_b_hbm, ...), custom_call_target="tpu_custom_call" | custom-call | flops 1048576 | bytes 6291456 | tf_op jit(solution)/shard_map/join/pallas_call | solution.py:393
  97.3 2.8 %collective-permute-start.5 = (bf16[2,128,1280]{2,1,0:T(8,128)(2,1)S(1)}, bf16[2,128,1280]{2,1,0:T(8,128)(2,1)S(1)}, u32[]{:S(2)}, u32[]{:S(2)}) collective-permute-start(bf16[2,128,1280]{2,1,0:T(8,128)(2,1)S(1)} %get-tuple-element.28), channel_id=1, source_target_pairs={{0,8},{8,0},{1,9},{9,1},{2,10},{10,2},{3,11},{11,3},{4,12},{12,4},... | collective-permute-start | bytes 1966088 | tf_op jit(solution)/shard_map/ppermute | solution.py:538
  100.1 7.5 %all-to-all-done.2.gathered = bf16[64,16,128]{2,1,0:T(8,128)(2,1)S(1)} async-done(((bf16[64,16,128]{2,1,0:T(8,128)(2,1)}), bf16[64,16,128]{2,1,0:T(8,128)(2,1)S(1)}, u32[]{:S(2)}, u32[]{:S(2)}) %all-to-all-start.2) | async-done | bytes 262176 | tf_op jit(solution)/shard_map/all_to_all | solution.py:533
  107.6 5.0 %collective-permute-start.6 = (bf16[64,16,128]{2,1,0:T(8,128)(2,1)S(1)}, bf16[64,16,128]{2,1,0:T(8,128)(2,1)S(1)}, u32[]{:S(2)}, u32[]{:S(2)}) collective-permute-start(bf16[64,16,128]{2,1,0:T(8,128)(2,1)S(1)} %all-to-all-done.2.gathered), channel_id=1, source_target_pairs={{0,8},{8,0},{1,9},{9,1},{2,10},{10,2},{3,11},{11,3},{4,12},{12,4},... | collective-permute-start | bytes 786440 | tf_op jit(solution)/shard_map/ppermute | solution.py:534
  112.6 1.6 %place_halves.1 = (bf16[128,2560]{1,0:T(8,128)(2,1)}, bf16[128,2560]{1,0:T(8,128)(2,1)}) custom-call(s32[2]{0:T(128)S(1)} %pad_add_fusion.place, bf16[2,128,1280]{2,1,0:T(8,128)(2,1)S(1)} %get-tuple-element.27.mine, bf16[2,128,1280]{2,1,0:T(8,128)(2,1)S(1)} %collective-permute-done.5.other), custom_call_target="tpu_custom_call" | custom-call | bytes 4194304 | tf_op jit(solution)/shard_map/place_halves/pallas_call | solution.py:422
  114.3 1.8 %finish.1 = (f32[64,2560]{1,0:T(8,128)}, f32[4,64,128]{2,1,0:T(8,128)}) custom-call(s32[2]{0:T(128)S(1)} %pad_add_fusion.place, bf16[64,16,128]{2,1,0:T(8,128)(2,1)S(1)} %all-to-all-done.2.gathered, bf16[64,16,128]{2,1,0:T(8,128)(2,1)S(1)} %collective-permute-done.6.swapped), custom_call_target="tpu_custom_call" | custom-call | tf_op jit(solution)/shard_map/finish/pallas_call | solution.py:487
  (12 shorter events, 0.1 us)
Async XLA Ops:
  2.6 11.5 %copy-start = (s32[1,1,16]{2,1,0:T(1,128)S(1)}, s32[1,1,16]{2,1,0:T(1,128)}, u32[]{:S(2)}) copy-start(s32[1,1,16]{2,1,0:T(1,128)} %param.14) | copy-start | bytes 196
  2.6 11.5 %copy-start.1 = (s32[1,1,16]{2,1,0:T(1,128)S(1)}, s32[1,1,16]{2,1,0:T(1,128)}, u32[]{:S(2)}) copy-start(s32[1,1,16]{2,1,0:T(1,128)} %param.15) | copy-start | bytes 196
  2.6 11.5 %collective-permute-start = (bf16[128,5248]{1,0:T(8,128)(2,1)S(1)}, bf16[128,5248]{1,0:T(8,128)(2,1)S(1)}, u32[]{:S(2)}, u32[]{:S(2)}) collective-permute-start(bf16[128,5248]{1,0:T(8,128)(2,1)S(1)} %take_far.1), channel_id=1, source_target_pairs={{0,8},{8,0},{1,9},{9,1},{2,10},{10,2},{3,11},{11,3},{4,12},{12,4},... | collective-permute-start | bytes 4030472 | tf_op jit(solution)/shard_map/ppermute | solution.py:518
  14.1 19.5 %copy-start.2 = (bf16[1,4,128,64]{2,3,1,0:T(8,128)(2,1)S(1)}, bf16[1,4,128,64]{2,3,1,0:T(8,128)(2,1)}, u32[]{:S(2)}) copy-start(bf16[1,4,128,64]{2,3,1,0:T(8,128)(2,1)} %param.16) | copy-start | bytes 196612
  14.9 18.7 %collective-permute-start.2 = (bf16[128,2688]{1,0:T(8,128)(2,1)S(1)}, bf16[128,2688]{1,0:T(8,128)(2,1)S(1)}, u32[]{:S(2)}, u32[]{:S(2)}) collective-permute-start(bf16[128,2688]{1,0:T(8,128)(2,1)S(1)} %get-tuple-element.20), channel_id=1, source_target_pairs={{16,0},{32,16},{48,32},{64,48},{80,64},{96,80},{112,96},{128,112},... | collective-permute-start | bytes 2064392 | tf_op jit(solution)/shard_map/ppermute | solution.py:522
  16.2 17.4 %collective-permute-start.1 = (bf16[128,2560]{1,0:T(8,128)(2,1)S(1)}, bf16[128,2560]{1,0:T(8,128)(2,1)S(1)}, u32[]{:S(2)}, u32[]{:S(2)}) collective-permute-start(bf16[128,2560]{1,0:T(8,128)(2,1)S(1)} %get-tuple-element.19), channel_id=1, source_target_pairs={{0,16},{16,32},{32,48},{48,64},{64,80},{80,96},{96,112},{112,128},... | collective-permute-start | bytes 1966088 | tf_op jit(solution)/shard_map/ppermute | solution.py:521
  47.3 25.8 %all-to-all-start = ((bf16[64,16,128]{2,1,0:T(8,128)(2,1)}), bf16[64,16,128]{2,1,0:T(8,128)(2,1)S(1)}, u32[]{:S(2)}, u32[]{:S(2)}) async-start(bf16[64,16,128]{2,1,0:T(8,128)(2,1)} %get-tuple-element.31), calls=%async_computation | async-start | bytes 524288 | tf_op jit(solution)/shard_map/all_to_all | solution.py:529
  60.5 34.3 %collective-permute-start.3 = (bf16[4,128,640]{2,1,0:T(8,128)(2,1)}, bf16[4,128,640]{2,1,0:T(8,128)(2,1)S(1)}, u32[]{:S(2)}, u32[]{:S(2)}) collective-permute-start(bf16[4,128,640]{2,1,0:T(8,128)(2,1)} %get-tuple-element.25), channel_id=1, source_target_pairs={{16,0},{32,16},{48,32},{64,48},{80,64},{96,80},{112,96},{128,112},... | collective-permute-start | bytes 1966088 | tf_op jit(solution)/shard_map/ppermute | solution.py:531
  61.8 33.0 %collective-permute-start.4 = (bf16[2,128,640]{2,1,0:T(8,128)(2,1)}, bf16[2,128,640]{2,1,0:T(8,128)(2,1)S(1)}, u32[]{:S(2)}, u32[]{:S(2)}) collective-permute-start(bf16[2,128,640]{2,1,0:T(8,128)(2,1)} %get-tuple-element.26), channel_id=1, source_target_pairs={{0,16},{16,32},{32,48},{48,64},{64,80},{80,96},{96,112},{112,128},... | collective-permute-start | bytes 983048 | tf_op jit(solution)/shard_map/ppermute | solution.py:532
  83.5 24.1 %all-to-all-start.2 = ((bf16[64,16,128]{2,1,0:T(8,128)(2,1)}), bf16[64,16,128]{2,1,0:T(8,128)(2,1)S(1)}, u32[]{:S(2)}, u32[]{:S(2)}) async-start(bf16[64,16,128]{2,1,0:T(8,128)(2,1)} %second_sum.1), calls=%async_computation.2 | async-start | bytes 524288 | tf_op jit(solution)/shard_map/all_to_all | solution.py:533
  97.3 15.3 %collective-permute-start.5 = (bf16[2,128,1280]{2,1,0:T(8,128)(2,1)S(1)}, bf16[2,128,1280]{2,1,0:T(8,128)(2,1)S(1)}, u32[]{:S(2)}, u32[]{:S(2)}) collective-permute-start(bf16[2,128,1280]{2,1,0:T(8,128)(2,1)S(1)} %get-tuple-element.28), channel_id=1, source_target_pairs={{0,8},{8,0},{1,9},{9,1},{2,10},{10,2},{3,11},{11,3},{4,12},{12,4},... | collective-permute-start | bytes 1966088 | tf_op jit(solution)/shard_map/ppermute | solution.py:538
  107.6 6.7 %collective-permute-start.6 = (bf16[64,16,128]{2,1,0:T(8,128)(2,1)S(1)}, bf16[64,16,128]{2,1,0:T(8,128)(2,1)S(1)}, u32[]{:S(2)}, u32[]{:S(2)}) collective-permute-start(bf16[64,16,128]{2,1,0:T(8,128)(2,1)S(1)} %all-to-all-done.2.gathered), channel_id=1, source_target_pairs={{0,8},{8,0},{1,9},{9,1},{2,10},{10,2},{3,11},{11,3},{4,12},{12,4},... | collective-permute-start | bytes 786440 | tf_op jit(solution)/shard_map/ppermute | solution.py:534

commit v6 on v5

--- a/solution.py
+++ b/solution.py
@@ -431,43 +431,40 @@
     )(place, mine, other)
 
 
-def first_sum_kernel(nz, ny, pieces, out):
-    for y in range(ny):
-        total = functools.reduce(jnp.add, [pieces[z * ny + y].astype(F32) for z in range(nz)]).astype(BF16)
-        for n in range(out.shape[0]):
-            out[n, y] = total
-
-
-def first_sum(pieces, nz, ny, peers):
-    return pl.pallas_call(
-        functools.partial(first_sum_kernel, nz, ny),
+def first_sum_kernel(pieces, out):
+    total = functools.reduce(jnp.add, [pieces[n].astype(F32) for n in range(pieces.shape[0])]).astype(BF16)
+    for n in range(out.shape[0]):
+        out[n] = total
+
+
+def first_sum(pieces, peers):
+    return pl.pallas_call(
+        first_sum_kernel,
         in_specs=[vmem()],
         out_specs=vmem(),
-        out_shape=pltpu.VMEM((peers, ny, ROWS, HEAD), BF16),
+        out_shape=pltpu.VMEM((peers,) + pieces.shape[1:], BF16),
         compiler_params=pltpu.CompilerParams(vmem_limit_bytes=2 * MIB),
         name="first_sum",
     )(pieces)
 
 
-def second_sum_kernel(nz, ny, up_rows, pieces, out):
-    totals = [functools.reduce(jnp.add, [pieces[n, y].astype(F32) for n in range(pieces.shape[0])]) for y in range(ny)]
-    everything = functools.reduce(jnp.add, totals)
-    is_up = lax.broadcasted_iota(jnp.int32, (ROWS, HEAD), 0) < up_rows
-    for y in range(ny):
-        message = jnp.where(is_up, everything, totals[y]).astype(BF16)
-        for z in range(nz):
-            out[z * ny + y] = message
-
-
-def second_sum(pieces, nz, ny, up_rows):
-    return pl.pallas_call(
-        functools.partial(second_sum_kernel, nz, ny, up_rows),
-        in_specs=[vmem()],
+def second_sum_kernel(up_rows, where, pieces, out):
+    everything = functools.reduce(jnp.add, [pieces[n].astype(F32) for n in range(pieces.shape[0])])
+    is_up = lax.broadcasted_iota(jnp.int32, everything.shape, 0) % ROWS < up_rows
+    message = jnp.where(is_up, everything, pieces[where[0]].astype(F32)).astype(BF16)
+    for n in range(out.shape[0]):
+        out[n] = message
+
+
+def second_sum(where, pieces, peers, up_rows):
+    return pl.pallas_call(
+        functools.partial(second_sum_kernel, up_rows),
+        in_specs=[smem(), vmem()],
         out_specs=vmem(),
-        out_shape=pltpu.VMEM((nz * ny, ROWS, HEAD), BF16),
+        out_shape=pltpu.VMEM((peers,) + pieces.shape[1:], BF16),
         compiler_params=pltpu.CompilerParams(vmem_limit_bytes=2 * MIB),
         name="second_sum",
-    )(pieces)
+    )(where, pieces)
 
 
 def finish_kernel(heads, place, gathered, swapped, up_grad, adapter_grad, one, two):
@@ -524,14 +521,17 @@
     payload, sum_a, sum_b, ret_down, ret_up = attend(scalars, table, near, oth, below, above, up_proj)
     ret_down, ret_up = hold(ret_down, ret_up)
 
-    plane, line = ("z", "y"), ("dp", "x")
-    peers = lax.axis_size("dp") * lax.axis_size("x")
-    pieces = lax.all_to_all(payload, plane, 0, 0, tiled=True)
-    pieces = lax.all_to_all(first_sum(pieces, nz, ny, peers), line, 0, 0, tiled=True)
+    plane = ("dp", "x", "z")
+    peers = lax.axis_size(plane)
+    share = (peers, RANK // peers * ROWS, HEAD)
+    pieces = lax.all_to_all(payload.reshape(share), plane, 0, 0, tiled=True)
+    pieces = lax.all_to_all(first_sum(pieces, ny), "y", 0, 0, tiled=True)
+    row = lax.axis_index("y").astype(jnp.int32).reshape(1)
+    message = second_sum(row, pieces, peers, heads // 2)
+    gathered = lax.all_to_all(message, plane, 0, 0, tiled=True).reshape(RANK, ROWS, HEAD)
+    swapped = lax.ppermute(gathered, "core", swap)
     from_above = lax.ppermute(ret_down, chain, downward)
     from_below = lax.ppermute(ret_up, chain, upward)
-    gathered = lax.all_to_all(second_sum(pieces, nz, ny, heads // 2), plane, 0, 0, tiled=True)
-    swapped = lax.ppermute(gathered, "core", swap)
     up_total, adapter_total = finish(place, gathered, swapped, heads)
     adapter_total = jnp.swapaxes(adapter_total, 1, 2)
     mine, theirs = join(scalars, sum_a, sum_b, from_above, from_below)

time: 117 us -> 111 us (0.949)
  blocking collectives: 9.62 us -> 0 us
  starting transfers between devices: 51.7 us -> 57.8 us
  waiting for transfers between devices: 29 us -> 25.9 us
    all_to_all x1 -> x0, blocking collectives: 9.62 us -> none  [local(): lax.all_to_all(first_sum(pieces, nz, ny, peers), line, 0, 0, tiled=True)]
    ppermute x1, starting transfers between devices: 2.78 us -> 7.11 us  [local(): lax.ppermute(theirs, 'core', swap)]
    ppermute x1, starting transfers between devices: 5 us -> 8.15 us  [local(): swapped = lax.ppermute(gathered, 'core', swap)]
    all_to_all x2 -> x3, waiting for transfers between devices: 14.8 us -> 11.7 us  [the longest x1 7.23 us: local(): pieces = lax.all_to_all(first_sum(pieces, ny), 'y', 0, 0, tiled=True)]
    all_to_all x2 -> x3, starting transfers between devices: 24.5 us -> 23.2 us  [the longest x1 10.7 us: local(): pieces = lax.all_to_all(payload.reshape(share), plane, 0, 0, tiled=True)]
  transfers between devices with their start and end apart: 9 -> 10, of which waited for: 4 -> 5; matrix products, arithmetic and copies ran while one was open for 0% -> 0% of each run, Pallas kernels for 6% -> 7%
where the time goes in v6:
time: 111 us; the launch traced here: 110 us
  starting transfers between devices  57.8 us (52%)
  waiting for transfers between devices  25.9 us (23%)
  Pallas kernels  25.5 us (23%)
    pallas_call x1, Pallas kernels, attend(): pl.pallas_call(functools.partial(attend_kernel, scalars[1].shape[0]), in_...  13.7 us
    ppermute x1, waiting for transfers between devices, local(): below = lax.ppermute(up_msg, chain, upward)  13.4 us
    all_to_all x1, starting transfers between devices, local(): pieces = lax.all_to_all(payload.reshape(share), plane, 0, 0, tiled=True)  10.7 us
    ppermute x1, starting transfers between devices, local(): oth = lax.ppermute(take_half(place, own, act, True), 'core', swap)  8.79 us
    ppermute x1, starting transfers between devices, local(): swapped = lax.ppermute(gathered, 'core', swap)  8.15 us
    all_to_all x1, waiting for transfers between devices, local(): pieces = lax.all_to_all(first_sum(pieces, ny), 'y', 0, 0, tiled=True)  7.23 us
    ppermute x1, starting transfers between devices, local(): lax.ppermute(theirs, 'core', swap)  7.11 us
    all_to_all x1, starting transfers between devices, local(): pieces = lax.all_to_all(first_sum(pieces, ny), 'y', 0, 0, tiled=True)  6.81 us
  transfers between devices with their start and end apart: 10, of which 5 were waited for; matrix products, arithmetic and copies ran while one was open for 0% of the time, Pallas kernels for 7%

profile of v6, /device:TPU:1, one launch (start us, length us, event | category | flops | bytes accessed | tf_op | source)
XLA Modules:
  0.0 110.2 jit_solution(11575693800948135076)
XLA Ops:
  0.7 1.9 %take_far.1 = bf16[128,5248]{1,0:T(8,128)(2,1)S(1)} custom-call(s32[2]{0:T(128)S(1)} %pad_add_fusion.place, bf16[128,2560]{1,0:T(8,128)(2,1)} %bitcast.29, bf16[128,2560]{1,0:T(8,128)(2,1)} %bitcast.31, bf16[128,2560]{1,0:T(8,128)(2,1)} %bitcast.33, bf16[128,2560]{1,0:T(8,128)(2,1)} %bitcast.35, bf16[128,128]{1,0:T(8,128)(2,1)} %bitcast.37), custom_call_target="tpu_custom_call" | custom-call | bytes 4194304 | tf_op jit(solution)/shard_map/take_far/pallas_call | solution.py:74
  2.6 8.8 %collective-permute-start = (bf16[128,5248]{1,0:T(8,128)(2,1)S(1)}, bf16[128,5248]{1,0:T(8,128)(2,1)S(1)}, u32[]{:S(2)}, u32[]{:S(2)}) collective-permute-start(bf16[128,5248]{1,0:T(8,128)(2,1)S(1)} %take_far.1), channel_id=1, source_target_pairs={{0,8},{8,0},{1,9},{9,1},{2,10},{10,2},{3,11},{11,3},{4,12},{12,4},... | collective-permute-start | bytes 4030472 | tf_op jit(solution)/shard_map/ppermute | solution.py:515
  11.4 1.9 %take_near.1.near = bf16[128,5248]{1,0:T(8,128)(2,1)S(1)} custom-call(s32[2]{0:T(128)S(1)} %pad_add_fusion.place, bf16[128,2560]{1,0:T(8,128)(2,1)} %bitcast.30, bf16[128,2560]{1,0:T(8,128)(2,1)} %bitcast.32, bf16[128,2560]{1,0:T(8,128)(2,1)} %bitcast.34, bf16[128,2560]{1,0:T(8,128)(2,1)} %bitcast.36, bf16[128,128]{1,0:T(8,128)(2,1)} %bitcast.38), custom_call_target="tpu_custom_call" | custom-call | bytes 4194304 | tf_op jit(solution)/shard_map/take_near/pallas_call | solution.py:74
  13.3 0.8 collective-permute-done.oth
  14.1 0.8 pack.1
  14.9 1.3 %collective-permute-start.2 = (bf16[128,2688]{1,0:T(8,128)(2,1)S(1)}, bf16[128,2688]{1,0:T(8,128)(2,1)S(1)}, u32[]{:S(2)}, u32[]{:S(2)}) collective-permute-start(bf16[128,2688]{1,0:T(8,128)(2,1)S(1)} %get-tuple-element.20), channel_id=1, source_target_pairs={{16,0},{32,16},{48,32},{64,48},{80,64},{96,80},{112,96},{128,112},... | collective-permute-start | bytes 2064392 | tf_op jit(solution)/shard_map/ppermute | solution.py:519
  16.2 4.0 %collective-permute-start.1 = (bf16[128,2560]{1,0:T(8,128)(2,1)S(1)}, bf16[128,2560]{1,0:T(8,128)(2,1)S(1)}, u32[]{:S(2)}, u32[]{:S(2)}) collective-permute-start(bf16[128,2560]{1,0:T(8,128)(2,1)S(1)} %get-tuple-element.19), channel_id=1, source_target_pairs={{0,16},{16,32},{32,48},{48,64},{64,80},{80,96},{96,112},{112,128},... | collective-permute-start | bytes 1966088 | tf_op jit(solution)/shard_map/ppermute | solution.py:518
  20.3 13.4 %collective-permute-done.1.below = bf16[128,2560]{1,0:T(8,128)(2,1)S(1)} collective-permute-done((bf16[128,2560]{1,0:T(8,128)(2,1)S(1)}, bf16[128,2560]{1,0:T(8,128)(2,1)S(1)}, u32[]{:S(2)}, u32[]{:S(2)}) %collective-permute-start.1) | collective-permute-done | bytes 655392 | tf_op jit(solution)/shard_map/ppermute | solution.py:518
  33.6 13.7 %attend.1 = (bf16[64,16,128]{2,1,0:T(8,128)(2,1)}, f32[2,2,128,640]{3,2,1,0:T(8,128)}, f32[2,2,128,640]{3,2,1,0:T(8,128)}, bf16[4,128,640]{2,1,0:T(8,128)(2,1)}, bf16[2,128,640]{2,1,0:T(8,128)(2,1)}) custom-call(s32[2]{0:T(128)S(1)} %pad_add_fusion.place, s32[16]{0:T(128)S(1)} %bitcast.23, s32[16]{0:T(128)S(1)} %bitcast.26, ...), custom_call_target="tpu_custom_call" | custom-call | flops 2013265920 | bytes 12582912 | tf_op jit(solution)/shard_map/attend/pallas_call | solution.py:317
  47.3 10.7 %all-to-all-start = ((bf16[32,32,128]{2,1,0:T(8,128)(2,1)}), bf16[32,32,128]{2,1,0:T(8,128)(2,1)S(1)}, u32[]{:S(2)}, u32[]{:S(2)}) async-start(bf16[32,32,128]{2,1,0:T(8,128)(2,1)} %bitcast.14), calls=%async_computation | async-start | bytes 524288 | tf_op jit(solution)/shard_map/all_to_all | solution.py:527
  58.0 1.3 %collective-permute-start.3 = (bf16[4,128,640]{2,1,0:T(8,128)(2,1)}, bf16[4,128,640]{2,1,0:T(8,128)(2,1)S(1)}, u32[]{:S(2)}, u32[]{:S(2)}) collective-permute-start(bf16[4,128,640]{2,1,0:T(8,128)(2,1)} %get-tuple-element.25), channel_id=1, source_target_pairs={{16,0},{32,16},{48,32},{64,48},{80,64},{96,80},{112,96},{128,112},... | collective-permute-start | bytes 1966088 | tf_op jit(solution)/shard_map/ppermute | solution.py:533
  59.3 4.0 %collective-permute-start.4 = (bf16[2,128,640]{2,1,0:T(8,128)(2,1)}, bf16[2,128,640]{2,1,0:T(8,128)(2,1)S(1)}, u32[]{:S(2)}, u32[]{:S(2)}) collective-permute-start(bf16[2,128,640]{2,1,0:T(8,128)(2,1)} %get-tuple-element.26), channel_id=1, source_target_pairs={{0,16},{16,32},{32,48},{48,64},{64,80},{80,96},{96,112},{112,128},... | collective-permute-start | bytes 983048 | tf_op jit(solution)/shard_map/ppermute | solution.py:534
  63.3 4.3 %all-to-all-done.pieces = bf16[32,32,128]{2,1,0:T(8,128)(2,1)S(1)} async-done(((bf16[32,32,128]{2,1,0:T(8,128)(2,1)}), bf16[32,32,128]{2,1,0:T(8,128)(2,1)S(1)}, u32[]{:S(2)}, u32[]{:S(2)}) %all-to-all-start) | async-done | bytes 262176 | tf_op jit(solution)/shard_map/all_to_all | solution.py:527
  67.6 0.7 first_sum.1
  68.3 6.8 %all-to-all-start.1 = ((bf16[8,32,128]{2,1,0:T(8,128)(2,1)}), bf16[8,32,128]{2,1,0:T(8,128)(2,1)S(1)}, u32[]{:S(2)}, u32[]{:S(2)}) async-start(bf16[8,32,128]{2,1,0:T(8,128)(2,1)} %first_sum.1), calls=%async_computation.1 | async-start | bytes 131072 | tf_op jit(solution)/shard_map/all_to_all | solution.py:528
  75.1 7.2 %all-to-all-done.1.pieces = bf16[8,32,128]{2,1,0:T(8,128)(2,1)S(1)} async-done(((bf16[8,32,128]{2,1,0:T(8,128)(2,1)}), bf16[8,32,128]{2,1,0:T(8,128)(2,1)S(1)}, u32[]{:S(2)}, u32[]{:S(2)}) %all-to-all-start.1) | async-done | bytes 65568 | tf_op jit(solution)/shard_map/all_to_all | solution.py:528
  82.3 0.7 second_sum.1
  83.1 5.7 %all-to-all-start.2 = ((bf16[32,32,128]{2,1,0:T(8,128)(2,1)}), bf16[32,32,128]{2,1,0:T(8,128)(2,1)S(1)}, u32[]{:S(2)}, u32[]{:S(2)}) async-start(bf16[32,32,128]{2,1,0:T(8,128)(2,1)} %second_sum.1), calls=%async_computation.2 | async-start | bytes 524288 | tf_op jit(solution)/shard_map/all_to_all | solution.py:531
  88.8 2.5 %join.1 = (bf16[2,128,1280]{2,1,0:T(8,128)(2,1)S(1)}, bf16[2,128,1280]{2,1,0:T(8,128)(2,1)S(1)}) custom-call(s32[2]{0:T(128)S(1)} %pad_add_fusion.place, s32[16]{0:T(128)S(1)} %bitcast.24, s32[16]{0:T(128)S(1)} %bitcast.27, f32[2,2,128,640]{3,2,1,0:T(8,128)} %get-tuple-element.21.sum_a_hbm, f32[2,2,128,640]{3,2,1,0:T(8,128)} %get-tuple-element.22.sum_b_hbm, ...), custom_call_target="tpu_custom_call" | custom-call | flops 1048576 | bytes 6291456 | tf_op jit(solution)/shard_map/join/pallas_call | solution.py:393
  91.3 7.1 %collective-permute-start.5 = (bf16[2,128,1280]{2,1,0:T(8,128)(2,1)S(1)}, bf16[2,128,1280]{2,1,0:T(8,128)(2,1)S(1)}, u32[]{:S(2)}, u32[]{:S(2)}) collective-permute-start(bf16[2,128,1280]{2,1,0:T(8,128)(2,1)S(1)} %get-tuple-element.28), channel_id=1, source_target_pairs={{0,8},{8,0},{1,9},{9,1},{2,10},{10,2},{3,11},{11,3},{4,12},{12,4},... | collective-permute-start | bytes 1966088 | tf_op jit(solution)/shard_map/ppermute | solution.py:538
  98.4 0.1 all-to-all-done.2
  98.5 8.2 %collective-permute-start.6 = (bf16[64,16,128]{2,1,0:T(8,128)(2,1)S(1)}, bf16[64,16,128]{2,1,0:T(8,128)(2,1)S(1)}, u32[]{:S(2)}, u32[]{:S(2)}) collective-permute-start(bf16[64,16,128]{2,1,0:T(8,128)(2,1)S(1)} %bitcast.20), channel_id=1, source_target_pairs={{0,8},{8,0},{1,9},{9,1},{2,10},{10,2},{3,11},{11,3},{4,12},{12,4},... | collective-permute-start | bytes 786440 | tf_op jit(solution)/shard_map/ppermute | solution.py:532
  106.7 1.6 %place_halves.1 = (bf16[128,2560]{1,0:T(8,128)(2,1)}, bf16[128,2560]{1,0:T(8,128)(2,1)}) custom-call(s32[2]{0:T(128)S(1)} %pad_add_fusion.place, bf16[2,128,1280]{2,1,0:T(8,128)(2,1)S(1)} %get-tuple-element.27.mine, bf16[2,128,1280]{2,1,0:T(8,128)(2,1)S(1)} %collective-permute-done.5.other), custom_call_target="tpu_custom_call" | custom-call | bytes 4194304 | tf_op jit(solution)/shard_map/place_halves/pallas_call | solution.py:422
  108.4 1.8 %finish.1 = (f32[64,2560]{1,0:T(8,128)}, f32[4,64,128]{2,1,0:T(8,128)}) custom-call(s32[2]{0:T(128)S(1)} %pad_add_fusion.place, bf16[64,16,128]{2,1,0:T(8,128)(2,1)S(1)} %bitcast.21, bf16[64,16,128]{2,1,0:T(8,128)(2,1)S(1)} %collective-permute-done.6.swapped), custom_call_target="tpu_custom_call" | custom-call | tf_op jit(solution)/shard_map/finish/pallas_call | solution.py:484
  (13 shorter events, 0.1 us)
Async XLA Ops:
  2.6 11.5 %copy-start = (s32[1,1,16]{2,1,0:T(1,128)S(1)}, s32[1,1,16]{2,1,0:T(1,128)}, u32[]{:S(2)}) copy-start(s32[1,1,16]{2,1,0:T(1,128)} %param.14) | copy-start | bytes 196
  2.6 11.5 %copy-start.1 = (s32[1,1,16]{2,1,0:T(1,128)S(1)}, s32[1,1,16]{2,1,0:T(1,128)}, u32[]{:S(2)}) copy-start(s32[1,1,16]{2,1,0:T(1,128)} %param.15) | copy-start | bytes 196
  2.6 11.5 %collective-permute-start = (bf16[128,5248]{1,0:T(8,128)(2,1)S(1)}, bf16[128,5248]{1,0:T(8,128)(2,1)S(1)}, u32[]{:S(2)}, u32[]{:S(2)}) collective-permute-start(bf16[128,5248]{1,0:T(8,128)(2,1)S(1)} %take_far.1), channel_id=1, source_target_pairs={{0,8},{8,0},{1,9},{9,1},{2,10},{10,2},{3,11},{11,3},{4,12},{12,4},... | collective-permute-start | bytes 4030472 | tf_op jit(solution)/shard_map/ppermute | solution.py:515
  14.1 19.5 %copy-start.2 = (bf16[1,4,128,64]{2,3,1,0:T(8,128)(2,1)S(1)}, bf16[1,4,128,64]{2,3,1,0:T(8,128)(2,1)}, u32[]{:S(2)}) copy-start(bf16[1,4,128,64]{2,3,1,0:T(8,128)(2,1)} %param.16) | copy-start | bytes 196612
  14.9 18.7 %collective-permute-start.2 = (bf16[128,2688]{1,0:T(8,128)(2,1)S(1)}, bf16[128,2688]{1,0:T(8,128)(2,1)S(1)}, u32[]{:S(2)}, u32[]{:S(2)}) collective-permute-start(bf16[128,2688]{1,0:T(8,128)(2,1)S(1)} %get-tuple-element.20), channel_id=1, source_target_pairs={{16,0},{32,16},{48,32},{64,48},{80,64},{96,80},{112,96},{128,112},... | collective-permute-start | bytes 2064392 | tf_op jit(solution)/shard_map/ppermute | solution.py:519
  16.2 17.4 %collective-permute-start.1 = (bf16[128,2560]{1,0:T(8,128)(2,1)S(1)}, bf16[128,2560]{1,0:T(8,128)(2,1)S(1)}, u32[]{:S(2)}, u32[]{:S(2)}) collective-permute-start(bf16[128,2560]{1,0:T(8,128)(2,1)S(1)} %get-tuple-element.19), channel_id=1, source_target_pairs={{0,16},{16,32},{32,48},{48,64},{64,80},{80,96},{96,112},{112,128},... | collective-permute-start | bytes 1966088 | tf_op jit(solution)/shard_map/ppermute | solution.py:518
  47.3 20.3 %all-to-all-start = ((bf16[32,32,128]{2,1,0:T(8,128)(2,1)}), bf16[32,32,128]{2,1,0:T(8,128)(2,1)S(1)}, u32[]{:S(2)}, u32[]{:S(2)}) async-start(bf16[32,32,128]{2,1,0:T(8,128)(2,1)} %bitcast.14), calls=%async_computation | async-start | bytes 524288 | tf_op jit(solution)/shard_map/all_to_all | solution.py:527
  58.0 30.8 %collective-permute-start.3 = (bf16[4,128,640]{2,1,0:T(8,128)(2,1)}, bf16[4,128,640]{2,1,0:T(8,128)(2,1)S(1)}, u32[]{:S(2)}, u32[]{:S(2)}) collective-permute-start(bf16[4,128,640]{2,1,0:T(8,128)(2,1)} %get-tuple-element.25), channel_id=1, source_target_pairs={{16,0},{32,16},{48,32},{64,48},{80,64},{96,80},{112,96},{128,112},... | collective-permute-start | bytes 1966088 | tf_op jit(solution)/shard_map/ppermute | solution.py:533
  59.3 29.5 %collective-permute-start.4 = (bf16[2,128,640]{2,1,0:T(8,128)(2,1)}, bf16[2,128,640]{2,1,0:T(8,128)(2,1)S(1)}, u32[]{:S(2)}, u32[]{:S(2)}) collective-permute-start(bf16[2,128,640]{2,1,0:T(8,128)(2,1)} %get-tuple-element.26), channel_id=1, source_target_pairs={{0,16},{16,32},{32,48},{48,64},{64,80},{80,96},{96,112},{112,128},... | collective-permute-start | bytes 983048 | tf_op jit(solution)/shard_map/ppermute | solution.py:534
  68.3 14.0 %all-to-all-start.1 = ((bf16[8,32,128]{2,1,0:T(8,128)(2,1)}), bf16[8,32,128]{2,1,0:T(8,128)(2,1)S(1)}, u32[]{:S(2)}, u32[]{:S(2)}) async-start(bf16[8,32,128]{2,1,0:T(8,128)(2,1)} %first_sum.1), calls=%async_computation.1 | async-start | bytes 131072 | tf_op jit(solution)/shard_map/all_to_all | solution.py:528
  83.1 15.5 %all-to-all-start.2 = ((bf16[32,32,128]{2,1,0:T(8,128)(2,1)}), bf16[32,32,128]{2,1,0:T(8,128)(2,1)S(1)}, u32[]{:S(2)}, u32[]{:S(2)}) async-start(bf16[32,32,128]{2,1,0:T(8,128)(2,1)} %second_sum.1), calls=%async_computation.2 | async-start | bytes 524288 | tf_op jit(solution)/shard_map/all_to_all | solution.py:531
  91.3 15.4 %collective-permute-start.5 = (bf16[2,128,1280]{2,1,0:T(8,128)(2,1)S(1)}, bf16[2,128,1280]{2,1,0:T(8,128)(2,1)S(1)}, u32[]{:S(2)}, u32[]{:S(2)}) collective-permute-start(bf16[2,128,1280]{2,1,0:T(8,128)(2,1)S(1)} %get-tuple-element.28), channel_id=1, source_target_pairs={{0,8},{8,0},{1,9},{9,1},{2,10},{10,2},{3,11},{11,3},{4,12},{12,4},... | collective-permute-start | bytes 1966088 | tf_op jit(solution)/shard_map/ppermute | solution.py:538
  98.5 9.8 %collective-permute-start.6 = (bf16[64,16,128]{2,1,0:T(8,128)(2,1)S(1)}, bf16[64,16,128]{2,1,0:T(8,128)(2,1)S(1)}, u32[]{:S(2)}, u32[]{:S(2)}) collective-permute-start(bf16[64,16,128]{2,1,0:T(8,128)(2,1)S(1)} %bitcast.20), channel_id=1, source_target_pairs={{0,8},{8,0},{1,9},{9,1},{2,10},{10,2},{3,11},{11,3},{4,12},{12,4},... | collective-permute-start | bytes 786440 | tf_op jit(solution)/shard_map/ppermute | solution.py:532

commit v7 on v6

--- a/solution.py
+++ b/solution.py
@@ -193,56 +193,112 @@
         self.scale_n = jnp.where(self.wide_above, 1.0, 0.0).astype(F32)
 
 
-def shifts(view, masks, adapters, adapted, adapted_t):
-    for n, (act, robot) in enumerate(zip(view.actions(), masks.robots)):
-        table = adapters[robot]
-        adapted[n * TOK:(n + 1) * TOK, :] = dot(act, table, 1, 1).astype(BF16)
-        if adapted_t is not None:
-            adapted_t[:, n * TOK:(n + 1) * TOK] = dot(table, act, 1, 1).astype(BF16)
-
-
-def narrow_head(view, masks, adapted, up_h, j):
+def shift_of(act, robot, adapters, adapted, adapted_t, n):
+    table = adapters[robot]
+    adapted[n * TOK:(n + 1) * TOK, :] = dot(act, table, 1, 1).astype(BF16)
+    adapted_t[:, n * TOK:(n + 1) * TOK] = dot(table, act, 1, 1).astype(BF16)
+
+
+def own_kernel(
+    clips, place, lengths, robots, adapters, near, oth, up_hbm,
+    adapted, adapted_t, queries, raws, prods, up, sem,
+):
+    view = Views(place, near, oth, None, None)
+    half, quarter = view.half, view.quarter
+    load = pltpu.make_async_copy(
+        up_hbm.at[:, pl.ds(pl.multiple_of(place[0] * half, HEAD), half)], up, sem.at[0]
+    )
+    load.start()
+    masks = Masks(clips, place, lengths, robots)
+    acts = view.pair(near[:, 4 * half:], oth[:, 4 * half:])
+    for n in range(2):
+        shift_of(acts[n], masks.robots[n], adapters, adapted, adapted_t, n)
+    load.wait()
+    for j in range(quarter // HEAD):
+        for group in range(2):
+            at = group * quarter + j * HEAD
+            shift = dot(adapted[...], up[:, at:at + HEAD], 1, 0)
+            query = (column(view.both(0, group, j)).astype(F32) + shift).astype(BF16)
+            queries[j, group] = query
+            grad = column(view.both(1, group, j))
+            for out, pair, rows in ((raws, view.both(2, group, j), query), (prods, view.both(3, group, j), grad)):
+                out[j, group, :, : 2 * TOK] = dot(pair[0], rows, 1, 1)
+                out[j, group, :, 2 * TOK:] = dot(pair[1], rows[TOK:], 1, 1)
+
+
+def own_scores(scalars, adapters, near, oth, up):
+    half = up.shape[1] // 2
+    five = half // 2 // HEAD
+    return pl.pallas_call(
+        functools.partial(own_kernel, scalars[1].shape[0]),
+        in_specs=[smem()] * 3 + [vmem()] * 3 + [hbm()],
+        out_specs=[vmem()] * 5,
+        out_shape=[
+            pltpu.VMEM((2 * TOK, RANK), BF16), pltpu.VMEM((RANK, 2 * TOK), BF16),
+            pltpu.VMEM((five, 2, 2 * TOK, HEAD), BF16),
+            pltpu.VMEM((five, 2, TOK, 3 * TOK), F32), pltpu.VMEM((five, 2, TOK, 3 * TOK), F32),
+        ],
+        scratch_shapes=[pltpu.VMEM((RANK, half), BF16), pltpu.SemaphoreType.DMA((1,))],
+        compiler_params=pltpu.CompilerParams(vmem_limit_bytes=12 * MIB),
+        cost_estimate=pl.CostEstimate(
+            flops=2 * five * 6 * 512 * 256 * 128, bytes_accessed=4 * MIB, transcendentals=0
+        ),
+        name="own_scores",
+    )(*scalars, adapters, near, oth, fixed(up))
+
+
+def narrow_head(view, masks, queries, raws, prods, j):
     none = jnp.zeros((TOK, TOK), BF16)
-    shift = dot(adapted[: 2 * TOK], up_h, 1, 0)
-    query = (column(view.both(0, 0, j)).astype(F32) + shift).astype(BF16)
+    query = queries[j, 0]
     grad = column(view.both(1, 0, j))
     keys = column([view.lower(2, j), view.lower(0, j)] + view.both(2, 0, j))
-    values = column([view.lower(3, j), view.lower(1, j)] + view.both(3, 0, j))
-    raw = dot(keys, query, 1, 1)
-    prod = dot(values, grad, 1, 1)
-    prob_a, dscore_a = soften([block(raw, i, 0) for i in range(3)], [block(prod, i, 0) for i in range(3)], masks.a)
-    prob_b, dscore_b = soften([block(raw, i, 1) for i in range(1, 4)], [block(prod, i, 1) for i in range(1, 4)], masks.b)
+
+    def blocks(p0, p1, rows, own):
+        far = dot(p1, rows, 1, 1)
+        near = own[j, 0]
+        row_a = [dot(p0, rows[:TOK], 1, 1), far[:, :TOK], near[:, :TOK]]
+        return row_a, [far[:, TOK:], near[:, TOK:2 * TOK], near[:, 2 * TOK:]]
+
+    raw_a, raw_b = blocks(view.lower(2, j), view.lower(0, j), query, raws)
+    prod_a, prod_b = blocks(view.lower(3, j), view.lower(1, j), grad, prods)
+    prob_a, dscore_a = soften(raw_a, prod_a, masks.a)
+    prob_b, dscore_b = soften(raw_b, prod_b, masks.b)
     prob = jnp.concatenate([column(prob_a + [none]), column([none] + prob_b)], 1)
     dscore = jnp.concatenate([column(dscore_a + [none]), column([none] + dscore_b)], 1)
     return query, grad, keys, prob, dscore
 
 
-def wide_head(view, masks, adapted, up_h, j):
+def wide_head(view, masks, queries, raws, prods, adapted_n, up_h, j):
     none = jnp.zeros((TOK, TOK), BF16)
-    shift = dot(adapted[...], up_h, 1, 0)
-    query = (column(view.both(0, 1, j) + [view.upper(0, j)]).astype(F32) + shift).astype(BF16)
-    grad = column(view.both(1, 1, j) + [view.upper(1, j)])
+    query = queries[j, 1]
+    query_n = (view.upper(0, j).astype(F32) + dot(adapted_n, up_h, 1, 0)).astype(BF16)
+    grad = column(view.both(1, 1, j))
+    grad_n = view.upper(1, j)
     keys = column([view.lower(2, j)] + view.both(2, 1, j) + [view.upper(2, j)])
-    values = column([view.lower(3, j)] + view.both(3, 1, j) + [view.upper(3, j)])
-    raw = dot(keys[: 3 * TOK], query[: 2 * TOK], 1, 1)
-    prod = dot(values[: 3 * TOK], grad[: 2 * TOK], 1, 1)
-    raw_n = dot(keys[TOK:], query[2 * TOK:], 1, 1)
-    prod_n = dot(values[TOK:], grad[2 * TOK:], 1, 1)
-    prob_a, dscore_a = soften(
-        [block(raw, i, 0) for i in range(2)], [block(prod, i, 0) for i in range(2)], masks.a[1:], masks.scale_a
-    )
-    prob_b, dscore_b = soften([block(raw, i, 1) for i in range(3)], [block(prod, i, 1) for i in range(3)], masks.b)
+    values = column(view.both(3, 1, j) + [view.upper(3, j)])
+
+    def blocks(p1, rows, own):
+        far = dot(p1, rows, 1, 1)
+        near = own[j, 1]
+        return [far[:, :TOK], near[:, :TOK]], [far[:, TOK:], near[:, TOK:2 * TOK], near[:, 2 * TOK:]]
+
+    raw_a, raw_b = blocks(view.lower(2, j), query, raws)
+    prod_a, prod_b = blocks(view.lower(3, j), grad, prods)
+    raw_n = dot(keys[TOK:], query_n, 1, 1)
+    prod_n = dot(values, grad_n, 1, 1)
+    prob_a, dscore_a = soften(raw_a, prod_a, masks.a[1:], masks.scale_a)
+    prob_b, dscore_b = soften(raw_b, prod_b, masks.b)
     prob_n, dscore_n = soften(
         [block(raw_n, i, 0) for i in range(3)], [block(prod_n, i, 0) for i in range(3)], masks.n, masks.scale_n
     )
     prob = jnp.concatenate([column(prob_a + [none, none]), column(prob_b + [none]), column([none] + prob_n)], 1)
     dscore = jnp.concatenate([column(dscore_a + [none, none]), column(dscore_b + [none]), column([none] + dscore_n)], 1)
-    return query, grad, keys, prob, dscore
+    return column([query, query_n]), column([grad, grad_n]), keys, prob, dscore
 
 
 def attend_kernel(
-    clips, place, lengths, robots, adapters, near, oth, below, above, up_hbm,
-    payload, sum_a, sum_b, ret_down, ret_up,
+    clips, place, lengths, robots, adapters, near, oth, below, above, adapted_own, adapted_own_t, queries, raws, prods,
+    up_hbm, payload, sum_a, sum_b, ret_down, ret_up,
     up, adapted, adapted_t, agrad_t, pay, keep_a, keep_b, keep_down, keep_up, sem_in, sem_out,
 ):
     view = Views(place, near, oth, below, above)
@@ -253,7 +309,9 @@
     )
     load.start()
     masks = Masks(clips, place, lengths, robots)
-    shifts(view, masks, adapters, adapted, adapted_t)
+    acts = view.actions()
+    adapted_t[:, : 2 * TOK] = adapted_own_t[...]
+    shift_of(acts[2], masks.robots[2], adapters, adapted, adapted_t, 2)
     agrad_t[...] = jnp.zeros_like(agrad_t)
     pay[:, 2 * five:, :] = jnp.zeros((RANK, ROWS - 2 * five, HEAD), F32)
     load.wait()
@@ -270,7 +328,7 @@
     for j in range(five):
         cols = slice(j * HEAD, (j + 1) * HEAD)
         up_h = up[:, cols]
-        query, grad, keys, prob, dscore = narrow_head(view, masks, adapted, up_h, j)
+        query, grad, keys, prob, dscore = narrow_head(view, masks, queries, raws, prods, j)
         sums(keys, dscore, up_h, 2 * TOK, j)
         wide_parts = []
         for n, part in enumerate((dot(dscore, query, 1, 0), dot(prob, grad, 1, 0))):
@@ -279,7 +337,7 @@
             keep_a[n, 0, :, cols] = part[2 * TOK:3 * TOK]
             keep_b[n, 0, :, cols] = part[3 * TOK:]
         up_h = up[:, quarter + j * HEAD:quarter + (j + 1) * HEAD]
-        query, grad, keys, prob, dscore = wide_head(view, masks, adapted, up_h, j)
+        query, grad, keys, prob, dscore = wide_head(view, masks, queries, raws, prods, adapted[2 * TOK:, :], up_h, j)
         sums(keys, dscore, up_h, 3 * TOK, five + j)
         for n, part in enumerate((dot(dscore, query, 1, 0), dot(prob, grad, 1, 0))):
             keep_down[2 + n, :, cols] = jnp.where(masks.wide_below, wide_parts[n], part[:TOK]).astype(BF16)
@@ -293,7 +351,7 @@
             stores[-1].start()
 
     terms = []
-    for n, act in enumerate(view.actions()):
+    for n, act in enumerate(acts):
         whole = agrad_t[:, n * TOK:(n + 1) * TOK]
         high = whole.astype(BF16)
         low = (whole - high.astype(F32)).astype(BF16)
@@ -308,7 +366,7 @@
         store.wait()
 
 
-def attend(scalars, adapters, near, oth, below, above, up):
+def attend(scalars, adapters, near, oth, below, above, stored, up):
     half = up.shape[1] // 2
     quarter = half // 2
     five = quarter // HEAD
@@ -316,7 +374,7 @@
     sums = ((2, 2, TOK, quarter), F32)
     return pl.pallas_call(
         functools.partial(attend_kernel, scalars[1].shape[0]),
-        in_specs=[smem()] * 3 + [vmem()] * 5 + [hbm()],
+        in_specs=[smem()] * 3 + [vmem()] * 10 + [hbm()],
         out_specs=[vmem()] + [hbm()] * 4,
         out_shape=[jax.ShapeDtypeStruct((RANK, ROWS, HEAD), BF16)] + [pltpu.HBM(*x) for x in (sums, sums, *shapes)],
         scratch_shapes=[
@@ -337,7 +395,7 @@
             flops=2 * five * 12 * 512 * 256 * 128, bytes_accessed=12 * MIB, transcendentals=five * 1024 * 256
         ),
         name="attend",
-    )(*scalars, adapters, near, oth, below, above, fixed(up))
+    )(*scalars, adapters, near, oth, below, above, *stored, fixed(up))
 
 
 def hold_kernel(down_in, up_in, down_out, up_out):
@@ -518,7 +576,10 @@
     below = lax.ppermute(up_msg, chain, upward)
     above = lax.ppermute(down_msg, chain, downward)
     table = jnp.swapaxes(adapters[0], 1, 2)
-    payload, sum_a, sum_b, ret_down, ret_up = attend(scalars, table, near, oth, below, above, up_proj)
+    stored = own_scores(scalars, table, near, oth, up_proj)
+    payload, sum_a, sum_b, ret_down, ret_up = attend(
+        scalars, table, near, oth, below, above, stored, up_proj
+    )
     ret_down, ret_up = hold(ret_down, ret_up)
 
     plane = ("dp", "x", "z")

time: 111 us -> 109 us (0.982)
  waiting for transfers between devices: 25.9 us -> 21.9 us
  Pallas kernels: 25.5 us -> 27.6 us
    ppermute x1, waiting for transfers between devices: 13.4 us -> 9.33 us  [local(): below = lax.ppermute(up_msg, chain, upward)]
    pallas_call x0 -> x1, Pallas kernels: none -> 4.02 us  [own_scores(): pl.pallas_call(functools.partial(own_kernel, scalars[1].shape[0]), in_spe...]
    pallas_call x1, Pallas kernels: 13.7 us -> 11.7 us  [attend(): pl.pallas_call(functools.partial(attend_kernel, scalars[1].shape[0]), in_...]
  transfers between devices with their start and end apart: 10 -> 10, of which waited for: 5 -> 5; matrix products, arithmetic and copies ran while one was open for 0% -> 0% of each run, Pallas kernels for 7% -> 11%
where the time goes in v7:
time: 109 us; the launch traced here: 108 us
  starting transfers between devices  57.8 us (53%)
  Pallas kernels  27.6 us (25%)
  waiting for transfers between devices  21.9 us (20%)
    pallas_call x1, Pallas kernels, attend(): pl.pallas_call(functools.partial(attend_kernel, scalars[1].shape[0]), in_...  11.7 us
    all_to_all x1, starting transfers between devices, local(): pieces = lax.all_to_all(payload.reshape(share), plane, 0, 0, tiled=True)  10.7 us
    ppermute x1, waiting for transfers between devices, local(): below = lax.ppermute(up_msg, chain, upward)  9.33 us
    ppermute x1, starting transfers between devices, local(): oth = lax.ppermute(take_half(place, own, act, True), 'core', swap)  8.79 us
    ppermute x1, starting transfers between devices, local(): swapped = lax.ppermute(gathered, 'core', swap)  8.15 us
    all_to_all x1, waiting for transfers between devices, local(): pieces = lax.all_to_all(first_sum(pieces, ny), 'y', 0, 0, tiled=True)  7.23 us
    ppermute x1, starting transfers between devices, local(): lax.ppermute(theirs, 'core', swap)  7.11 us
    all_to_all x1, starting transfers between devices, local(): pieces = lax.all_to_all(first_sum(pieces, ny), 'y', 0, 0, tiled=True)  6.82 us
  transfers between devices with their start and end apart: 10, of which 5 were waited for; matrix products, arithmetic and copies ran while one was open for 0% of the time, Pallas kernels for 11%

profile of v7, /device:TPU:1, one launch (start us, length us, event | category | flops | bytes accessed | tf_op | source)
XLA Modules:
  0.0 108.2 jit_solution(3744951744108100086)
XLA Ops:
  0.7 1.9 %take_far.1 = bf16[128,5248]{1,0:T(8,128)(2,1)S(1)} custom-call(s32[2]{0:T(128)S(1)} %pad_add_fusion.place, bf16[128,2560]{1,0:T(8,128)(2,1)} %bitcast.32, bf16[128,2560]{1,0:T(8,128)(2,1)} %bitcast.34, bf16[128,2560]{1,0:T(8,128)(2,1)} %bitcast.36, bf16[128,2560]{1,0:T(8,128)(2,1)} %bitcast.38, bf16[128,128]{1,0:T(8,128)(2,1)} %bitcast.40), custom_call_target="tpu_custom_call" | custom-call | bytes 4194304 | tf_op jit(solution)/shard_map/take_far/pallas_call | solution.py:74
  2.6 8.8 %collective-permute-start = (bf16[128,5248]{1,0:T(8,128)(2,1)S(1)}, bf16[128,5248]{1,0:T(8,128)(2,1)S(1)}, u32[]{:S(2)}, u32[]{:S(2)}) collective-permute-start(bf16[128,5248]{1,0:T(8,128)(2,1)S(1)} %take_far.1), channel_id=1, source_target_pairs={{0,8},{8,0},{1,9},{9,1},{2,10},{10,2},{3,11},{11,3},{4,12},{12,4},... | collective-permute-start | bytes 4030472 | tf_op jit(solution)/shard_map/ppermute | solution.py:573
  11.4 1.9 %take_near.1.near = bf16[128,5248]{1,0:T(8,128)(2,1)S(1)} custom-call(s32[2]{0:T(128)S(1)} %pad_add_fusion.place, bf16[128,2560]{1,0:T(8,128)(2,1)} %bitcast.33, bf16[128,2560]{1,0:T(8,128)(2,1)} %bitcast.35, bf16[128,2560]{1,0:T(8,128)(2,1)} %bitcast.37, bf16[128,2560]{1,0:T(8,128)(2,1)} %bitcast.39, bf16[128,128]{1,0:T(8,128)(2,1)} %bitcast.41), custom_call_target="tpu_custom_call" | custom-call | bytes 4194304 | tf_op jit(solution)/shard_map/take_near/pallas_call | solution.py:74
  13.3 0.8 collective-permute-done.oth
  14.1 0.8 pack.1
  14.9 1.3 %collective-permute-start.2 = (bf16[128,2688]{1,0:T(8,128)(2,1)S(1)}, bf16[128,2688]{1,0:T(8,128)(2,1)S(1)}, u32[]{:S(2)}, u32[]{:S(2)}) collective-permute-start(bf16[128,2688]{1,0:T(8,128)(2,1)S(1)} %get-tuple-element.25), channel_id=1, source_target_pairs={{16,0},{32,16},{48,32},{64,48},{80,64},{96,80},{112,96},{128,112},... | collective-permute-start | bytes 2064392 | tf_op jit(solution)/shard_map/ppermute | solution.py:577
  16.2 4.0 %collective-permute-start.1 = (bf16[128,2560]{1,0:T(8,128)(2,1)S(1)}, bf16[128,2560]{1,0:T(8,128)(2,1)S(1)}, u32[]{:S(2)}, u32[]{:S(2)}) collective-permute-start(bf16[128,2560]{1,0:T(8,128)(2,1)S(1)} %get-tuple-element.24), channel_id=1, source_target_pairs={{0,16},{16,32},{32,48},{48,64},{64,80},{80,96},{96,112},{112,128},... | collective-permute-start | bytes 1966088 | tf_op jit(solution)/shard_map/ppermute | solution.py:576
  20.3 4.0 %own_scores.1 = (bf16[256,64]{1,0:T(8,128)(2,1)S(1)}, bf16[64,256]{1,0:T(8,128)(2,1)S(1)}, bf16[5,2,256,128]{3,2,1,0:T(8,128)(2,1)S(1)}, f32[5,2,128,384]{3,2,1,0:T(8,128)S(1)}, f32[5,2,128,384]{3,2,1,0:T(8,128)S(1)}) custom-call(s32[2]{0:T(128)S(1)} %pad_add_fusion.place, s32[16]{0:T(128)S(1)} %bitcast.25, s32[16]{0:T(128)S(1)} %bitcast.29, ...), custom_call_target="tpu_custom_call" | custom-call | flops 1006632960 | bytes 4194304 | tf_op jit(solution)/shard_map/own_scores/pallas_call | solution.py:232
  24.3 9.3 %collective-permute-done.1.below = bf16[128,2560]{1,0:T(8,128)(2,1)S(1)} collective-permute-done((bf16[128,2560]{1,0:T(8,128)(2,1)S(1)}, bf16[128,2560]{1,0:T(8,128)(2,1)S(1)}, u32[]{:S(2)}, u32[]{:S(2)}) %collective-permute-start.1) | collective-permute-done | bytes 655392 | tf_op jit(solution)/shard_map/ppermute | solution.py:576
  33.6 11.7 %attend.1 = (bf16[64,16,128]{2,1,0:T(8,128)(2,1)}, f32[2,2,128,640]{3,2,1,0:T(8,128)}, f32[2,2,128,640]{3,2,1,0:T(8,128)}, bf16[4,128,640]{2,1,0:T(8,128)(2,1)}, bf16[2,128,640]{2,1,0:T(8,128)(2,1)}) custom-call(s32[2]{0:T(128)S(1)} %pad_add_fusion.place, s32[16]{0:T(128)S(1)} %bitcast.26, s32[16]{0:T(128)S(1)} %bitcast.30, ...), custom_call_target="tpu_custom_call" | custom-call | flops 2013265920 | bytes 12582912 | tf_op jit(solution)/shard_map/attend/pallas_call | solution.py:375
  45.3 10.7 %all-to-all-start = ((bf16[32,32,128]{2,1,0:T(8,128)(2,1)}), bf16[32,32,128]{2,1,0:T(8,128)(2,1)S(1)}, u32[]{:S(2)}, u32[]{:S(2)}) async-start(bf16[32,32,128]{2,1,0:T(8,128)(2,1)} %bitcast.15), calls=%async_computation | async-start | bytes 524288 | tf_op jit(solution)/shard_map/all_to_all | solution.py:588
  56.0 1.3 %collective-permute-start.3 = (bf16[4,128,640]{2,1,0:T(8,128)(2,1)}, bf16[4,128,640]{2,1,0:T(8,128)(2,1)S(1)}, u32[]{:S(2)}, u32[]{:S(2)}) collective-permute-start(bf16[4,128,640]{2,1,0:T(8,128)(2,1)} %get-tuple-element.35), channel_id=1, source_target_pairs={{16,0},{32,16},{48,32},{64,48},{80,64},{96,80},{112,96},{128,112},... | collective-permute-start | bytes 1966088 | tf_op jit(solution)/shard_map/ppermute | solution.py:594
  57.3 4.0 %collective-permute-start.4 = (bf16[2,128,640]{2,1,0:T(8,128)(2,1)}, bf16[2,128,640]{2,1,0:T(8,128)(2,1)S(1)}, u32[]{:S(2)}, u32[]{:S(2)}) collective-permute-start(bf16[2,128,640]{2,1,0:T(8,128)(2,1)} %get-tuple-element.36), channel_id=1, source_target_pairs={{0,16},{16,32},{32,48},{48,64},{64,80},{80,96},{96,112},{112,128},... | collective-permute-start | bytes 983048 | tf_op jit(solution)/shard_map/ppermute | solution.py:595
  61.3 4.3 %all-to-all-done.pieces = bf16[32,32,128]{2,1,0:T(8,128)(2,1)S(1)} async-done(((bf16[32,32,128]{2,1,0:T(8,128)(2,1)}), bf16[32,32,128]{2,1,0:T(8,128)(2,1)S(1)}, u32[]{:S(2)}, u32[]{:S(2)}) %all-to-all-start) | async-done | bytes 262176 | tf_op jit(solution)/shard_map/all_to_all | solution.py:588
  65.7 0.7 first_sum.1
  66.3 6.8 %all-to-all-start.1 = ((bf16[8,32,128]{2,1,0:T(8,128)(2,1)}), bf16[8,32,128]{2,1,0:T(8,128)(2,1)S(1)}, u32[]{:S(2)}, u32[]{:S(2)}) async-start(bf16[8,32,128]{2,1,0:T(8,128)(2,1)} %first_sum.1), calls=%async_computation.1 | async-start | bytes 131072 | tf_op jit(solution)/shard_map/all_to_all | solution.py:589
  73.2 7.2 %all-to-all-done.1.pieces = bf16[8,32,128]{2,1,0:T(8,128)(2,1)S(1)} async-done(((bf16[8,32,128]{2,1,0:T(8,128)(2,1)}), bf16[8,32,128]{2,1,0:T(8,128)(2,1)S(1)}, u32[]{:S(2)}, u32[]{:S(2)}) %all-to-all-start.1) | async-done | bytes 65568 | tf_op jit(solution)/shard_map/all_to_all | solution.py:589
  80.4 0.7 second_sum.1
  81.1 5.7 %all-to-all-start.2 = ((bf16[32,32,128]{2,1,0:T(8,128)(2,1)}), bf16[32,32,128]{2,1,0:T(8,128)(2,1)S(1)}, u32[]{:S(2)}, u32[]{:S(2)}) async-start(bf16[32,32,128]{2,1,0:T(8,128)(2,1)} %second_sum.1), calls=%async_computation.2 | async-start | bytes 524288 | tf_op jit(solution)/shard_map/all_to_all | solution.py:592
  86.9 2.5 %join.1 = (bf16[2,128,1280]{2,1,0:T(8,128)(2,1)S(1)}, bf16[2,128,1280]{2,1,0:T(8,128)(2,1)S(1)}) custom-call(s32[2]{0:T(128)S(1)} %pad_add_fusion.place, s32[16]{0:T(128)S(1)} %bitcast.27, s32[16]{0:T(128)S(1)} %bitcast.31, f32[2,2,128,640]{3,2,1,0:T(8,128)} %get-tuple-element.31.sum_a_hbm, f32[2,2,128,640]{3,2,1,0:T(8,128)} %get-tuple-element.32.sum_b_hbm, ...), custom_call_target="tpu_custom_call" | custom-call | flops 1048576 | bytes 6291456 | tf_op jit(solution)/shard_map/join/pallas_call | solution.py:451
  89.3 7.1 %collective-permute-start.5 = (bf16[2,128,1280]{2,1,0:T(8,128)(2,1)S(1)}, bf16[2,128,1280]{2,1,0:T(8,128)(2,1)S(1)}, u32[]{:S(2)}, u32[]{:S(2)}) collective-permute-start(bf16[2,128,1280]{2,1,0:T(8,128)(2,1)S(1)} %get-tuple-element.38), channel_id=1, source_target_pairs={{0,8},{8,0},{1,9},{9,1},{2,10},{10,2},{3,11},{11,3},{4,12},{12,4},... | collective-permute-start | bytes 1966088 | tf_op jit(solution)/shard_map/ppermute | solution.py:599
  96.6 8.1 %collective-permute-start.6 = (bf16[64,16,128]{2,1,0:T(8,128)(2,1)S(1)}, bf16[64,16,128]{2,1,0:T(8,128)(2,1)S(1)}, u32[]{:S(2)}, u32[]{:S(2)}) collective-permute-start(bf16[64,16,128]{2,1,0:T(8,128)(2,1)S(1)} %bitcast.20), channel_id=1, source_target_pairs={{0,8},{8,0},{1,9},{9,1},{2,10},{10,2},{3,11},{11,3},{4,12},{12,4},... | collective-permute-start | bytes 786440 | tf_op jit(solution)/shard_map/ppermute | solution.py:593
  104.8 1.6 %place_halves.1 = (bf16[128,2560]{1,0:T(8,128)(2,1)}, bf16[128,2560]{1,0:T(8,128)(2,1)}) custom-call(s32[2]{0:T(128)S(1)} %pad_add_fusion.place, bf16[2,128,1280]{2,1,0:T(8,128)(2,1)S(1)} %get-tuple-element.37.mine, bf16[2,128,1280]{2,1,0:T(8,128)(2,1)S(1)} %collective-permute-done.5.other), custom_call_target="tpu_custom_call" | custom-call | bytes 4194304 | tf_op jit(solution)/shard_map/place_halves/pallas_call | solution.py:480
  106.4 1.8 %finish.1 = (f32[64,2560]{1,0:T(8,128)}, f32[4,64,128]{2,1,0:T(8,128)}) custom-call(s32[2]{0:T(128)S(1)} %pad_add_fusion.place, bf16[64,16,128]{2,1,0:T(8,128)(2,1)S(1)} %bitcast.21, bf16[64,16,128]{2,1,0:T(8,128)(2,1)S(1)} %collective-permute-done.6.swapped), custom_call_target="tpu_custom_call" | custom-call | tf_op jit(solution)/shard_map/finish/pallas_call | solution.py:542
  (14 shorter events, 0.3 us)
Async XLA Ops:
  2.6 11.5 %copy-start.1 = (s32[1,1,16]{2,1,0:T(1,128)S(1)}, s32[1,1,16]{2,1,0:T(1,128)}, u32[]{:S(2)}) copy-start(s32[1,1,16]{2,1,0:T(1,128)} %param.14) | copy-start | bytes 196
  2.6 11.5 %copy-start.2 = (s32[1,1,16]{2,1,0:T(1,128)S(1)}, s32[1,1,16]{2,1,0:T(1,128)}, u32[]{:S(2)}) copy-start(s32[1,1,16]{2,1,0:T(1,128)} %param.15) | copy-start | bytes 196
  2.6 11.5 %collective-permute-start = (bf16[128,5248]{1,0:T(8,128)(2,1)S(1)}, bf16[128,5248]{1,0:T(8,128)(2,1)S(1)}, u32[]{:S(2)}, u32[]{:S(2)}) collective-permute-start(bf16[128,5248]{1,0:T(8,128)(2,1)S(1)} %take_far.1), channel_id=1, source_target_pairs={{0,8},{8,0},{1,9},{9,1},{2,10},{10,2},{3,11},{11,3},{4,12},{12,4},... | collective-permute-start | bytes 4030472 | tf_op jit(solution)/shard_map/ppermute | solution.py:573
  14.1 6.2 %copy-start = (bf16[1,4,128,64]{2,3,1,0:T(8,128)(2,1)S(1)}, bf16[1,4,128,64]{2,3,1,0:T(8,128)(2,1)}, u32[]{:S(2)}) copy-start(bf16[1,4,128,64]{2,3,1,0:T(8,128)(2,1)} %param.16) | copy-start | bytes 196612
  14.9 18.7 %collective-permute-start.2 = (bf16[128,2688]{1,0:T(8,128)(2,1)S(1)}, bf16[128,2688]{1,0:T(8,128)(2,1)S(1)}, u32[]{:S(2)}, u32[]{:S(2)}) collective-permute-start(bf16[128,2688]{1,0:T(8,128)(2,1)S(1)} %get-tuple-element.25), channel_id=1, source_target_pairs={{16,0},{32,16},{48,32},{64,48},{80,64},{96,80},{112,96},{128,112},... | collective-permute-start | bytes 2064392 | tf_op jit(solution)/shard_map/ppermute | solution.py:577
  16.2 17.4 %collective-permute-start.1 = (bf16[128,2560]{1,0:T(8,128)(2,1)S(1)}, bf16[128,2560]{1,0:T(8,128)(2,1)S(1)}, u32[]{:S(2)}, u32[]{:S(2)}) collective-permute-start(bf16[128,2560]{1,0:T(8,128)(2,1)S(1)} %get-tuple-element.24), channel_id=1, source_target_pairs={{0,16},{16,32},{32,48},{48,64},{64,80},{80,96},{96,112},{112,128},... | collective-permute-start | bytes 1966088 | tf_op jit(solution)/shard_map/ppermute | solution.py:576
  45.3 20.3 %all-to-all-start = ((bf16[32,32,128]{2,1,0:T(8,128)(2,1)}), bf16[32,32,128]{2,1,0:T(8,128)(2,1)S(1)}, u32[]{:S(2)}, u32[]{:S(2)}) async-start(bf16[32,32,128]{2,1,0:T(8,128)(2,1)} %bitcast.15), calls=%async_computation | async-start | bytes 524288 | tf_op jit(solution)/shard_map/all_to_all | solution.py:588
  56.0 30.8 %collective-permute-start.3 = (bf16[4,128,640]{2,1,0:T(8,128)(2,1)}, bf16[4,128,640]{2,1,0:T(8,128)(2,1)S(1)}, u32[]{:S(2)}, u32[]{:S(2)}) collective-permute-start(bf16[4,128,640]{2,1,0:T(8,128)(2,1)} %get-tuple-element.35), channel_id=1, source_target_pairs={{16,0},{32,16},{48,32},{64,48},{80,64},{96,80},{112,96},{128,112},... | collective-permute-start | bytes 1966088 | tf_op jit(solution)/shard_map/ppermute | solution.py:594
  57.3 29.5 %collective-permute-start.4 = (bf16[2,128,640]{2,1,0:T(8,128)(2,1)}, bf16[2,128,640]{2,1,0:T(8,128)(2,1)S(1)}, u32[]{:S(2)}, u32[]{:S(2)}) collective-permute-start(bf16[2,128,640]{2,1,0:T(8,128)(2,1)} %get-tuple-element.36), channel_id=1, source_target_pairs={{0,16},{16,32},{32,48},{48,64},{64,80},{80,96},{96,112},{112,128},... | collective-permute-start | bytes 983048 | tf_op jit(solution)/shard_map/ppermute | solution.py:595
  66.3 14.0 %all-to-all-start.1 = ((bf16[8,32,128]{2,1,0:T(8,128)(2,1)}), bf16[8,32,128]{2,1,0:T(8,128)(2,1)S(1)}, u32[]{:S(2)}, u32[]{:S(2)}) async-start(bf16[8,32,128]{2,1,0:T(8,128)(2,1)} %first_sum.1), calls=%async_computation.1 | async-start | bytes 131072 | tf_op jit(solution)/shard_map/all_to_all | solution.py:589
  81.1 15.5 %all-to-all-start.2 = ((bf16[32,32,128]{2,1,0:T(8,128)(2,1)}), bf16[32,32,128]{2,1,0:T(8,128)(2,1)S(1)}, u32[]{:S(2)}, u32[]{:S(2)}) async-start(bf16[32,32,128]{2,1,0:T(8,128)(2,1)} %second_sum.1), calls=%async_computation.2 | async-start | bytes 524288 | tf_op jit(solution)/shard_map/all_to_all | solution.py:592
  89.3 15.4 %collective-permute-start.5 = (bf16[2,128,1280]{2,1,0:T(8,128)(2,1)S(1)}, bf16[2,128,1280]{2,1,0:T(8,128)(2,1)S(1)}, u32[]{:S(2)}, u32[]{:S(2)}) collective-permute-start(bf16[2,128,1280]{2,1,0:T(8,128)(2,1)S(1)} %get-tuple-element.38), channel_id=1, source_target_pairs={{0,8},{8,0},{1,9},{9,1},{2,10},{10,2},{3,11},{11,3},{4,12},{12,4},... | collective-permute-start | bytes 1966088 | tf_op jit(solution)/shard_map/ppermute | solution.py:599
  96.6 9.8 %collective-permute-start.6 = (bf16[64,16,128]{2,1,0:T(8,128)(2,1)S(1)}, bf16[64,16,128]{2,1,0:T(8,128)(2,1)S(1)}, u32[]{:S(2)}, u32[]{:S(2)}) collective-permute-start(bf16[64,16,128]{2,1,0:T(8,128)(2,1)S(1)} %bitcast.20), channel_id=1, source_target_pairs={{0,8},{8,0},{1,9},{9,1},{2,10},{10,2},{3,11},{11,3},{4,12},{12,4},... | collective-permute-start | bytes 786440 | tf_op jit(solution)/shard_map/ppermute | solution.py:593

commit v8 on v7

--- a/solution.py
+++ b/solution.py
@@ -155,21 +155,52 @@
     return jnp.concatenate(blocks, 0)
 
 
-def soften(raw, prods, biases, keep=None):
+def soften(raw, prods, biases, own=None, keep=None):
     tops = [jnp.max(r, 0, keepdims=True) + b for r, b in zip(raw, biases)]
+    if own is not None:
+        own_weights, own_prods, (own_top, own_total, own_moment) = own
+        tops.append(own_top)
     top = functools.reduce(jnp.maximum, tops)
     weights = [jnp.exp2(r * SCALE2 + (b - top) * SCALE2) for r, b in zip(raw, biases)]
     total = jnp.sum(functools.reduce(jnp.add, weights), 0, keepdims=True)
     mixed = [w * p for w, p in zip(weights, prods)]
     moment = jnp.sum(functools.reduce(jnp.add, mixed), 0, keepdims=True)
+    factors = [None] * len(weights)
+    if own is not None:
+        factor = jnp.exp2((own_top - top) * SCALE2)
+        total = total + own_total * factor
+        moment = moment + own_moment * factor
+        weights = weights + own_weights
+        prods = prods + own_prods
+        factors += [factor] * len(own_weights)
     inverse = 1.0 / total
     if keep is not None:
         inverse = inverse * keep
     delta = moment * inverse
-    scaled = inverse * SCALE
-    prob = [(w * inverse).astype(BF16) for w in weights]
-    dscore = [((w * scaled) * (p - delta)).astype(BF16) for w, p in zip(weights, prods)]
+    prob, dscore = [], []
+    for w, p, factor in zip(weights, prods, factors):
+        share = inverse if factor is None else inverse * factor
+        prob.append((w * share).astype(BF16))
+        dscore.append(((w * (share * SCALE)) * (p - delta)).astype(BF16))
     return prob, dscore
+
+
+def weigh(raw, prods, biases):
+    tops = [jnp.max(r, 0, keepdims=True) + b for r, b in zip(raw, biases)]
+    top = functools.reduce(jnp.maximum, tops)
+    weights = [jnp.exp2(r * SCALE2 + (b - top) * SCALE2) for r, b in zip(raw, biases)]
+    total = jnp.sum(functools.reduce(jnp.add, weights), 0, keepdims=True)
+    moment = jnp.sum(functools.reduce(jnp.add, [w * p for w, p in zip(weights, prods)]), 0, keepdims=True)
+    return weights, (top, total, moment)
+
+
+def own_row(weights, prods, stats, row):
+    cuts = ((0,), (1, 2))[row]
+    return (
+        [weights[:, i * TOK:(i + 1) * TOK] for i in cuts],
+        [prods[:, i * TOK:(i + 1) * TOK] for i in cuts],
+        tuple(stats[3 * row + i:3 * row + i + 1] for i in range(3)),
+    )
 
 
 class Masks:
@@ -201,7 +232,7 @@
 
 def own_kernel(
     clips, place, lengths, robots, adapters, near, oth, up_hbm,
-    adapted, adapted_t, queries, raws, prods, up, sem,
+    adapted, adapted_t, queries, weights, prods, stats, up, sem,
 ):
     view = Views(place, near, oth, None, None)
     half, quarter = view.half, view.quarter
@@ -221,9 +252,17 @@
             query = (column(view.both(0, group, j)).astype(F32) + shift).astype(BF16)
             queries[j, group] = query
             grad = column(view.both(1, group, j))
-            for out, pair, rows in ((raws, view.both(2, group, j), query), (prods, view.both(3, group, j), grad)):
-                out[j, group, :, : 2 * TOK] = dot(pair[0], rows, 1, 1)
-                out[j, group, :, 2 * TOK:] = dot(pair[1], rows[TOK:], 1, 1)
+            raw, prod = [], []
+            for out, pair, rows in ((raw, view.both(2, group, j), query), (prod, view.both(3, group, j), grad)):
+                first = dot(pair[0], rows, 1, 1)
+                out += [first[:, :TOK], first[:, TOK:], dot(pair[1], rows[TOK:], 1, 1)]
+            row_a, stats_a = weigh(raw[:1], prod[:1], masks.a[2:])
+            row_b, stats_b = weigh(raw[1:], prod[1:], masks.b[1:])
+            for i, (w, p) in enumerate(zip(row_a + row_b, prod)):
+                weights[j, group, :, i * TOK:(i + 1) * TOK] = w
+                prods[j, group, :, i * TOK:(i + 1) * TOK] = p
+            for i, stat in enumerate(stats_a + stats_b):
+                stats[j, group, i:i + 1, :] = stat
 
 
 def own_scores(scalars, adapters, near, oth, up):
@@ -232,11 +271,12 @@
     return pl.pallas_call(
         functools.partial(own_kernel, scalars[1].shape[0]),
         in_specs=[smem()] * 3 + [vmem()] * 3 + [hbm()],
-        out_specs=[vmem()] * 5,
+        out_specs=[vmem()] * 6,
         out_shape=[
             pltpu.VMEM((2 * TOK, RANK), BF16), pltpu.VMEM((RANK, 2 * TOK), BF16),
             pltpu.VMEM((five, 2, 2 * TOK, HEAD), BF16),
             pltpu.VMEM((five, 2, TOK, 3 * TOK), F32), pltpu.VMEM((five, 2, TOK, 3 * TOK), F32),
+            pltpu.VMEM((five, 2, 8, TOK), F32),
         ],
         scratch_shapes=[pltpu.VMEM((RANK, half), BF16), pltpu.SemaphoreType.DMA((1,))],
         compiler_params=pltpu.CompilerParams(vmem_limit_bytes=12 * MIB),
@@ -247,28 +287,27 @@
     )(*scalars, adapters, near, oth, fixed(up))
 
 
-def narrow_head(view, masks, queries, raws, prods, j):
+def narrow_head(view, masks, queries, weights, prods, stats, j):
     none = jnp.zeros((TOK, TOK), BF16)
     query = queries[j, 0]
     grad = column(view.both(1, 0, j))
     keys = column([view.lower(2, j), view.lower(0, j)] + view.both(2, 0, j))
 
-    def blocks(p0, p1, rows, own):
+    def blocks(p0, p1, rows):
         far = dot(p1, rows, 1, 1)
-        near = own[j, 0]
-        row_a = [dot(p0, rows[:TOK], 1, 1), far[:, :TOK], near[:, :TOK]]
-        return row_a, [far[:, TOK:], near[:, TOK:2 * TOK], near[:, 2 * TOK:]]
-
-    raw_a, raw_b = blocks(view.lower(2, j), view.lower(0, j), query, raws)
-    prod_a, prod_b = blocks(view.lower(3, j), view.lower(1, j), grad, prods)
-    prob_a, dscore_a = soften(raw_a, prod_a, masks.a)
-    prob_b, dscore_b = soften(raw_b, prod_b, masks.b)
+        return [dot(p0, rows[:TOK], 1, 1), far[:, :TOK]], [far[:, TOK:]]
+
+    raw_a, raw_b = blocks(view.lower(2, j), view.lower(0, j), query)
+    prod_a, prod_b = blocks(view.lower(3, j), view.lower(1, j), grad)
+    own = [own_row(weights[j, 0], prods[j, 0], stats[j, 0], row) for row in range(2)]
+    prob_a, dscore_a = soften(raw_a, prod_a, masks.a[:2], own[0])
+    prob_b, dscore_b = soften(raw_b, prod_b, masks.b[:1], own[1])
     prob = jnp.concatenate([column(prob_a + [none]), column([none] + prob_b)], 1)
     dscore = jnp.concatenate([column(dscore_a + [none]), column([none] + dscore_b)], 1)
     return query, grad, keys, prob, dscore
 
 
-def wide_head(view, masks, queries, raws, prods, adapted_n, up_h, j):
+def wide_head(view, masks, queries, weights, prods, stats, adapted_n, up_h, j):
     none = jnp.zeros((TOK, TOK), BF16)
     query = queries[j, 1]
     query_n = (view.upper(0, j).astype(F32) + dot(adapted_n, up_h, 1, 0)).astype(BF16)
@@ -276,20 +315,15 @@
     grad_n = view.upper(1, j)
     keys = column([view.lower(2, j)] + view.both(2, 1, j) + [view.upper(2, j)])
     values = column(view.both(3, 1, j) + [view.upper(3, j)])
-
-    def blocks(p1, rows, own):
-        far = dot(p1, rows, 1, 1)
-        near = own[j, 1]
-        return [far[:, :TOK], near[:, :TOK]], [far[:, TOK:], near[:, TOK:2 * TOK], near[:, 2 * TOK:]]
-
-    raw_a, raw_b = blocks(view.lower(2, j), query, raws)
-    prod_a, prod_b = blocks(view.lower(3, j), grad, prods)
+    raw = dot(view.lower(2, j), query, 1, 1)
+    prod = dot(view.lower(3, j), grad, 1, 1)
     raw_n = dot(keys[TOK:], query_n, 1, 1)
     prod_n = dot(values, grad_n, 1, 1)
-    prob_a, dscore_a = soften(raw_a, prod_a, masks.a[1:], masks.scale_a)
-    prob_b, dscore_b = soften(raw_b, prod_b, masks.b)
+    own = [own_row(weights[j, 1], prods[j, 1], stats[j, 1], row) for row in range(2)]
+    prob_a, dscore_a = soften([raw[:, :TOK]], [prod[:, :TOK]], masks.a[1:2], own[0], masks.scale_a)
+    prob_b, dscore_b = soften([raw[:, TOK:]], [prod[:, TOK:]], masks.b[:1], own[1])
     prob_n, dscore_n = soften(
-        [block(raw_n, i, 0) for i in range(3)], [block(prod_n, i, 0) for i in range(3)], masks.n, masks.scale_n
+        [block(raw_n, i, 0) for i in range(3)], [block(prod_n, i, 0) for i in range(3)], masks.n, None, masks.scale_n
     )
     prob = jnp.concatenate([column(prob_a + [none, none]), column(prob_b + [none]), column([none] + prob_n)], 1)
     dscore = jnp.concatenate([column(dscore_a + [none, none]), column(dscore_b + [none]), column([none] + dscore_n)], 1)
@@ -297,8 +331,8 @@
 
 
 def attend_kernel(
-    clips, place, lengths, robots, adapters, near, oth, below, above, adapted_own, adapted_own_t, queries, raws, prods,
-    up_hbm, payload, sum_a, sum_b, ret_down, ret_up,
+    clips, place, lengths, robots, adapters, near, oth, below, above, adapted_own, adapted_own_t, queries, weights, prods,
+    stats, up_hbm, payload, sum_a, sum_b, ret_down, ret_up,
     up, adapted, adapted_t, agrad_t, pay, keep_a, keep_b, keep_down, keep_up, sem_in, sem_out,
 ):
     view = Views(place, near, oth, below, above)
@@ -325,30 +359,44 @@
         pay[:, head, :] = term
 
     stores = []
-    for j in range(five):
+
+    def ahead(h):
+        j, group = h // 2, h % 2
+        up_h = up[:, group * quarter + j * HEAD:group * quarter + (j + 1) * HEAD]
+        if group == 0:
+            return up_h, narrow_head(view, masks, queries, weights, prods, stats, j)
+        return up_h, wide_head(view, masks, queries, weights, prods, stats, adapted[2 * TOK:, :], up_h, j)
+
+    def behind(h, made, wide_parts):
+        j, group = h // 2, h % 2
         cols = slice(j * HEAD, (j + 1) * HEAD)
-        up_h = up[:, cols]
-        query, grad, keys, prob, dscore = narrow_head(view, masks, queries, raws, prods, j)
-        sums(keys, dscore, up_h, 2 * TOK, j)
-        wide_parts = []
-        for n, part in enumerate((dot(dscore, query, 1, 0), dot(prob, grad, 1, 0))):
-            wide_parts.append(part[:TOK])
-            keep_down[n, :, cols] = part[TOK:2 * TOK].astype(BF16)
-            keep_a[n, 0, :, cols] = part[2 * TOK:3 * TOK]
-            keep_b[n, 0, :, cols] = part[3 * TOK:]
-        up_h = up[:, quarter + j * HEAD:quarter + (j + 1) * HEAD]
-        query, grad, keys, prob, dscore = wide_head(view, masks, queries, raws, prods, adapted[2 * TOK:, :], up_h, j)
-        sums(keys, dscore, up_h, 3 * TOK, five + j)
-        for n, part in enumerate((dot(dscore, query, 1, 0), dot(prob, grad, 1, 0))):
-            keep_down[2 + n, :, cols] = jnp.where(masks.wide_below, wide_parts[n], part[:TOK]).astype(BF16)
-            keep_a[n, 1, :, cols] = part[TOK:2 * TOK]
-            keep_b[n, 1, :, cols] = part[2 * TOK:3 * TOK]
-            keep_up[n, :, cols] = part[3 * TOK:].astype(BF16)
+        up_h, (query, grad, keys, prob, dscore) = made
+        sums(keys, dscore, up_h, (2 + group) * TOK, group * five + j)
+        parts = (dot(dscore, query, 1, 0), dot(prob, grad, 1, 0))
+        for n, part in enumerate(parts):
+            if group == 0:
+                keep_down[n, :, cols] = part[TOK:2 * TOK].astype(BF16)
+                keep_a[n, 0, :, cols] = part[2 * TOK:3 * TOK]
+                keep_b[n, 0, :, cols] = part[3 * TOK:]
+            else:
+                keep_down[2 + n, :, cols] = jnp.where(masks.wide_below, wide_parts[n], part[:TOK]).astype(BF16)
+                keep_a[n, 1, :, cols] = part[TOK:2 * TOK]
+                keep_b[n, 1, :, cols] = part[2 * TOK:3 * TOK]
+                keep_up[n, :, cols] = part[3 * TOK:].astype(BF16)
+        if group == 0:
+            return [part[:TOK] for part in parts]
         span = pl.ds(j * HEAD, HEAD)
         for n, (x, y) in enumerate(((keep_down, ret_down), (keep_up, ret_up), (keep_a, sum_a), (keep_b, sum_b))):
             at = (slice(None),) * (len(x.shape) - 1) + (span,)
             stores.append(pltpu.make_async_copy(x.at[at], y.at[at], sem_out.at[j, n]))
             stores[-1].start()
+        return None
+
+    made, kept = ahead(0), None
+    for h in range(2 * five):
+        following = ahead(h + 1) if h + 1 < 2 * five else None
+        kept = behind(h, made, kept)
+        made = following
 
     terms = []
     for n, act in enumerate(acts):
@@ -374,7 +422,7 @@
     sums = ((2, 2, TOK, quarter), F32)
     return pl.pallas_call(
         functools.partial(attend_kernel, scalars[1].shape[0]),
-        in_specs=[smem()] * 3 + [vmem()] * 10 + [hbm()],
+        in_specs=[smem()] * 3 + [vmem()] * 11 + [hbm()],
         out_specs=[vmem()] + [hbm()] * 4,
         out_shape=[jax.ShapeDtypeStruct((RANK, ROWS, HEAD), BF16)] + [pltpu.HBM(*x) for x in (sums, sums, *shapes)],
         scratch_shapes=[
@@ -398,21 +446,21 @@
     )(*scalars, adapters, near, oth, below, above, *stored, fixed(up))
 
 
-def hold_kernel(down_in, up_in, down_out, up_out):
+def hold_kernel(held_in, after, held_out):
     pass
 
 
-def hold(ret_down, ret_up):
+def hold(held, after):
     return pl.pallas_call(
         hold_kernel,
         in_specs=[hbm()] * 2,
-        out_specs=[hbm()] * 2,
-        out_shape=[pltpu.HBM(x.shape, x.dtype) for x in (ret_down, ret_up)],
-        input_output_aliases={0: 0, 1: 1},
+        out_specs=hbm(),
+        out_shape=pltpu.HBM(held.shape, held.dtype),
+        input_output_aliases={0: 0},
         compiler_params=pltpu.CompilerParams(vmem_limit_bytes=MIB),
         cost_estimate=pl.CostEstimate(flops=MIB, bytes_accessed=MIB, transcendentals=0),
         name="hold",
-    )(fixed(ret_down), fixed(ret_up))
+    )(fixed(held), after)
 
 
 def join_kernel(
@@ -580,13 +628,14 @@
     payload, sum_a, sum_b, ret_down, ret_up = attend(
         scalars, table, near, oth, below, above, stored, up_proj
     )
-    ret_down, ret_up = hold(ret_down, ret_up)
+    ret_down, ret_up = hold(ret_down, payload), hold(ret_up, payload)
 
     plane = ("dp", "x", "z")
     peers = lax.axis_size(plane)
     share = (peers, RANK // peers * ROWS, HEAD)
     pieces = lax.all_to_all(payload.reshape(share), plane, 0, 0, tiled=True)
-    pieces = lax.all_to_all(first_sum(pieces, ny), "y", 0, 0, tiled=True)
+    message = first_sum(pieces, ny)
+    pieces = lax.all_to_all(message, "y", 0, 0, tiled=True)
     row = lax.axis_index("y").astype(jnp.int32).reshape(1)
     message = second_sum(row, pieces, peers, heads // 2)
     gathered = lax.all_to_all(message, plane, 0, 0, tiled=True).reshape(RANK, ROWS, HEAD)

time: 109 us -> 107 us (0.982)
  Pallas kernels: 27.6 us -> 25.7 us
    pallas_call x1, Pallas kernels: 11.7 us -> 9.66 us  [attend(): pl.pallas_call(functools.partial(attend_kernel, scalars[1].shape[0]), in_...]
where the time goes in v8:
time: 107 us; the launch traced here: 106 us
  starting transfers between devices  57.8 us (54%)
  Pallas kernels  25.7 us (24%)
  waiting for transfers between devices  21.7 us (20%)
    all_to_all x1, starting transfers between devices, local(): pieces = lax.all_to_all(payload.reshape(share), plane, 0, 0, tiled=True)  10.7 us
    pallas_call x1, Pallas kernels, attend(): pl.pallas_call(functools.partial(attend_kernel, scalars[1].shape[0]), in_...  9.66 us
    ppermute x1, waiting for transfers between devices, local(): below = lax.ppermute(up_msg, chain, upward)  9.14 us
    ppermute x1, starting transfers between devices, local(): oth = lax.ppermute(take_half(place, own, act, True), 'core', swap)  8.79 us
    ppermute x1, starting transfers between devices, local(): swapped = lax.ppermute(gathered, 'core', swap)  8.13 us
    all_to_all x1, waiting for transfers between devices, local(): pieces = lax.all_to_all(message, 'y', 0, 0, tiled=True)  7.23 us
    ppermute x1, starting transfers between devices, local(): lax.ppermute(theirs, 'core', swap)  7.09 us
    all_to_all x1, starting transfers between devices, local(): pieces = lax.all_to_all(message, 'y', 0, 0, tiled=True)  6.83 us
  transfers between devices with their start and end apart: 10, of which 5 were waited for; matrix products, arithmetic and copies ran while one was open for 0% of the time, Pallas kernels for 11%

profile of v8, /device:TPU:1, one launch (start us, length us, event | category | flops | bytes accessed | tf_op | source)
XLA Modules:
  0.0 106.1 jit_solution(14820976490326486651)
XLA Ops:
  0.7 1.9 %take_far.1 = bf16[128,5248]{1,0:T(8,128)(2,1)S(1)} custom-call(s32[2]{0:T(128)S(1)} %pad_add_fusion.place, bf16[128,2560]{1,0:T(8,128)(2,1)} %bitcast.32, bf16[128,2560]{1,0:T(8,128)(2,1)} %bitcast.34, bf16[128,2560]{1,0:T(8,128)(2,1)} %bitcast.36, bf16[128,2560]{1,0:T(8,128)(2,1)} %bitcast.38, bf16[128,128]{1,0:T(8,128)(2,1)} %bitcast.40), custom_call_target="tpu_custom_call" | custom-call | bytes 4194304 | tf_op jit(solution)/shard_map/take_far/pallas_call | solution.py:74
  2.6 8.8 %collective-permute-start = (bf16[128,5248]{1,0:T(8,128)(2,1)S(1)}, bf16[128,5248]{1,0:T(8,128)(2,1)S(1)}, u32[]{:S(2)}, u32[]{:S(2)}) collective-permute-start(bf16[128,5248]{1,0:T(8,128)(2,1)S(1)} %take_far.1), channel_id=1, source_target_pairs={{0,8},{8,0},{1,9},{9,1},{2,10},{10,2},{3,11},{11,3},{4,12},{12,4},... | collective-permute-start | bytes 4030472 | tf_op jit(solution)/shard_map/ppermute | solution.py:621
  11.4 1.9 %take_near.1.near = bf16[128,5248]{1,0:T(8,128)(2,1)S(1)} custom-call(s32[2]{0:T(128)S(1)} %pad_add_fusion.place, bf16[128,2560]{1,0:T(8,128)(2,1)} %bitcast.33, bf16[128,2560]{1,0:T(8,128)(2,1)} %bitcast.35, bf16[128,2560]{1,0:T(8,128)(2,1)} %bitcast.37, bf16[128,2560]{1,0:T(8,128)(2,1)} %bitcast.39, bf16[128,128]{1,0:T(8,128)(2,1)} %bitcast.41), custom_call_target="tpu_custom_call" | custom-call | bytes 4194304 | tf_op jit(solution)/shard_map/take_near/pallas_call | solution.py:74
  13.3 0.8 collective-permute-done.oth
  14.1 0.8 pack.1
  14.9 1.3 %collective-permute-start.2 = (bf16[128,2688]{1,0:T(8,128)(2,1)S(1)}, bf16[128,2688]{1,0:T(8,128)(2,1)S(1)}, u32[]{:S(2)}, u32[]{:S(2)}) collective-permute-start(bf16[128,2688]{1,0:T(8,128)(2,1)S(1)} %get-tuple-element.24), channel_id=1, source_target_pairs={{16,0},{32,16},{48,32},{64,48},{80,64},{96,80},{112,96},{128,112},... | collective-permute-start | bytes 2064392 | tf_op jit(solution)/shard_map/ppermute | solution.py:625
  16.2 4.0 %collective-permute-start.1 = (bf16[128,2560]{1,0:T(8,128)(2,1)S(1)}, bf16[128,2560]{1,0:T(8,128)(2,1)S(1)}, u32[]{:S(2)}, u32[]{:S(2)}) collective-permute-start(bf16[128,2560]{1,0:T(8,128)(2,1)S(1)} %get-tuple-element.23), channel_id=1, source_target_pairs={{0,16},{16,32},{32,48},{48,64},{64,80},{80,96},{96,112},{112,128},... | collective-permute-start | bytes 1966088 | tf_op jit(solution)/shard_map/ppermute | solution.py:624
  20.2 4.2 %own_scores.1 = (bf16[256,64]{1,0:T(8,128)(2,1)S(1)}, bf16[64,256]{1,0:T(8,128)(2,1)S(1)}, bf16[5,2,256,128]{3,2,1,0:T(8,128)(2,1)S(1)}, f32[5,2,128,384]{3,2,1,...) custom-call(s32[2]{0:T(128)S(1)} %pad_add_fusion.place, s32[16]{0:T(128)S(1)} %bitcast.25, ...), custom_call_target="tpu_custom_call" | custom-call | flops 1006632960 | bytes 4194304 | tf_op jit(solution)/shard_map/own_scores/pallas_call | solution.py:271
  24.4 9.1 %collective-permute-done.1.below = bf16[128,2560]{1,0:T(8,128)(2,1)S(1)} collective-permute-done((bf16[128,2560]{1,0:T(8,128)(2,1)S(1)}, bf16[128,2560]{1,0:T(8,128)(2,1)S(1)}, u32[]{:S(2)}, u32[]{:S(2)}) %collective-permute-start.1) | collective-permute-done | bytes 655392 | tf_op jit(solution)/shard_map/ppermute | solution.py:624
  33.6 9.7 %attend.1 = (bf16[64,16,128]{2,1,0:T(8,128)(2,1)}, f32[2,2,128,640]{3,2,1,0:T(8,128)}, f32[2,2,128,640]{3,2,1,0:T(8,128)}, bf16[4,128,640]{2,1,0:T(8,128)(2,1)}, bf16[2,128,640]{2,1,0:T(8,128)(2,1)}) custom-call(s32[2]{0:T(128)S(1)} %pad_add_fusion.place, s32[16]{0:T(128)S(1)} %bitcast.26, s32[16]{0:T(128)S(1)} %bitcast.30, ...), custom_call_target="tpu_custom_call" | custom-call | flops 2013265920 | bytes 12582912 | tf_op jit(solution)/shard_map/attend/pallas_call | solution.py:423
  43.3 10.7 %all-to-all-start = ((bf16[32,32,128]{2,1,0:T(8,128)(2,1)}), bf16[32,32,128]{2,1,0:T(8,128)(2,1)S(1)}, u32[]{:S(2)}, u32[]{:S(2)}) async-start(bf16[32,32,128]{2,1,0:T(8,128)(2,1)} %bitcast.15), calls=%async_computation | async-start | bytes 524288 | tf_op jit(solution)/shard_map/all_to_all | solution.py:636
  53.9 1.3 %collective-permute-start.3 = (bf16[4,128,640]{2,1,0:T(8,128)(2,1)}, bf16[4,128,640]{2,1,0:T(8,128)(2,1)S(1)}, u32[]{:S(2)}, u32[]{:S(2)}) collective-permute-start(bf16[4,128,640]{2,1,0:T(8,128)(2,1)} %hold.2), channel_id=1, source_target_pairs={{16,0},{32,16},{48,32},{64,48},{80,64},{96,80},{112,96},{128,112},... | collective-permute-start | bytes 1966088 | tf_op jit(solution)/shard_map/ppermute | solution.py:643
  55.2 4.0 %collective-permute-start.4 = (bf16[2,128,640]{2,1,0:T(8,128)(2,1)}, bf16[2,128,640]{2,1,0:T(8,128)(2,1)S(1)}, u32[]{:S(2)}, u32[]{:S(2)}) collective-permute-start(bf16[2,128,640]{2,1,0:T(8,128)(2,1)} %hold.3), channel_id=1, source_target_pairs={{0,16},{16,32},{32,48},{48,64},{64,80},{80,96},{96,112},{112,128},... | collective-permute-start | bytes 983048 | tf_op jit(solution)/shard_map/ppermute | solution.py:644
  59.2 4.3 %all-to-all-done.pieces = bf16[32,32,128]{2,1,0:T(8,128)(2,1)S(1)} async-done(((bf16[32,32,128]{2,1,0:T(8,128)(2,1)}), bf16[32,32,128]{2,1,0:T(8,128)(2,1)S(1)}, u32[]{:S(2)}, u32[]{:S(2)}) %all-to-all-start) | async-done | bytes 262176 | tf_op jit(solution)/shard_map/all_to_all | solution.py:636
  63.6 0.7 first_sum.1
  64.2 6.8 %all-to-all-start.1 = ((bf16[8,32,128]{2,1,0:T(8,128)(2,1)}), bf16[8,32,128]{2,1,0:T(8,128)(2,1)S(1)}, u32[]{:S(2)}, u32[]{:S(2)}) async-start(bf16[8,32,128]{2,1,0:T(8,128)(2,1)} %first_sum.1), calls=%async_computation.1 | async-start | bytes 131072 | tf_op jit(solution)/shard_map/all_to_all | solution.py:638
  71.1 7.2 %all-to-all-done.1.pieces = bf16[8,32,128]{2,1,0:T(8,128)(2,1)S(1)} async-done(((bf16[8,32,128]{2,1,0:T(8,128)(2,1)}), bf16[8,32,128]{2,1,0:T(8,128)(2,1)S(1)}, u32[]{:S(2)}, u32[]{:S(2)}) %all-to-all-start.1) | async-done | bytes 65568 | tf_op jit(solution)/shard_map/all_to_all | solution.py:638
  78.3 0.7 second_sum.1
  79.0 5.7 %all-to-all-start.2 = ((bf16[32,32,128]{2,1,0:T(8,128)(2,1)}), bf16[32,32,128]{2,1,0:T(8,128)(2,1)S(1)}, u32[]{:S(2)}, u32[]{:S(2)}) async-start(bf16[32,32,128]{2,1,0:T(8,128)(2,1)} %second_sum.1), calls=%async_computation.2 | async-start | bytes 524288 | tf_op jit(solution)/shard_map/all_to_all | solution.py:641
  84.8 2.5 %join.1 = (bf16[2,128,1280]{2,1,0:T(8,128)(2,1)S(1)}, bf16[2,128,1280]{2,1,0:T(8,128)(2,1)S(1)}) custom-call(s32[2]{0:T(128)S(1)} %pad_add_fusion.place, s32[16]{0:T(128)S(1)} %bitcast.27, s32[16]{0:T(128)S(1)} %bitcast.31, f32[2,2,128,640]{3,2,1,0:T(8,128)} %get-tuple-element.31.sum_a_hbm, f32[2,2,128,640]{3,2,1,0:T(8,128)} %get-tuple-element.32.sum_b_hbm, ...), custom_call_target="tpu_custom_call" | custom-call | flops 1048576 | bytes 6291456 | tf_op jit(solution)/shard_map/join/pallas_call | solution.py:499
  87.3 7.1 %collective-permute-start.5 = (bf16[2,128,1280]{2,1,0:T(8,128)(2,1)S(1)}, bf16[2,128,1280]{2,1,0:T(8,128)(2,1)S(1)}, u32[]{:S(2)}, u32[]{:S(2)}) collective-permute-start(bf16[2,128,1280]{2,1,0:T(8,128)(2,1)S(1)} %get-tuple-element.37), channel_id=1, source_target_pairs={{0,8},{8,0},{1,9},{9,1},{2,10},{10,2},{3,11},{11,3},{4,12},{12,4},... | collective-permute-start | bytes 1966088 | tf_op jit(solution)/shard_map/ppermute | solution.py:648
  94.5 8.1 %collective-permute-start.6 = (bf16[64,16,128]{2,1,0:T(8,128)(2,1)S(1)}, bf16[64,16,128]{2,1,0:T(8,128)(2,1)S(1)}, u32[]{:S(2)}, u32[]{:S(2)}) collective-permute-start(bf16[64,16,128]{2,1,0:T(8,128)(2,1)S(1)} %bitcast.20), channel_id=1, source_target_pairs={{0,8},{8,0},{1,9},{9,1},{2,10},{10,2},{3,11},{11,3},{4,12},{12,4},... | collective-permute-start | bytes 786440 | tf_op jit(solution)/shard_map/ppermute | solution.py:642
  102.7 1.6 %place_halves.1 = (bf16[128,2560]{1,0:T(8,128)(2,1)}, bf16[128,2560]{1,0:T(8,128)(2,1)}) custom-call(s32[2]{0:T(128)S(1)} %pad_add_fusion.place, bf16[2,128,1280]{2,1,0:T(8,128)(2,1)S(1)} %get-tuple-element.36.mine, bf16[2,128,1280]{2,1,0:T(8,128)(2,1)S(1)} %collective-permute-done.5.other), custom_call_target="tpu_custom_call" | custom-call | bytes 4194304 | tf_op jit(solution)/shard_map/place_halves/pallas_call | solution.py:528
  104.3 1.8 %finish.1 = (f32[64,2560]{1,0:T(8,128)}, f32[4,64,128]{2,1,0:T(8,128)}) custom-call(s32[2]{0:T(128)S(1)} %pad_add_fusion.place, bf16[64,16,128]{2,1,0:T(8,128)(2,1)S(1)} %bitcast.21, bf16[64,16,128]{2,1,0:T(8,128)(2,1)S(1)} %collective-permute-done.6.swapped), custom_call_target="tpu_custom_call" | custom-call | tf_op jit(solution)/shard_map/finish/pallas_call | solution.py:590
  (15 shorter events, 0.2 us)
Async XLA Ops:
  2.6 11.5 %copy-start.1 = (s32[1,1,16]{2,1,0:T(1,128)S(1)}, s32[1,1,16]{2,1,0:T(1,128)}, u32[]{:S(2)}) copy-start(s32[1,1,16]{2,1,0:T(1,128)} %param.14) | copy-start | bytes 196
  2.6 11.5 %copy-start.2 = (s32[1,1,16]{2,1,0:T(1,128)S(1)}, s32[1,1,16]{2,1,0:T(1,128)}, u32[]{:S(2)}) copy-start(s32[1,1,16]{2,1,0:T(1,128)} %param.15) | copy-start | bytes 196
  2.6 11.5 %collective-permute-start = (bf16[128,5248]{1,0:T(8,128)(2,1)S(1)}, bf16[128,5248]{1,0:T(8,128)(2,1)S(1)}, u32[]{:S(2)}, u32[]{:S(2)}) collective-permute-start(bf16[128,5248]{1,0:T(8,128)(2,1)S(1)} %take_far.1), channel_id=1, source_target_pairs={{0,8},{8,0},{1,9},{9,1},{2,10},{10,2},{3,11},{11,3},{4,12},{12,4},... | collective-permute-start | bytes 4030472 | tf_op jit(solution)/shard_map/ppermute | solution.py:621
  14.1 6.1 %copy-start = (bf16[1,4,128,64]{2,3,1,0:T(8,128)(2,1)S(1)}, bf16[1,4,128,64]{2,3,1,0:T(8,128)(2,1)}, u32[]{:S(2)}) copy-start(bf16[1,4,128,64]{2,3,1,0:T(8,128)(2,1)} %param.16) | copy-start | bytes 196612
  14.9 18.7 %collective-permute-start.2 = (bf16[128,2688]{1,0:T(8,128)(2,1)S(1)}, bf16[128,2688]{1,0:T(8,128)(2,1)S(1)}, u32[]{:S(2)}, u32[]{:S(2)}) collective-permute-start(bf16[128,2688]{1,0:T(8,128)(2,1)S(1)} %get-tuple-element.24), channel_id=1, source_target_pairs={{16,0},{32,16},{48,32},{64,48},{80,64},{96,80},{112,96},{128,112},... | collective-permute-start | bytes 2064392 | tf_op jit(solution)/shard_map/ppermute | solution.py:625
  16.2 17.4 %collective-permute-start.1 = (bf16[128,2560]{1,0:T(8,128)(2,1)S(1)}, bf16[128,2560]{1,0:T(8,128)(2,1)S(1)}, u32[]{:S(2)}, u32[]{:S(2)}) collective-permute-start(bf16[128,2560]{1,0:T(8,128)(2,1)S(1)} %get-tuple-element.23), channel_id=1, source_target_pairs={{0,16},{16,32},{32,48},{48,64},{64,80},{80,96},{96,112},{112,128},... | collective-permute-start | bytes 1966088 | tf_op jit(solution)/shard_map/ppermute | solution.py:624
  43.3 20.3 %all-to-all-start = ((bf16[32,32,128]{2,1,0:T(8,128)(2,1)}), bf16[32,32,128]{2,1,0:T(8,128)(2,1)S(1)}, u32[]{:S(2)}, u32[]{:S(2)}) async-start(bf16[32,32,128]{2,1,0:T(8,128)(2,1)} %bitcast.15), calls=%async_computation | async-start | bytes 524288 | tf_op jit(solution)/shard_map/all_to_all | solution.py:636
  53.9 30.9 %collective-permute-start.3 = (bf16[4,128,640]{2,1,0:T(8,128)(2,1)}, bf16[4,128,640]{2,1,0:T(8,128)(2,1)S(1)}, u32[]{:S(2)}, u32[]{:S(2)}) collective-permute-start(bf16[4,128,640]{2,1,0:T(8,128)(2,1)} %hold.2), channel_id=1, source_target_pairs={{16,0},{32,16},{48,32},{64,48},{80,64},{96,80},{112,96},{128,112},... | collective-permute-start | bytes 1966088 | tf_op jit(solution)/shard_map/ppermute | solution.py:643
  55.2 29.5 %collective-permute-start.4 = (bf16[2,128,640]{2,1,0:T(8,128)(2,1)}, bf16[2,128,640]{2,1,0:T(8,128)(2,1)S(1)}, u32[]{:S(2)}, u32[]{:S(2)}) collective-permute-start(bf16[2,128,640]{2,1,0:T(8,128)(2,1)} %hold.3), channel_id=1, source_target_pairs={{0,16},{16,32},{32,48},{48,64},{64,80},{80,96},{96,112},{112,128},... | collective-permute-start | bytes 983048 | tf_op jit(solution)/shard_map/ppermute | solution.py:644
  64.2 14.1 %all-to-all-start.1 = ((bf16[8,32,128]{2,1,0:T(8,128)(2,1)}), bf16[8,32,128]{2,1,0:T(8,128)(2,1)S(1)}, u32[]{:S(2)}, u32[]{:S(2)}) async-start(bf16[8,32,128]{2,1,0:T(8,128)(2,1)} %first_sum.1), calls=%async_computation.1 | async-start | bytes 131072 | tf_op jit(solution)/shard_map/all_to_all | solution.py:638
  79.0 15.5 %all-to-all-start.2 = ((bf16[32,32,128]{2,1,0:T(8,128)(2,1)}), bf16[32,32,128]{2,1,0:T(8,128)(2,1)S(1)}, u32[]{:S(2)}, u32[]{:S(2)}) async-start(bf16[32,32,128]{2,1,0:T(8,128)(2,1)} %second_sum.1), calls=%async_computation.2 | async-start | bytes 524288 | tf_op jit(solution)/shard_map/all_to_all | solution.py:641
  87.3 15.4 %collective-permute-start.5 = (bf16[2,128,1280]{2,1,0:T(8,128)(2,1)S(1)}, bf16[2,128,1280]{2,1,0:T(8,128)(2,1)S(1)}, u32[]{:S(2)}, u32[]{:S(2)}) collective-permute-start(bf16[2,128,1280]{2,1,0:T(8,128)(2,1)S(1)} %get-tuple-element.37), channel_id=1, source_target_pairs={{0,8},{8,0},{1,9},{9,1},{2,10},{10,2},{3,11},{11,3},{4,12},{12,4},... | collective-permute-start | bytes 1966088 | tf_op jit(solution)/shard_map/ppermute | solution.py:648
  94.5 9.8 %collective-permute-start.6 = (bf16[64,16,128]{2,1,0:T(8,128)(2,1)S(1)}, bf16[64,16,128]{2,1,0:T(8,128)(2,1)S(1)}, u32[]{:S(2)}, u32[]{:S(2)}) collective-permute-start(bf16[64,16,128]{2,1,0:T(8,128)(2,1)S(1)} %bitcast.20), channel_id=1, source_target_pairs={{0,8},{8,0},{1,9},{9,1},{2,10},{10,2},{3,11},{11,3},{4,12},{12,4},... | collective-permute-start | bytes 786440 | tf_op jit(solution)/shard_map/ppermute | solution.py:642

commit v9 on v8

--- a/solution.py
+++ b/solution.py
@@ -299,12 +299,16 @@
 
     raw_a, raw_b = blocks(view.lower(2, j), view.lower(0, j), query)
     prod_a, prod_b = blocks(view.lower(3, j), view.lower(1, j), grad)
-    own = [own_row(weights[j, 0], prods[j, 0], stats[j, 0], row) for row in range(2)]
-    prob_a, dscore_a = soften(raw_a, prod_a, masks.a[:2], own[0])
-    prob_b, dscore_b = soften(raw_b, prod_b, masks.b[:1], own[1])
-    prob = jnp.concatenate([column(prob_a + [none]), column([none] + prob_b)], 1)
-    dscore = jnp.concatenate([column(dscore_a + [none]), column([none] + dscore_b)], 1)
-    return query, grad, keys, prob, dscore
+
+    def rest():
+        own = [own_row(weights[j, 0], prods[j, 0], stats[j, 0], row) for row in range(2)]
+        prob_a, dscore_a = soften(raw_a, prod_a, masks.a[:2], own[0])
+        prob_b, dscore_b = soften(raw_b, prod_b, masks.b[:1], own[1])
+        prob = jnp.concatenate([column(prob_a + [none]), column([none] + prob_b)], 1)
+        dscore = jnp.concatenate([column(dscore_a + [none]), column([none] + dscore_b)], 1)
+        return query, grad, keys, prob, dscore
+
+    return rest
 
 
 def wide_head(view, masks, queries, weights, prods, stats, adapted_n, up_h, j):
@@ -319,15 +323,20 @@
     prod = dot(view.lower(3, j), grad, 1, 1)
     raw_n = dot(keys[TOK:], query_n, 1, 1)
     prod_n = dot(values, grad_n, 1, 1)
-    own = [own_row(weights[j, 1], prods[j, 1], stats[j, 1], row) for row in range(2)]
-    prob_a, dscore_a = soften([raw[:, :TOK]], [prod[:, :TOK]], masks.a[1:2], own[0], masks.scale_a)
-    prob_b, dscore_b = soften([raw[:, TOK:]], [prod[:, TOK:]], masks.b[:1], own[1])
-    prob_n, dscore_n = soften(
-        [block(raw_n, i, 0) for i in range(3)], [block(prod_n, i, 0) for i in range(3)], masks.n, None, masks.scale_n
-    )
-    prob = jnp.concatenate([column(prob_a + [none, none]), column(prob_b + [none]), column([none] + prob_n)], 1)
-    dscore = jnp.concatenate([column(dscore_a + [none, none]), column(dscore_b + [none]), column([none] + dscore_n)], 1)
-    return column([query, query_n]), column([grad, grad_n]), keys, prob, dscore
+
+    def rest():
+        own = [own_row(weights[j, 1], prods[j, 1], stats[j, 1], row) for row in range(2)]
+        prob_a, dscore_a = soften([raw[:, :TOK]], [prod[:, :TOK]], masks.a[1:2], own[0], masks.scale_a)
+        prob_b, dscore_b = soften([raw[:, TOK:]], [prod[:, TOK:]], masks.b[:1], own[1])
+        prob_n, dscore_n = soften(
+            [block(raw_n, i, 0) for i in range(3)], [block(prod_n, i, 0) for i in range(3)], masks.n, None, masks.scale_n
+        )
+        probs = [column(prob_a + [none, none]), column(prob_b + [none]), column([none] + prob_n)]
+        dscores = [column(dscore_a + [none, none]), column(dscore_b + [none]), column([none] + dscore_n)]
+        both_rows = column([query, query_n]), column([grad, grad_n])
+        return *both_rows, keys, jnp.concatenate(probs, 1), jnp.concatenate(dscores, 1)
+
+    return rest
 
 
 def attend_kernel(
@@ -351,11 +360,9 @@
     load.wait()
 
     def sums(keys, dscore, up_h, rows, head):
-        query_grad = dot(keys, dscore, 0, 0)
-        high = query_grad.astype(BF16)
-        low = (query_grad - high.astype(F32)).astype(BF16)
-        agrad_t[:, :rows] += dot(up_h, high, 1, 0) + dot(up_h, low, 1, 0)
-        term = dot(adapted_t[:, :rows], high, 1, 1) + dot(adapted_t[:, :rows], low, 1, 1)
+        query_grad = dot(keys, dscore, 0, 0).astype(BF16)
+        agrad_t[:, :rows] += dot(up_h, query_grad, 1, 0)
+        term = dot(adapted_t[:, :rows], query_grad, 1, 1)
         pay[:, head, :] = term
 
     stores = []
@@ -392,11 +399,15 @@
             stores[-1].start()
         return None
 
-    made, kept = ahead(0), None
-    for h in range(2 * five):
-        following = ahead(h + 1) if h + 1 < 2 * five else None
-        kept = behind(h, made, kept)
-        made = following
+    raw, made, kept = {}, {}, None
+    for h in range(2 * five + 2):
+        if h < 2 * five:
+            raw[h] = ahead(h)
+        if 0 < h <= 2 * five:
+            up_h, rest = raw.pop(h - 1)
+            made[h - 1] = up_h, rest()
+        if h > 1:
+            kept = behind(h - 2, made.pop(h - 2), kept)
 
     terms = []
     for n, act in enumerate(acts):

time: 107 us -> 106 us (level)
  no operation moved by 1% of the time
where the time goes in v9:
time: 106 us
  starting transfers between devices  57.8 us (55%)
  Pallas kernels  25.4 us (24%)
  waiting for transfers between devices  21.6 us (20%)
    all_to_all x1, starting transfers between devices, local(): pieces = lax.all_to_all(payload.reshape(share), plane, 0, 0, tiled=True)  10.7 us
    pallas_call x1, Pallas kernels, attend(): pl.pallas_call(functools.partial(attend_kernel, scalars[1].shape[0]), in_...  9.31 us
    ppermute x1, waiting for transfers between devices, local(): below = lax.ppermute(up_msg, chain, upward)  9.14 us
    ppermute x1, starting transfers between devices, local(): oth = lax.ppermute(take_half(place, own, act, True), 'core', swap)  8.79 us
    ppermute x1, starting transfers between devices, local(): swapped = lax.ppermute(gathered, 'core', swap)  8.14 us
    all_to_all x1, waiting for transfers between devices, local(): pieces = lax.all_to_all(message, 'y', 0, 0, tiled=True)  7.23 us
    ppermute x1, starting transfers between devices, local(): lax.ppermute(theirs, 'core', swap)  7.1 us
    all_to_all x1, starting transfers between devices, local(): pieces = lax.all_to_all(message, 'y', 0, 0, tiled=True)  6.82 us
  transfers between devices with their start and end apart: 10, of which 5 were waited for; matrix products, arithmetic and copies ran while one was open for 0% of the time, Pallas kernels for 11%

profile of v9, /device:TPU:1, one launch (start us, length us, event | category | flops | bytes accessed | tf_op | source)
XLA Modules:
  0.0 105.8 jit_solution(812847947112559383)
XLA Ops:
  0.7 1.9 %take_far.1 = bf16[128,5248]{1,0:T(8,128)(2,1)S(1)} custom-call(s32[2]{0:T(128)S(1)} %pad_add_fusion.place, bf16[128,2560]{1,0:T(8,128)(2,1)} %bitcast.32, bf16[128,2560]{1,0:T(8,128)(2,1)} %bitcast.34, bf16[128,2560]{1,0:T(8,128)(2,1)} %bitcast.36, bf16[128,2560]{1,0:T(8,128)(2,1)} %bitcast.38, bf16[128,128]{1,0:T(8,128)(2,1)} %bitcast.40), custom_call_target="tpu_custom_call" | custom-call | bytes 4194304 | tf_op jit(solution)/shard_map/take_far/pallas_call | solution.py:74
  2.6 8.8 %collective-permute-start = (bf16[128,5248]{1,0:T(8,128)(2,1)S(1)}, bf16[128,5248]{1,0:T(8,128)(2,1)S(1)}, u32[]{:S(2)}, u32[]{:S(2)}) collective-permute-start(bf16[128,5248]{1,0:T(8,128)(2,1)S(1)} %take_far.1), channel_id=1, source_target_pairs={{0,8},{8,0},{1,9},{9,1},{2,10},{10,2},{3,11},{11,3},{4,12},{12,4},... | collective-permute-start | bytes 4030472 | tf_op jit(solution)/shard_map/ppermute | solution.py:632
  11.4 1.9 %take_near.1.near = bf16[128,5248]{1,0:T(8,128)(2,1)S(1)} custom-call(s32[2]{0:T(128)S(1)} %pad_add_fusion.place, bf16[128,2560]{1,0:T(8,128)(2,1)} %bitcast.33, bf16[128,2560]{1,0:T(8,128)(2,1)} %bitcast.35, bf16[128,2560]{1,0:T(8,128)(2,1)} %bitcast.37, bf16[128,2560]{1,0:T(8,128)(2,1)} %bitcast.39, bf16[128,128]{1,0:T(8,128)(2,1)} %bitcast.41), custom_call_target="tpu_custom_call" | custom-call | bytes 4194304 | tf_op jit(solution)/shard_map/take_near/pallas_call | solution.py:74
  13.3 0.8 collective-permute-done.oth
  14.1 0.8 pack.1
  14.9 1.3 %collective-permute-start.2 = (bf16[128,2688]{1,0:T(8,128)(2,1)S(1)}, bf16[128,2688]{1,0:T(8,128)(2,1)S(1)}, u32[]{:S(2)}, u32[]{:S(2)}) collective-permute-start(bf16[128,2688]{1,0:T(8,128)(2,1)S(1)} %get-tuple-element.24), channel_id=1, source_target_pairs={{16,0},{32,16},{48,32},{64,48},{80,64},{96,80},{112,96},{128,112},... | collective-permute-start | bytes 2064392 | tf_op jit(solution)/shard_map/ppermute | solution.py:636
  16.2 4.0 %collective-permute-start.1 = (bf16[128,2560]{1,0:T(8,128)(2,1)S(1)}, bf16[128,2560]{1,0:T(8,128)(2,1)S(1)}, u32[]{:S(2)}, u32[]{:S(2)}) collective-permute-start(bf16[128,2560]{1,0:T(8,128)(2,1)S(1)} %get-tuple-element.23), channel_id=1, source_target_pairs={{0,16},{16,32},{32,48},{48,64},{64,80},{80,96},{96,112},{112,128},... | collective-permute-start | bytes 1966088 | tf_op jit(solution)/shard_map/ppermute | solution.py:635
  20.2 4.2 %own_scores.1 = (bf16[256,64]{1,0:T(8,128)(2,1)S(1)}, bf16[64,256]{1,0:T(8,128)(2,1)S(1)}, bf16[5,2,256,128]{3,2,1,0:T(8,128)(2,1)S(1)}, f32[5,2,128,384]{3,2,1,...) custom-call(s32[2]{0:T(128)S(1)} %pad_add_fusion.place, s32[16]{0:T(128)S(1)} %bitcast.25, ...), custom_call_target="tpu_custom_call" | custom-call | flops 1006632960 | bytes 4194304 | tf_op jit(solution)/shard_map/own_scores/pallas_call | solution.py:271
  24.4 9.1 %collective-permute-done.1.below = bf16[128,2560]{1,0:T(8,128)(2,1)S(1)} collective-permute-done((bf16[128,2560]{1,0:T(8,128)(2,1)S(1)}, bf16[128,2560]{1,0:T(8,128)(2,1)S(1)}, u32[]{:S(2)}, u32[]{:S(2)}) %collective-permute-start.1) | collective-permute-done | bytes 655392 | tf_op jit(solution)/shard_map/ppermute | solution.py:635
  33.6 9.3 %attend.1 = (bf16[64,16,128]{2,1,0:T(8,128)(2,1)}, f32[2,2,128,640]{3,2,1,0:T(8,128)}, f32[2,2,128,640]{3,2,1,0:T(8,128)}, bf16[4,128,640]{2,1,0:T(8,128)(2,1)}, bf16[2,128,640]{2,1,0:T(8,128)(2,1)}) custom-call(s32[2]{0:T(128)S(1)} %pad_add_fusion.place, s32[16]{0:T(128)S(1)} %bitcast.26, s32[16]{0:T(128)S(1)} %bitcast.30, ...), custom_call_target="tpu_custom_call" | custom-call | flops 2013265920 | bytes 12582912 | tf_op jit(solution)/shard_map/attend/pallas_call | solution.py:434
  42.9 10.7 %all-to-all-start = ((bf16[32,32,128]{2,1,0:T(8,128)(2,1)}), bf16[32,32,128]{2,1,0:T(8,128)(2,1)S(1)}, u32[]{:S(2)}, u32[]{:S(2)}) async-start(bf16[32,32,128]{2,1,0:T(8,128)(2,1)} %bitcast.15), calls=%async_computation | async-start | bytes 524288 | tf_op jit(solution)/shard_map/all_to_all | solution.py:647
  53.6 1.3 %collective-permute-start.3 = (bf16[4,128,640]{2,1,0:T(8,128)(2,1)}, bf16[4,128,640]{2,1,0:T(8,128)(2,1)S(1)}, u32[]{:S(2)}, u32[]{:S(2)}) collective-permute-start(bf16[4,128,640]{2,1,0:T(8,128)(2,1)} %hold.2), channel_id=1, source_target_pairs={{16,0},{32,16},{48,32},{64,48},{80,64},{96,80},{112,96},{128,112},... | collective-permute-start | bytes 1966088 | tf_op jit(solution)/shard_map/ppermute | solution.py:654
  54.9 4.0 %collective-permute-start.4 = (bf16[2,128,640]{2,1,0:T(8,128)(2,1)}, bf16[2,128,640]{2,1,0:T(8,128)(2,1)S(1)}, u32[]{:S(2)}, u32[]{:S(2)}) collective-permute-start(bf16[2,128,640]{2,1,0:T(8,128)(2,1)} %hold.3), channel_id=1, source_target_pairs={{0,16},{16,32},{32,48},{48,64},{64,80},{80,96},{96,112},{112,128},... | collective-permute-start | bytes 983048 | tf_op jit(solution)/shard_map/ppermute | solution.py:655
  58.9 4.3 %all-to-all-done.pieces = bf16[32,32,128]{2,1,0:T(8,128)(2,1)S(1)} async-done(((bf16[32,32,128]{2,1,0:T(8,128)(2,1)}), bf16[32,32,128]{2,1,0:T(8,128)(2,1)S(1)}, u32[]{:S(2)}, u32[]{:S(2)}) %all-to-all-start) | async-done | bytes 262176 | tf_op jit(solution)/shard_map/all_to_all | solution.py:647
  63.2 0.7 first_sum.1
  63.9 6.8 %all-to-all-start.1 = ((bf16[8,32,128]{2,1,0:T(8,128)(2,1)}), bf16[8,32,128]{2,1,0:T(8,128)(2,1)S(1)}, u32[]{:S(2)}, u32[]{:S(2)}) async-start(bf16[8,32,128]{2,1,0:T(8,128)(2,1)} %first_sum.1), calls=%async_computation.1 | async-start | bytes 131072 | tf_op jit(solution)/shard_map/all_to_all | solution.py:649
  70.7 7.2 %all-to-all-done.1.pieces = bf16[8,32,128]{2,1,0:T(8,128)(2,1)S(1)} async-done(((bf16[8,32,128]{2,1,0:T(8,128)(2,1)}), bf16[8,32,128]{2,1,0:T(8,128)(2,1)S(1)}, u32[]{:S(2)}, u32[]{:S(2)}) %all-to-all-start.1) | async-done | bytes 65568 | tf_op jit(solution)/shard_map/all_to_all | solution.py:649
  77.9 0.7 second_sum.1
  78.7 5.7 %all-to-all-start.2 = ((bf16[32,32,128]{2,1,0:T(8,128)(2,1)}), bf16[32,32,128]{2,1,0:T(8,128)(2,1)S(1)}, u32[]{:S(2)}, u32[]{:S(2)}) async-start(bf16[32,32,128]{2,1,0:T(8,128)(2,1)} %second_sum.1), calls=%async_computation.2 | async-start | bytes 524288 | tf_op jit(solution)/shard_map/all_to_all | solution.py:652
  84.4 2.5 %join.1 = (bf16[2,128,1280]{2,1,0:T(8,128)(2,1)S(1)}, bf16[2,128,1280]{2,1,0:T(8,128)(2,1)S(1)}) custom-call(s32[2]{0:T(128)S(1)} %pad_add_fusion.place, s32[16]{0:T(128)S(1)} %bitcast.27, s32[16]{0:T(128)S(1)} %bitcast.31, f32[2,2,128,640]{3,2,1,0:T(8,128)} %get-tuple-element.31.sum_a_hbm, f32[2,2,128,640]{3,2,1,0:T(8,128)} %get-tuple-element.32.sum_b_hbm, ...), custom_call_target="tpu_custom_call" | custom-call | flops 1048576 | bytes 6291456 | tf_op jit(solution)/shard_map/join/pallas_call | solution.py:510
  86.9 7.1 %collective-permute-start.5 = (bf16[2,128,1280]{2,1,0:T(8,128)(2,1)S(1)}, bf16[2,128,1280]{2,1,0:T(8,128)(2,1)S(1)}, u32[]{:S(2)}, u32[]{:S(2)}) collective-permute-start(bf16[2,128,1280]{2,1,0:T(8,128)(2,1)S(1)} %get-tuple-element.37), channel_id=1, source_target_pairs={{0,8},{8,0},{1,9},{9,1},{2,10},{10,2},{3,11},{11,3},{4,12},{12,4},... | collective-permute-start | bytes 1966088 | tf_op jit(solution)/shard_map/ppermute | solution.py:659
  94.2 8.1 %collective-permute-start.6 = (bf16[64,16,128]{2,1,0:T(8,128)(2,1)S(1)}, bf16[64,16,128]{2,1,0:T(8,128)(2,1)S(1)}, u32[]{:S(2)}, u32[]{:S(2)}) collective-permute-start(bf16[64,16,128]{2,1,0:T(8,128)(2,1)S(1)} %bitcast.20), channel_id=1, source_target_pairs={{0,8},{8,0},{1,9},{9,1},{2,10},{10,2},{3,11},{11,3},{4,12},{12,4},... | collective-permute-start | bytes 786440 | tf_op jit(solution)/shard_map/ppermute | solution.py:653
  102.3 1.6 %place_halves.1 = (bf16[128,2560]{1,0:T(8,128)(2,1)}, bf16[128,2560]{1,0:T(8,128)(2,1)}) custom-call(s32[2]{0:T(128)S(1)} %pad_add_fusion.place, bf16[2,128,1280]{2,1,0:T(8,128)(2,1)S(1)} %get-tuple-element.36.mine, bf16[2,128,1280]{2,1,0:T(8,128)(2,1)S(1)} %collective-permute-done.5.other), custom_call_target="tpu_custom_call" | custom-call | bytes 4194304 | tf_op jit(solution)/shard_map/place_halves/pallas_call | solution.py:539
  104.0 1.8 %finish.1 = (f32[64,2560]{1,0:T(8,128)}, f32[4,64,128]{2,1,0:T(8,128)}) custom-call(s32[2]{0:T(128)S(1)} %pad_add_fusion.place, bf16[64,16,128]{2,1,0:T(8,128)(2,1)S(1)} %bitcast.21, bf16[64,16,128]{2,1,0:T(8,128)(2,1)S(1)} %collective-permute-done.6.swapped), custom_call_target="tpu_custom_call" | custom-call | tf_op jit(solution)/shard_map/finish/pallas_call | solution.py:601
  (15 shorter events, 0.2 us)
Async XLA Ops:
  2.6 11.5 %copy-start.1 = (s32[1,1,16]{2,1,0:T(1,128)S(1)}, s32[1,1,16]{2,1,0:T(1,128)}, u32[]{:S(2)}) copy-start(s32[1,1,16]{2,1,0:T(1,128)} %param.14) | copy-start | bytes 196
  2.6 11.5 %copy-start.2 = (s32[1,1,16]{2,1,0:T(1,128)S(1)}, s32[1,1,16]{2,1,0:T(1,128)}, u32[]{:S(2)}) copy-start(s32[1,1,16]{2,1,0:T(1,128)} %param.15) | copy-start | bytes 196
  2.6 11.5 %collective-permute-start = (bf16[128,5248]{1,0:T(8,128)(2,1)S(1)}, bf16[128,5248]{1,0:T(8,128)(2,1)S(1)}, u32[]{:S(2)}, u32[]{:S(2)}) collective-permute-start(bf16[128,5248]{1,0:T(8,128)(2,1)S(1)} %take_far.1), channel_id=1, source_target_pairs={{0,8},{8,0},{1,9},{9,1},{2,10},{10,2},{3,11},{11,3},{4,12},{12,4},... | collective-permute-start | bytes 4030472 | tf_op jit(solution)/shard_map/ppermute | solution.py:632
  14.1 6.1 %copy-start = (bf16[1,4,128,64]{2,3,1,0:T(8,128)(2,1)S(1)}, bf16[1,4,128,64]{2,3,1,0:T(8,128)(2,1)}, u32[]{:S(2)}) copy-start(bf16[1,4,128,64]{2,3,1,0:T(8,128)(2,1)} %param.16) | copy-start | bytes 196612
  14.9 18.7 %collective-permute-start.2 = (bf16[128,2688]{1,0:T(8,128)(2,1)S(1)}, bf16[128,2688]{1,0:T(8,128)(2,1)S(1)}, u32[]{:S(2)}, u32[]{:S(2)}) collective-permute-start(bf16[128,2688]{1,0:T(8,128)(2,1)S(1)} %get-tuple-element.24), channel_id=1, source_target_pairs={{16,0},{32,16},{48,32},{64,48},{80,64},{96,80},{112,96},{128,112},... | collective-permute-start | bytes 2064392 | tf_op jit(solution)/shard_map/ppermute | solution.py:636
  16.2 17.4 %collective-permute-start.1 = (bf16[128,2560]{1,0:T(8,128)(2,1)S(1)}, bf16[128,2560]{1,0:T(8,128)(2,1)S(1)}, u32[]{:S(2)}, u32[]{:S(2)}) collective-permute-start(bf16[128,2560]{1,0:T(8,128)(2,1)S(1)} %get-tuple-element.23), channel_id=1, source_target_pairs={{0,16},{16,32},{32,48},{48,64},{64,80},{80,96},{96,112},{112,128},... | collective-permute-start | bytes 1966088 | tf_op jit(solution)/shard_map/ppermute | solution.py:635
  42.9 20.3 %all-to-all-start = ((bf16[32,32,128]{2,1,0:T(8,128)(2,1)}), bf16[32,32,128]{2,1,0:T(8,128)(2,1)S(1)}, u32[]{:S(2)}, u32[]{:S(2)}) async-start(bf16[32,32,128]{2,1,0:T(8,128)(2,1)} %bitcast.15), calls=%async_computation | async-start | bytes 524288 | tf_op jit(solution)/shard_map/all_to_all | solution.py:647
  53.6 30.8 %collective-permute-start.3 = (bf16[4,128,640]{2,1,0:T(8,128)(2,1)}, bf16[4,128,640]{2,1,0:T(8,128)(2,1)S(1)}, u32[]{:S(2)}, u32[]{:S(2)}) collective-permute-start(bf16[4,128,640]{2,1,0:T(8,128)(2,1)} %hold.2), channel_id=1, source_target_pairs={{16,0},{32,16},{48,32},{64,48},{80,64},{96,80},{112,96},{128,112},... | collective-permute-start | bytes 1966088 | tf_op jit(solution)/shard_map/ppermute | solution.py:654
  54.9 29.5 %collective-permute-start.4 = (bf16[2,128,640]{2,1,0:T(8,128)(2,1)}, bf16[2,128,640]{2,1,0:T(8,128)(2,1)S(1)}, u32[]{:S(2)}, u32[]{:S(2)}) collective-permute-start(bf16[2,128,640]{2,1,0:T(8,128)(2,1)} %hold.3), channel_id=1, source_target_pairs={{0,16},{16,32},{32,48},{48,64},{64,80},{80,96},{96,112},{112,128},... | collective-permute-start | bytes 983048 | tf_op jit(solution)/shard_map/ppermute | solution.py:655
  63.9 14.0 %all-to-all-start.1 = ((bf16[8,32,128]{2,1,0:T(8,128)(2,1)}), bf16[8,32,128]{2,1,0:T(8,128)(2,1)S(1)}, u32[]{:S(2)}, u32[]{:S(2)}) async-start(bf16[8,32,128]{2,1,0:T(8,128)(2,1)} %first_sum.1), calls=%async_computation.1 | async-start | bytes 131072 | tf_op jit(solution)/shard_map/all_to_all | solution.py:649
  78.7 15.5 %all-to-all-start.2 = ((bf16[32,32,128]{2,1,0:T(8,128)(2,1)}), bf16[32,32,128]{2,1,0:T(8,128)(2,1)S(1)}, u32[]{:S(2)}, u32[]{:S(2)}) async-start(bf16[32,32,128]{2,1,0:T(8,128)(2,1)} %second_sum.1), calls=%async_computation.2 | async-start | bytes 524288 | tf_op jit(solution)/shard_map/all_to_all | solution.py:652
  86.9 15.4 %collective-permute-start.5 = (bf16[2,128,1280]{2,1,0:T(8,128)(2,1)S(1)}, bf16[2,128,1280]{2,1,0:T(8,128)(2,1)S(1)}, u32[]{:S(2)}, u32[]{:S(2)}) collective-permute-start(bf16[2,128,1280]{2,1,0:T(8,128)(2,1)S(1)} %get-tuple-element.37), channel_id=1, source_target_pairs={{0,8},{8,0},{1,9},{9,1},{2,10},{10,2},{3,11},{11,3},{4,12},{12,4},... | collective-permute-start | bytes 1966088 | tf_op jit(solution)/shard_map/ppermute | solution.py:659
  94.2 9.8 %collective-permute-start.6 = (bf16[64,16,128]{2,1,0:T(8,128)(2,1)S(1)}, bf16[64,16,128]{2,1,0:T(8,128)(2,1)S(1)}, u32[]{:S(2)}, u32[]{:S(2)}) collective-permute-start(bf16[64,16,128]{2,1,0:T(8,128)(2,1)S(1)} %bitcast.20), channel_id=1, source_target_pairs={{0,8},{8,0},{1,9},{9,1},{2,10},{10,2},{3,11},{11,3},{4,12},{12,4},... | collective-permute-start | bytes 786440 | tf_op jit(solution)/shard_map/ppermute | solution.py:653
